TPU v7x, 32 devices: a whole 2x2x4 slice. The times are simulated.
32 devices in a mesh: grp: 2 (over y), chan: 4 (over z), win: 2 (over x), rep: 2 (over core).
Axes of the slice: x: 2, y: 2, z: 4, core: 2. Of those that a mesh axis runs over, the one named last changes fastest.
Arguments:
- sources: bfloat16 [8, 256, 4096], P(('grp', 'chan'), None, 'win'), parts along dimension 0, may hold values from -6 to 6
- receivers: bfloat16 [32, 4096], P(('grp', 'chan'), 'win'), parts along dimension 0, may hold values from -6 to 6
- plan: int32 [2, 2], P('grp'), parts along dimension 0, may hold values from 0 to 3, as said below
- pair_index: int32 [2, 4, 4, 512], P('grp', 'chan'), parts along dimension 0, may hold values from 0 to 2047, as said below
- keep: int32 [2, 4, 4, 512], P('grp', 'chan'), parts along dimension 0, may hold values 0 or 1
Outputs:
- stacks: float32 [8, 1, 4, 512, 2048], P(('grp', 'chan'), None, None, None, ('win', 'rep')), parts along dimension 0
There are 2 independent parts, one for each index of `grp`. A program takes and returns all parts, laid end to end along the dimension named above; each array names one. Nothing has to cross between parts.
Inputs may be any that keep to these rules, and one draw needn't show every extreme that they name: `plan`: the entries of one round name different blocks. For each round k and group c, pair_index[k, c] names every number below 2048 exactly once.
All inputs are finite; a program needn't handle non-finite values. No bound on the sum of `keep` on one device may be relied on, other than what follows from the above.
Results may differ from a plain program's by a relative error of at most 0.0003.
Values may be sent and summed in bfloat16 or wider, within the bound.
No kernel may reach another device: no remote copies, remote signals or barrier semaphores. Data moves between devices by JAX's collectives and lax.ppermute only.
A program may use at most 64 MiB of HBM per device.

v0:
```python
import functools
import math

import jax
import jax.numpy as jnp
from jax import lax
from jax.experimental import pallas as pl
from jax.experimental.pallas import tpu as pltpu
from jax.sharding import PartitionSpec as P

LAGS = 2048
LANES = 128
SHIFT_ROWS = 8
STEP = 2 * LANES
CHAINS = 1
DIGIT = 64
HANKEL_BYTES = 24 * 2**20
VMEM_BYTES = 26 * 2**20
F32 = jnp.float32
BF16 = jnp.bfloat16


def swapped(block, axis, first):
    size = lax.axis_size(axis)
    route = []
    for i in range(first, size - 1, 2):
        route += [(i, i + 1), (i + 1, i)]
    return lax.ppermute(block, axis, route)


def turned(block, axis, distance):
    size = lax.axis_size(axis)
    return lax.ppermute(block, axis, [(i, (i + distance) % size) for i in range(size)])


def in_hbm(array):
    return pltpu.with_memory_space_constraint(array, pltpu.HBM)


def params(vmem):
    return pltpu.CompilerParams(vmem_limit_bytes=vmem)


def pack_kernel(halves, lags, plan_hbm, source_ref, receiver_hbm, pair_hbm, keep_hbm, parcel_ref, number_ref, *refs):
    chain_refs, small_refs, sems = refs[:-5], refs[-5:-1], refs[-1]
    plan_ref, receiver_ref, pair_ref, keep_ref = small_refs
    small = []
    for place, source in enumerate((plan_hbm, receiver_hbm, pair_hbm, keep_hbm)):
        small.append(pltpu.make_async_copy(source, small_refs[place], sems.at[CHAINS + place]))
        small[-1].start()
    r_dev, samples = receiver_ref.shape
    n_chan, cap = pair_ref.shape
    n_win = parcel_ref.shape[0] // n_chan
    chan, win, rep = lax.axis_index("chan"), lax.axis_index("win"), lax.axis_index("rep")
    block_rows = source_ref.shape[0]
    half_rows = block_rows // halves
    rows = chain_refs[0].shape[0]
    copies = []
    for chain, chain_ref in enumerate(chain_refs):
        start = pl.multiple_of(rep * half_rows + chain * rows, rows)
        copies.append(pltpu.make_async_copy(source_ref.at[pl.ds(start, rows)], chain_ref, sems.at[chain]))
        copies[-1].start()
    for copy in small:
        copy.wait()

    packed = pair_ref[...] * 2 + keep_ref[...]
    digits = jnp.concatenate([packed // DIGIT, packed % DIGIT], axis=1).astype(F32)
    heard = receiver_ref[...].astype(F32)
    part = 2 * cap // r_dev
    spare = parcel_ref.shape[2] - samples - part
    for d in range(n_chan):
        lists = [digits[d : d + 1, i * part : (i + 1) * part] for i in range(r_dev)]
        parcel = [heard, jnp.concatenate(lists, axis=0)]
        if spare:
            parcel.append(jnp.zeros((r_dev, spare), F32))
        parcel = jnp.concatenate(parcel, axis=1).astype(BF16)
        for w in range(n_win):
            parcel_ref[d * n_win + w] = parcel

    one, two = plan_ref[0, 0], plan_ref[0, 1]
    nearer = jnp.where(jnp.abs(one - chan) <= jnp.abs(two - chan), 0, 1)
    sign = jnp.where(chan % 2 == 0, 1, -1)
    number_ref[0] = nearer
    number_ref[1] = block_rows - rep * half_rows
    number_ref[2] = sign * (jnp.where(nearer == 0, one, two) - chan)
    number_ref[3] = sign * (jnp.where(nearer == 0, two, one) - chan)
    for v in range(n_win):
        number_ref[4 + v] = (win + n_win - v) % n_win * samples + (win * halves + rep) * lags
    for copy in copies:
        copy.wait()


def pack(plan, sources, receivers, pair_index, keep, halves, lags, n_chan, n_win):
    r_dev, samples = receivers.shape
    chain_rows = sources.shape[0] // halves // CHAINS
    beside = -(-2 * pair_index.shape[1] // r_dev // LANES) * LANES
    vmem, smem = pl.BlockSpec(memory_space=pltpu.VMEM), pl.BlockSpec(memory_space=pltpu.SMEM)
    shapes = [jax.ShapeDtypeStruct((n_chan * n_win, r_dev, samples + beside), BF16)]
    shapes.append(jax.ShapeDtypeStruct((4 + n_win,), jnp.int32))
    shapes += [jax.ShapeDtypeStruct((chain_rows, samples), BF16)] * CHAINS
    return pl.pallas_call(
        functools.partial(pack_kernel, halves, lags),
        in_specs=[pl.BlockSpec(memory_space=pl.ANY)] * 5,
        out_specs=[vmem, smem] + [vmem] * CHAINS,
        out_shape=shapes,
        scratch_shapes=[
            pltpu.SMEM(plan.shape, plan.dtype),
            pltpu.VMEM(receivers.shape, receivers.dtype),
            pltpu.VMEM(pair_index.shape, pair_index.dtype),
            pltpu.VMEM(keep.shape, keep.dtype),
            pltpu.SemaphoreType.DMA((CHAINS + 4,)),
        ],
        compiler_params=params(VMEM_BYTES // 2),
        name="pack",
    )(*[in_hbm(a) for a in (plan, sources, receivers, pair_index, keep)])


def choose_kernel(which, offsets, number_ref, *refs):
    out_ref, sems = refs[-2:]
    rows = out_ref.shape[0] // CHAINS
    where = number_ref[which]
    waits = []
    for chain in range(CHAINS):
        target = out_ref.at[pl.ds(chain * rows, rows)]
        for place, offset in enumerate(offsets):
            copy = pltpu.make_async_copy(refs[chain * len(offsets) + place], target, sems.at[chain])

            @pl.when(where == offset)
            def _():
                copy.start()

        waits.append(copy)
    for copy in waits:
        copy.wait()


def choose(numbers, which, arrived, offsets):
    pieces = [there[offset] for there in arrived for offset in offsets]
    rows, samples = pieces[0].shape
    any_spec = pl.BlockSpec(memory_space=pl.ANY)
    return pl.pallas_call(
        functools.partial(choose_kernel, which, offsets),
        in_specs=[pl.BlockSpec(memory_space=pltpu.SMEM)] + [any_spec] * len(pieces),
        out_specs=pl.BlockSpec(memory_space=pltpu.VMEM),
        out_shape=jax.ShapeDtypeStruct((rows * CHAINS, samples), BF16),
        scratch_shapes=[pltpu.SemaphoreType.DMA((CHAINS,))],
        compiler_params=params(VMEM_BYTES // 4),
        name="choose",
    )(numbers, *pieces)


def column(row):
    return jnp.broadcast_to(row, (SHIFT_ROWS, row.shape[1])).T[:, :1]


def ones_where(condition):
    return jnp.where(condition, 1.0, 0.0).astype(BF16)


def index_kernel(r_dev, n_win, samples, cap, tile, block_rows, number_ref, parcel_ref, pick_ref, place_ref, pass_ref,
                 count_ref, more_pick_ref, more_place_ref, pick_scratch, place_scratch):
    nearer, offset = number_ref[0], number_ref[1]
    slots = 2 * r_dev * tile
    part = 2 * cap // r_dev
    beside = parcel_ref.shape[2] - samples
    below = lax.broadcasted_iota(jnp.int32, (cap, cap), 0) < lax.broadcasted_iota(jnp.int32, (cap, cap), 1)
    below = ones_where(below)
    later = []
    for place in range(pick_ref.shape[0]):
        group = pl.program_id(0) * pick_ref.shape[0] + place
        digits = parcel_ref[place * n_win, :, pl.ds(samples, beside)].astype(F32)
        digits = jnp.concatenate([digits[i : i + 1, :part] for i in range(r_dev)], axis=1).astype(jnp.int32)
        packed = digits[:, :cap] * DIGIT + digits[:, cap:]
        pairs, kept = packed // 2, packed % 2 == 1
        source_row, receiver = pairs // r_dev, pairs % r_dev
        turn = jnp.where(source_row // block_rows == nearer, 0, 1)
        row = (source_row + offset) % block_rows
        segment = jnp.where(kept, turn * r_dev + receiver, -1)
        member = lax.broadcasted_iota(jnp.int32, (2 * r_dev, cap), 0) == segment
        earlier = jnp.dot(ones_where(member), below, preferred_element_type=F32)
        rank = jnp.sum(jnp.where(member, earlier, 0.0), axis=0, keepdims=True).astype(jnp.int32)
        code = (rank // tile) * slots + (turn * r_dev + receiver) * tile + rank % tile
        code = jnp.where(kept, code, -1)
        counts = jnp.sum(jnp.where(member, 1.0, 0.0), axis=1, keepdims=True)
        which = lax.broadcasted_iota(jnp.int32, counts.shape, 0) % r_dev
        passes = 0
        for r in range(r_dev):
            count = jnp.max(jnp.where(which == r, counts, 0.0)).astype(jnp.int32)
            count_ref[group * r_dev + r] = count
            passes = jnp.maximum(passes, (count + tile - 1) // tile)
        pass_ref[group] = passes
        code_column = column(code.astype(F32)).astype(jnp.int32)
        row_column = column(row.astype(F32)).astype(jnp.int32)

        def matrices(number, code=code, code_column=code_column, row_column=row_column):
            start = number * slots
            row_ones = ones_where(row_column == lax.broadcasted_iota(jnp.int32, (cap, block_rows), 1))
            by_slot = ones_where(lax.broadcasted_iota(jnp.int32, (slots, cap), 0) + start == code)
            pick = jnp.dot(by_slot, row_ones, preferred_element_type=F32).astype(BF16)
            return pick, ones_where(lax.broadcasted_iota(jnp.int32, (cap, slots), 1) + start == code_column)

        pick_ref[place], place_ref[place] = matrices(0)
        later.append((group, passes, matrices))

    for group, passes, matrices in later:

        @pl.when(passes > 1)
        def _():
            def one_pass(number, carry):
                pick_scratch[...], place_scratch[...] = matrices(number)
                pltpu.sync_copy(pick_scratch, more_pick_ref.at[group, number - 1])
                pltpu.sync_copy(place_scratch, more_place_ref.at[group, number - 1])
                return carry

            lax.fori_loop(1, passes, one_pass, 0)


def index(parcels, numbers, n_win, samples, r_dev, cap, tile, block_rows):
    groups = parcels.shape[0] // n_win
    at_once = math.gcd(groups, 4)
    slots = 2 * r_dev * tile
    more = max(1, -(-min(block_rows, cap) // tile) - 1)
    return pl.pallas_call(
        functools.partial(index_kernel, r_dev, n_win, samples, cap, tile, block_rows),
        grid_spec=pltpu.PrefetchScalarGridSpec(
            num_scalar_prefetch=1,
            grid=(groups // at_once,),
            in_specs=[pl.BlockSpec((at_once * n_win,) + parcels.shape[1:], lambda i, *_: (i, 0, 0))],
            out_specs=[
                pl.BlockSpec((at_once, slots, block_rows), lambda i, *_: (i, 0, 0)),
                pl.BlockSpec((at_once, cap, slots), lambda i, *_: (i, 0, 0)),
                pl.BlockSpec(memory_space=pltpu.SMEM),
                pl.BlockSpec(memory_space=pltpu.SMEM),
                pl.BlockSpec(memory_space=pl.ANY),
                pl.BlockSpec(memory_space=pl.ANY),
            ],
            scratch_shapes=[pltpu.VMEM((slots, block_rows), BF16), pltpu.VMEM((cap, slots), BF16)],
        ),
        out_shape=[
            jax.ShapeDtypeStruct((groups, slots, block_rows), BF16),
            jax.ShapeDtypeStruct((groups, cap, slots), BF16),
            jax.ShapeDtypeStruct((groups,), jnp.int32),
            jax.ShapeDtypeStruct((groups * r_dev,), jnp.int32),
            pltpu.HBM((groups, more, slots, block_rows), BF16),
            pltpu.HBM((groups, more, cap, slots), BF16),
        ],
        compiler_params=params(VMEM_BYTES),
        name="index",
    )(numbers, parcels)


def lay_out(parcel_ref, signal_ref, samples):
    n_win, r_dev, _ = parcel_ref.shape
    for w in range(n_win):
        signal_ref[:r_dev, w * samples : (w + 1) * samples] = parcel_ref[w, :, :samples].astype(F32)
    tail = signal_ref.shape[1] - n_win * samples
    signal_ref[:r_dev, n_win * samples :] = jnp.zeros((r_dev, tail), F32)


def hankel_rows(signal_ref, r, begin, width, out_ref, place):
    length = width + LANES
    signal = signal_ref[r : r + 1, pl.ds(pl.multiple_of(begin, LANES), length)]
    base = jnp.broadcast_to(signal, (SHIFT_ROWS, length))
    sublane = lax.broadcasted_iota(jnp.int32, base.shape, 0)
    for bit in (1, 2, 4):
        base = jnp.where(sublane & bit != 0, pltpu.roll(base, length - bit, 1), base)
    for first in range(0, LANES, 2 * SHIFT_ROWS):
        both = []
        for shift in (first, first + SHIFT_ROWS):
            rolled = pltpu.roll(base, length - shift, 1) if shift else base
            both.append(rolled[:, :width])
        out_ref[place, first : first + 2 * SHIFT_ROWS, :] = jnp.concatenate(both, axis=0).astype(BF16)


def hankel_kernel(v, samples, number_ref, parcel_ref, out_ref, signal_ref):
    lay_out(parcel_ref, signal_ref, samples)
    r_dev = parcel_ref.shape[1]
    for r in range(r_dev):
        hankel_rows(signal_ref, r, number_ref[4 + v], out_ref.shape[2], out_ref, pl.program_id(0) * r_dev + r)


def build_hankel(parcels, numbers, v, n_win, samples, width):
    groups, r_dev = parcels.shape[0] // n_win, parcels.shape[1]
    shape = (groups * r_dev, LANES, width)
    return pl.pallas_call(
        functools.partial(hankel_kernel, v, samples),
        grid_spec=pltpu.PrefetchScalarGridSpec(
            num_scalar_prefetch=1,
            grid=(groups,),
            in_specs=[pl.BlockSpec((n_win,) + parcels.shape[1:], lambda i, *_: (i, 0, 0))],
            out_specs=pl.BlockSpec(memory_space=pltpu.VMEM),
            scratch_shapes=[pltpu.VMEM((SHIFT_ROWS, n_win * samples + LAGS), F32)],
        ),
        out_shape=jax.ShapeDtypeStruct(shape, BF16),
        cost_estimate=pl.CostEstimate(
            flops=math.prod(shape), bytes_accessed=2 * math.prod(shape), transcendentals=0
        ),
        compiler_params=params(VMEM_BYTES // 2),
        name="hankel",
    )(numbers, parcels)


def pick_rows(pieces, pick, gathered):
    parts = len(pieces) // 2
    count, samples = gathered.shape[1:]
    for q in range(2):
        block_pieces = pieces[q * parts : (q + 1) * parts]
        ones = pick[q * count : (q + 1) * count, :]
        for t in range(0, samples, STEP):
            block = jnp.concatenate([piece[:, t : t + STEP] for piece in block_pieces], axis=0)
            gathered[q, :, t : t + STEP] = jnp.dot(ones, block, preferred_element_type=F32).astype(BF16)


def multiply(gathered, hankel_ref, place, r, tile, lag):
    samples = gathered.shape[2]
    chosen = jnp.concatenate([gathered[q, r * tile : (r + 1) * tile, :] for q in range(2)], axis=0)
    wide = jnp.concatenate(
        [hankel_ref[place, :, t + lag : t + lag + STEP] for t in range(0, samples, LANES)], axis=0
    )
    return jnp.dot(chosen, wide, preferred_element_type=F32)


def split(total, high, low, slots, lags):
    upper = total.astype(BF16)
    high[slots, lags] = upper
    low[slots, lags] = (total - upper.astype(F32)).astype(BF16)


def placed(place, high, low):
    return jnp.dot(place, high[...], preferred_element_type=F32) + jnp.dot(
        place, low[...], preferred_element_type=F32
    )


def correlate_kernel(parts, v, tile, norming, prebuilt, first, last, pass_ref, count_ref, number_ref, *refs):
    refs = list(refs)
    pieces = [refs.pop(0) for _ in range(2 * parts)]
    signal_ref, pick_ref, place_ref, more_pick_ref, more_place_ref = [refs.pop(0) for _ in range(5)]
    if not first:
        sums_ref, extra_ref = refs.pop(0), refs.pop(0)
    if last:
        out_ref = refs.pop(0)
    else:
        handed_ref, left_ref = refs.pop(0), refs.pop(0)
    gathered, high, low, extra, pick_scratch, place_scratch = refs[:6]
    r_dev = gathered.shape[1] // tile
    samples = pieces[0].shape[1]
    lag_dev = extra.shape[1]
    group = pl.program_id(0)

    if prebuilt:
        hankel_ref, hankel_place = signal_ref, group * r_dev
    else:
        hankel_place = 0
        hankel_ref, row_ref = refs[6:]
        lay_out(signal_ref, row_ref, samples)
        for r in range(r_dev):
            hankel_rows(row_ref, r, number_ref[4 + v], hankel_ref.shape[2], hankel_ref, r)

    pick_rows(pieces, pick_ref.at[0], gathered)
    for r in range(r_dev):
        for lag in range(0, lag_dev, STEP):
            lags = slice(lag, lag + STEP)
            both = multiply(gathered, hankel_ref, hankel_place + r, r, tile, lag)
            for q in range(2):
                total = both[q * tile : (q + 1) * tile]
                slots = slice((q * r_dev + r) * tile, (q * r_dev + r + 1) * tile)
                if not first:
                    total += sums_ref[group, slots, lags]
                if last:
                    split(total * norming, high, low, slots, lags)
                else:
                    handed_ref[group, slots, lags] = total
    if last:
        out_ref[0] = placed(place_ref[0], high, low)

    @pl.when(pass_ref[group] > 1)
    def _():
        if first:
            extra[...] = jnp.zeros(extra.shape, F32)
        else:
            pltpu.sync_copy(extra_ref.at[group], extra)

        def one_pass(number, carry):
            pltpu.sync_copy(more_pick_ref.at[group, number - 1], pick_scratch)
            pltpu.sync_copy(more_place_ref.at[group, number - 1], place_scratch)
            pick_rows(pieces, pick_scratch, gathered)
            for r in range(r_dev):
                needed = count_ref[group * r_dev + r] > number * tile
                places = [slice((q * r_dev + r) * tile, (q * r_dev + r + 1) * tile) for q in range(2)]

                @pl.when(needed)
                def _():
                    for lag in range(0, lag_dev, STEP):
                        both = multiply(gathered, hankel_ref, hankel_place + r, r, tile, lag) * norming
                        for q, slots in enumerate(places):
                            split(both[q * tile : (q + 1) * tile], high, low, slots, slice(lag, lag + STEP))

                @pl.when(jnp.logical_not(needed))
                def _():
                    for slots in places:
                        high[slots, :] = jnp.zeros((tile, lag_dev), BF16)
                        low[slots, :] = jnp.zeros((tile, lag_dev), BF16)

            extra[...] += placed(place_scratch[...], high, low)
            return carry

        lax.fori_loop(1, pass_ref[group], one_pass, 0)
        if last:
            out_ref[0] += extra[...]
        else:
            pltpu.sync_copy(extra, left_ref.at[group])


def correlate(pieces, signal, prebuilt, numbers, v, matrices, before, last, tile, norming, lag_dev, n_win, r_dev):
    pick, place, passes, counts, more_pick, more_place = matrices
    parts = len(pieces) // 2
    groups, cap, slots = place.shape
    part_rows, samples = pieces[0].shape
    width = samples - LANES + lag_dev
    by_group = lambda shape: pl.BlockSpec(shape, lambda i, *_: (i, 0, 0))
    any_spec = pl.BlockSpec(memory_space=pl.ANY)
    whole_spec = pl.BlockSpec(memory_space=pltpu.VMEM)
    sums_shape = jax.ShapeDtypeStruct((groups, slots, lag_dev), F32)
    out_shape = jax.ShapeDtypeStruct((groups, cap, lag_dev), F32)
    in_specs = [whole_spec] * len(pieces)
    in_specs.append(whole_spec if prebuilt else by_group((n_win,) + signal.shape[1:]))
    in_specs += [by_group((1,) + pick.shape[1:]), by_group((1,) + place.shape[1:]), any_spec, any_spec]
    args = pieces + [signal, pick, place, in_hbm(more_pick), in_hbm(more_place)]
    if before is not None:
        in_specs += [whole_spec, any_spec]
        args += [before[0], in_hbm(before[1])]
    scratch = [
        pltpu.VMEM((2, r_dev * tile, samples), BF16),
        pltpu.VMEM((slots, lag_dev), BF16),
        pltpu.VMEM((slots, lag_dev), BF16),
        pltpu.VMEM((cap, lag_dev), F32),
        pltpu.VMEM(pick.shape[1:], BF16),
        pltpu.VMEM(place.shape[1:], BF16),
    ]
    if not prebuilt:
        scratch.append(pltpu.VMEM((r_dev, LANES, width), BF16))
        scratch.append(pltpu.VMEM((SHIFT_ROWS, n_win * samples + LAGS), F32))
    body = functools.partial(correlate_kernel, parts, v, tile, norming, prebuilt, before is None, last)
    return pl.pallas_call(
        body,
        grid_spec=pltpu.PrefetchScalarGridSpec(
            num_scalar_prefetch=3,
            grid=(groups,),
            in_specs=in_specs,
            out_specs=by_group((1, cap, lag_dev)) if last else [whole_spec, any_spec],
            scratch_shapes=scratch,
        ),
        out_shape=out_shape if last else [sums_shape, pltpu.HBM(out_shape.shape, F32)],
        cost_estimate=pl.CostEstimate(
            flops=4 * groups * r_dev * tile * samples * (lag_dev + parts * part_rows),
            bytes_accessed=signal.size * signal.dtype.itemsize + 2 * groups * cap * lag_dev * 4,
            transcendentals=0,
        ),
        compiler_params=params(VMEM_BYTES if prebuilt else 2 * VMEM_BYTES),
        name="correlate",
    )(passes, counts, numbers, *args)


def shards(sources, receivers, plan, pair_index, keep):
    _, block_rows, samples = sources.shape
    r_dev = receivers.shape[0]
    n_chan = lax.axis_size("chan")
    n_win = lax.axis_size("win")
    n_rep = lax.axis_size("rep")
    cap = pair_index.shape[3]
    lag_dev = LAGS // (n_win * n_rep)
    tile = max(16, cap // 8)
    norming = 1.0 / math.sqrt(samples * n_win)
    width = samples - LANES + lag_dev
    prebuilt = n_chan * r_dev * n_win * LANES * width * 2 <= HANKEL_BYTES

    parcels, numbers, *owns = pack(
        plan, sources[0], receivers, pair_index[0, 0], keep[0, 0], n_rep, lag_dev, n_chan, n_win
    )
    parcels = lax.all_to_all(parcels, ("chan", "win"), split_axis=0, concat_axis=0, tiled=True)

    arrived = [{0: own} for own in owns]

    def relay(step):
        for there in arrived:
            there[step] = swapped(there[1 - step], "chan", 0)
            if step < n_chan - 1:
                there[-step] = swapped(there[step - 1], "chan", 1)

    def after_arrival(step, value):
        for there in arrived:
            for key in (step, -step):
                if key in there:
                    value, there[key] = lax.optimization_barrier((value, there[key]))
        return value

    def before_start(step, value):
        for there in arrived:
            for key in (1 - step, step - 1):
                value, there[key] = lax.optimization_barrier((value, there[key]))
        return value

    def halves(piece):
        return [piece] + [turned(piece, "rep", -u) for u in range(1, n_rep)]

    def spans(piece):
        return [piece] + [turned(piece, "win", v) for v in range(1, n_win)]

    signals = [parcels] * n_win
    relay(1)
    parcels = after_arrival(1, parcels)
    relay(2)
    matrices = index(parcels, numbers, n_win, samples, r_dev, cap, tile, block_rows)
    if prebuilt:
        signals[0] = build_hankel(parcels, numbers, 0, n_win, samples, width)
    matrices, signals[0] = before_start(3, (matrices, signals[0]))
    reach = range(-(n_chan - 2), n_chan - 1)
    near = choose(numbers, 2, arrived, [offset for offset in reach if offset in arrived[0]])
    if prebuilt:
        parcels = after_arrival(2, parcels)
        parcels, near = lax.optimization_barrier((parcels, near))
        for v in range(1, n_win):
            signals[v] = build_hankel(parcels, numbers, v, n_win, samples, width)
    for step in range(3, n_chan):
        relay(step)
    near_halves = [halves(piece) for piece in spans(near)]
    if prebuilt:
        signals = after_arrival(n_chan - 1, signals)
    far_spans = spans(choose(numbers, 3, arrived, sorted(arrived[0])))

    result = None
    for v in range(n_win):
        if v:
            far_spans, result = lax.optimization_barrier((far_spans, result))
        result = correlate(
            near_halves[v] + halves(far_spans[v]), signals[v], prebuilt, numbers, v, matrices, result, v == n_win - 1,
            tile, norming, lag_dev, n_win, r_dev,
        )
    return result[None, None]


def solution(mesh):
    placed_at = (
        P(("grp", "chan"), None, "win"),
        P(("grp", "chan"), "win"),
        P("grp", None),
        P("grp", "chan", None, None),
        P("grp", "chan", None, None),
    )
    return jax.shard_map(
        shards,
        mesh=mesh,
        in_specs=placed_at,
        out_specs=P(("grp", "chan"), None, None, None, ("win", "rep")),
        check_vma=False,
    )
```

profile of v0, /device:TPU:9, one launch (start us, length us, event | category | flops | bytes accessed | tf_op | source)
XLA Modules:
  0.0 86.0 jit_solution(2059702406879211685)
XLA Ops:
  0.0 1.7 %pack.1 = (bf16[8,4,2304]{2,1,0:T(4,128)(2,1)S(1)}, s32[6]{0:T(128)S(1)}, bf16[128,2048]{1,0:T(8,128)(2,1)S(1)}) custom-call(s32[1,2]{1,0:T(1,128)} %plan_hbm.1, bf16[256,2048]{1,0:T(8,128)(2,1)} %bitcast.4, bf16[4,2048]{1,0:T(4,128)(2,1)} %receiver_hbm.1, s32[4,512]{1,0:T(4,128)} %bitcast.5, s32[4,512]{1,0:T(4,128)} %bitcast.6), custom_call_target="tpu_custom_call" | custom-call | tf_op jit(solution)/shard_map/pack/pallas_call | solution.py:101
  1.7 0.1 collective-permute-start
  1.8 4.5 %collective-permute-start.1 = (bf16[128,2048]{1,0:T(8,128)(2,1)S(1)}, bf16[128,2048]{1,0:T(8,128)(2,1)S(1)}, u32[]{:S(2)}, u32[]{:S(2)}) collective-permute-start(bf16[128,2048]{1,0:T(8,128)(2,1)S(1)} %get-tuple-element.50.refs_2_), channel_id=1, source_target_pairs={{4,8},{8,4},{5,9},{9,5},{6,10},{10,6},{7,11},{11,7},{20,24},{24,20... | collective-permute-start | bytes 1572872 | tf_op jit(solution)/shard_map/ppermute | solution.py:28
  6.3 14.7 %all_to_all.5.parcel_ref = bf16[8,4,2304]{2,1,0:T(4,128)(2,1)S(1)} all-to-all(bf16[8,4,2304]{2,1,0:T(4,128)(2,1)S(1)} %get-tuple-element.49), channel_id=1, replica_groups=mesh['grp'=2,'chan'=4,'win'=2,'rep'=2] {'chan','win'}, dimensions={0} | all-to-all | bytes 294912 | tf_op jit(solution)/shard_map/all_to_all | solution.py:481
  21.0 3.0 %collective-permute-start.2 = (bf16[128,2048]{1,0:T(8,128)(2,1)S(1)}, bf16[128,2048]{1,0:T(8,128)(2,1)S(1)}, u32[]{:S(2)}, u32[]{:S(2)}) collective-permute-start(bf16[128,2048]{1,0:T(8,128)(2,1)S(1)} %collective-permute-done.refs_3_), channel_id=1, source_target_pairs={{4,8},{8,4},{5,9},{9,5},{6,10},{10,6},{7,11},{11,7},{20,24},{24,20... | collective-permute-start | bytes 1572872 | tf_op jit(solution)/shard_map/ppermute | solution.py:28
  24.1 0.1 collective-permute-start.3
  24.1 5.3 %index.1 = (bf16[4,512,256]{2,1,0:T(8,128)(2,1)S(1)}, bf16[4,512,512]{2,1,0:T(8,128)(2,1)S(1)}, s32[4]{0:T(128)S(1)}, s32[16]{0:T(128)S(1)}, bf16[4,3,512,256]{3...) custom-call(s32[6]{0:T(128)S(1)} %get-tuple-element.48.number_ref, bf16[8,4,2304]{2,1,0:T(4,128)(2,1)S(1)} %all_to_all.5.parcel_ref), custom_call_target="tpu_custom_call" | custom-call | tf_op jit(solution)/shard_map/index/pallas_call | solution.py:223
  29.4 6.4 %hankel.2.refs_4_ = bf16[16,128,2432]{2,1,0:T(8,128)(2,1)S(1)} custom-call(s32[6]{0:T(128)S(1)} %get-tuple-element.48.number_ref, bf16[8,4,2304]{2,1,0:T(4,128)(2,1)S(1)} %all_to_all.5.parcel_ref), custom_call_target="tpu_custom_call" | custom-call | flops 4980736 | bytes 9961472 | tf_op jit(solution)/shard_map/hankel/pallas_call | solution.py:285
  35.8 0.0 collective-permute-done.3.refs_4_
  35.9 0.1 collective-permute-start.6
  35.9 0.6 choose.2.refs_0_
  36.6 2.9 %collective-permute-start.8 = (bf16[128,2048]{1,0:T(8,128)(2,1)S(1)}, bf16[128,2048]{1,0:T(8,128)(2,1)S(1)}, u32[]{:S(2)}, u32[]{:S(2)}) collective-permute-start(bf16[128,2048]{1,0:T(8,128)(2,1)S(1)} %choose.2.refs_0_), channel_id=1, source_target_pairs={{0,1},{1,0},{2,3},{3,2},{4,5},{5,4},{6,7},{7,6},{8,9},{9,8},{10,11... | collective-permute-start | bytes 1572872 | tf_op jit(solution)/shard_map/ppermute | solution.py:33
  39.4 0.2 collective-permute-start.4
  39.6 6.4 %hankel.3.refs_4_ = bf16[16,128,2432]{2,1,0:T(8,128)(2,1)S(1)} custom-call(s32[6]{0:T(128)S(1)} %get-tuple-element.48.number_ref, bf16[8,4,2304]{2,1,0:T(4,128)(2,1)S(1)} %all_to_all.5.parcel_ref), custom_call_target="tpu_custom_call" | custom-call | flops 4980736 | bytes 9961472 | tf_op jit(solution)/shard_map/hankel/pallas_call | solution.py:285
  46.0 0.7 collective-permute-done.6.refs_5_
  46.7 0.8 choose.3.refs_2_
  47.5 3.6 %collective-permute-start.9 = (bf16[128,2048]{1,0:T(8,128)(2,1)S(1)}, bf16[128,2048]{1,0:T(8,128)(2,1)S(1)}, u32[]{:S(2)}, u32[]{:S(2)}) collective-permute-start(bf16[128,2048]{1,0:T(8,128)(2,1)S(1)} %choose.3.refs_2_), channel_id=1, source_target_pairs={{0,1},{1,0},{2,3},{3,2},{4,5},{5,4},{6,7},{7,6},{8,9},{9,8},{10,11... | collective-permute-start | bytes 1572872 | tf_op jit(solution)/shard_map/ppermute | solution.py:33
  51.1 0.2 collective-permute-start.7
  51.3 1.6 %collective-permute-done.4.refs_0_ = bf16[128,2048]{1,0:T(8,128)(2,1)S(1)} collective-permute-done((bf16[128,2048]{1,0:T(8,128)(2,1)S(1)}, bf16[128,2048]{1,0:T(8,128)(2,1)S(1)}, u32[]{:S(2)}, u32[]{:S(2)}) %collective-permute-start.4) | collective-permute-done | bytes 524320 | tf_op jit(solution)/shard_map/ppermute | solution.py:33
  52.9 0.8 collective-permute-start.5
  53.8 13.1 %correlate.2 = (f32[4,512,512]{2,1,0:T(8,128)S(1)}, f32[4,512,512]{2,1,0:T(8,128)}) custom-call(s32[4]{0:T(128)S(1)} %get-tuple-element.68.pass_ref, s32[16]{0:T(128)S(1)} %get-tuple-element.69.count_ref, s32[6]{0:T(128)S(1)} %get-tuple-element.48.number_ref, bf16[128,2048]{1,0:T(8,128)(2,1)S(1)} %choose.2.refs_0_, ...), custom_call_target="tpu_custom_call" | custom-call | flops 6442450944 | bytes 18350080 | tf_op jit(solution)/shard_map/correlate/pallas_call | solution.py:445
  66.9 0.1 collective-permute-start.10
  67.0 1.9 %collective-permute-done.10.refs_3_ = bf16[128,2048]{1,0:T(8,128)(2,1)S(1)} collective-permute-done((bf16[128,2048]{1,0:T(8,128)(2,1)S(1)}, bf16[128,2048]{1,0:T(8,128)(2,1)S(1)}, u32[]{:S(2)}, u32[]{:S(2)}) %collective-permute-start.10) | collective-permute-done | bytes 524320 | tf_op jit(solution)/shard_map/ppermute | solution.py:33
  68.9 17.2 %correlate.3 = f32[4,512,512]{2,1,0:T(8,128)} custom-call(s32[4]{0:T(128)S(1)} %get-tuple-element.68.pass_ref, s32[16]{0:T(128)S(1)} %get-tuple-element.69.count_ref, s32[6]{0:T(128)S(1)} %get-tuple-element.48.number_ref, bf16[128,2048]{1,0:T(8,128)(2,1)S(1)} %collective-permute-done.4.refs_0_, bf16[128,2048]{1,0:T(8,128)(2,1)S(1)} %collective-permute-done.5.refs_1_, ...), custom_call_target="tpu_custom_call" | custom-call | flops 6442450944 | bytes 18350080 | tf_op jit(solution)/shard_map/correlate/pallas_call | solution.py:445
  (7 shorter events, 0.0 us)
Async XLA Ops:
  1.7 19.3 %collective-permute-start = (bf16[128,2048]{1,0:T(8,128)(2,1)S(1)}, bf16[128,2048]{1,0:T(8,128)(2,1)S(1)}, u32[]{:S(2)}, u32[]{:S(2)}) collective-permute-start(bf16[128,2048]{1,0:T(8,128)(2,1)S(1)} %get-tuple-element.50.refs_2_), channel_id=1, source_target_pairs={{0,4},{4,0},{8,12},{12,8},{1,5},{5,1},{9,13},{13,9},{2,6},{6,2},{1... | collective-permute-start | bytes 1572872 | tf_op jit(solution)/shard_map/ppermute | solution.py:28
  1.8 22.2 %collective-permute-start.1 = (bf16[128,2048]{1,0:T(8,128)(2,1)S(1)}, bf16[128,2048]{1,0:T(8,128)(2,1)S(1)}, u32[]{:S(2)}, u32[]{:S(2)}) collective-permute-start(bf16[128,2048]{1,0:T(8,128)(2,1)S(1)} %get-tuple-element.50.refs_2_), channel_id=1, source_target_pairs={{4,8},{8,4},{5,9},{9,5},{6,10},{10,6},{7,11},{11,7},{20,24},{24,20... | collective-permute-start | bytes 1572872 | tf_op jit(solution)/shard_map/ppermute | solution.py:28
  21.0 14.8 %collective-permute-start.2 = (bf16[128,2048]{1,0:T(8,128)(2,1)S(1)}, bf16[128,2048]{1,0:T(8,128)(2,1)S(1)}, u32[]{:S(2)}, u32[]{:S(2)}) collective-permute-start(bf16[128,2048]{1,0:T(8,128)(2,1)S(1)} %collective-permute-done.refs_3_), channel_id=1, source_target_pairs={{4,8},{8,4},{5,9},{9,5},{6,10},{10,6},{7,11},{11,7},{20,24},{24,20... | collective-permute-start | bytes 1572872 | tf_op jit(solution)/shard_map/ppermute | solution.py:28
  24.1 11.8 %collective-permute-start.3 = (bf16[128,2048]{1,0:T(8,128)(2,1)S(1)}, bf16[128,2048]{1,0:T(8,128)(2,1)S(1)}, u32[]{:S(2)}, u32[]{:S(2)}) collective-permute-start(bf16[128,2048]{1,0:T(8,128)(2,1)S(1)} %collective-permute-done.1.refs_1_), channel_id=1, source_target_pairs={{0,4},{4,0},{8,12},{12,8},{1,5},{5,1},{9,13},{13,9},{2,6},{6,2},{1... | collective-permute-start | bytes 1572872 | tf_op jit(solution)/shard_map/ppermute | solution.py:28
  35.9 10.8 %collective-permute-start.6 = (bf16[128,2048]{1,0:T(8,128)(2,1)S(1)}, bf16[128,2048]{1,0:T(8,128)(2,1)S(1)}, u32[]{:S(2)}, u32[]{:S(2)}) collective-permute-start(bf16[128,2048]{1,0:T(8,128)(2,1)S(1)} %collective-permute-done.2.refs_0_), channel_id=1, source_target_pairs={{0,4},{4,0},{8,12},{12,8},{1,5},{5,1},{9,13},{13,9},{2,6},{6,2},{1... | collective-permute-start | bytes 1572872 | tf_op jit(solution)/shard_map/ppermute | solution.py:28
  36.6 17.2 %collective-permute-start.8 = (bf16[128,2048]{1,0:T(8,128)(2,1)S(1)}, bf16[128,2048]{1,0:T(8,128)(2,1)S(1)}, u32[]{:S(2)}, u32[]{:S(2)}) collective-permute-start(bf16[128,2048]{1,0:T(8,128)(2,1)S(1)} %choose.2.refs_0_), channel_id=1, source_target_pairs={{0,1},{1,0},{2,3},{3,2},{4,5},{5,4},{6,7},{7,6},{8,9},{9,8},{10,11... | collective-permute-start | bytes 1572872 | tf_op jit(solution)/shard_map/ppermute | solution.py:33
  39.4 13.5 %collective-permute-start.4 = (bf16[128,2048]{1,0:T(8,128)(2,1)S(1)}, bf16[128,2048]{1,0:T(8,128)(2,1)S(1)}, u32[]{:S(2)}, u32[]{:S(2)}) collective-permute-start(bf16[128,2048]{1,0:T(8,128)(2,1)S(1)} %choose.2.refs_0_), channel_id=1, source_target_pairs={{0,2},{2,0},{1,3},{3,1},{4,6},{6,4},{5,7},{7,5},{8,10},{10,8},{9,1... | collective-permute-start | bytes 1572872 | tf_op jit(solution)/shard_map/ppermute | solution.py:33
  47.5 6.3 %collective-permute-start.9 = (bf16[128,2048]{1,0:T(8,128)(2,1)S(1)}, bf16[128,2048]{1,0:T(8,128)(2,1)S(1)}, u32[]{:S(2)}, u32[]{:S(2)}) collective-permute-start(bf16[128,2048]{1,0:T(8,128)(2,1)S(1)} %choose.3.refs_2_), channel_id=1, source_target_pairs={{0,1},{1,0},{2,3},{3,2},{4,5},{5,4},{6,7},{7,6},{8,9},{9,8},{10,11... | collective-permute-start | bytes 1572872 | tf_op jit(solution)/shard_map/ppermute | solution.py:33
  51.1 15.7 %collective-permute-start.7 = (bf16[128,2048]{1,0:T(8,128)(2,1)S(1)}, bf16[128,2048]{1,0:T(8,128)(2,1)S(1)}, u32[]{:S(2)}, u32[]{:S(2)}) collective-permute-start(bf16[128,2048]{1,0:T(8,128)(2,1)S(1)} %choose.3.refs_2_), channel_id=1, source_target_pairs={{0,2},{2,0},{1,3},{3,1},{4,6},{6,4},{5,7},{7,5},{8,10},{10,8},{9,1... | collective-permute-start | bytes 1572872 | tf_op jit(solution)/shard_map/ppermute | solution.py:33
  52.9 14.0 %collective-permute-start.5 = (bf16[128,2048]{1,0:T(8,128)(2,1)S(1)}, bf16[128,2048]{1,0:T(8,128)(2,1)S(1)}, u32[]{:S(2)}, u32[]{:S(2)}) collective-permute-start(bf16[128,2048]{1,0:T(8,128)(2,1)S(1)} %collective-permute-done.4.refs_0_), channel_id=1, source_target_pairs={{0,1},{1,0},{2,3},{3,2},{4,5},{5,4},{6,7},{7,6},{8,9},{9,8},{10,11... | collective-permute-start | bytes 1572872 | tf_op jit(solution)/shard_map/ppermute | solution.py:33
  66.9 2.0 %collective-permute-start.10 = (bf16[128,2048]{1,0:T(8,128)(2,1)S(1)}, bf16[128,2048]{1,0:T(8,128)(2,1)S(1)}, u32[]{:S(2)}, u32[]{:S(2)}) collective-permute-start(bf16[128,2048]{1,0:T(8,128)(2,1)S(1)} %collective-permute-done.7.refs_2_), channel_id=1, source_target_pairs={{0,1},{1,0},{2,3},{3,2},{4,5},{5,4},{6,7},{7,6},{8,9},{9,8},{10,11... | collective-permute-start | bytes 1572872 | tf_op jit(solution)/shard_map/ppermute | solution.py:33
where the time goes:
time: 86 us
  Pallas kernels  51.5 us (60%)
  starting transfers between devices  15.6 us (18%)
  blocking collectives  14.7 us (17%)
  waiting for transfers between devices  4.17 us (5%)
    pallas_call x2, Pallas kernels, correlate(): pl.pallas_call(body, grid_spec=pltpu.PrefetchScalarGridSpec(num_scalar_pr...  30.2 us
    all_to_all x1, blocking collectives, shards(): lax.all_to_all(parcels, ('chan', 'win'), split_axis=0, concat_axis=0, til...  14.7 us
    pallas_call x2, Pallas kernels, build_hankel(): pl.pallas_call(functools.partial(hankel_kernel, v, samples), grid_spec=pl...  12.8 us
    ppermute x6, starting transfers between devices, turned(): lax.ppermute(block, axis, [(i, (i + distance) % size) for i in range(size)])  7.83 us
    ppermute x5, starting transfers between devices, swapped(): return lax.ppermute(block, axis, route)  7.72 us
    pallas_call x1, Pallas kernels, index(): pl.pallas_call(functools.partial(index_kernel, r_dev, n_win, samples, cap...  5.27 us
    ppermute x6, waiting for transfers between devices, turned(): lax.ppermute(block, axis, [(i, (i + distance) % size) for i in range(size)])  3.5 us
    pallas_call x1, Pallas kernels, pack(): pl.pallas_call(functools.partial(pack_kernel, halves, lags), in_specs=[pl...  1.73 us
  transfers between devices with their start and end apart: 11, of which 3 were waited for; matrix products, arithmetic and copies ran while one was open for 0% of the time, Pallas kernels for 38%

commit v1 on v0

v1 whole, which is shorter than its diff:
```python
import functools
import math

import jax
import jax.numpy as jnp
from jax import lax
from jax.experimental import pallas as pl
from jax.experimental.pallas import tpu as pltpu
from jax.sharding import PartitionSpec as P

LAGS = 2048
LANES = 128
SHIFT_ROWS = 8
STEP = 2 * LANES
CHAINS = 1
SPARE = 16
DIGIT = 64
HANKEL_BYTES = 24 * 2**20
VMEM_BYTES = 26 * 2**20
F32 = jnp.float32
BF16 = jnp.bfloat16


def swapped(block, axis, first):
    size = lax.axis_size(axis)
    route = []
    for i in range(first, size - 1, 2):
        route += [(i, i + 1), (i + 1, i)]
    return lax.ppermute(block, axis, route)


def turned(block, axis, distance):
    size = lax.axis_size(axis)
    return lax.ppermute(block, axis, [(i, (i + distance) % size) for i in range(size)])


def turned_both(block, chan_distance, win_distance):
    n_chan, n_win = lax.axis_size("chan"), lax.axis_size("win")
    route = []
    for c in range(n_chan):
        for w in range(n_win):
            there = (c + chan_distance) % n_chan * n_win + (w + win_distance) % n_win
            route.append((c * n_win + w, there))
    return lax.ppermute(block, ("chan", "win"), route)


def in_hbm(array):
    return pltpu.with_memory_space_constraint(array, pltpu.HBM)


def params(vmem):
    return pltpu.CompilerParams(vmem_limit_bytes=vmem)


def pack_kernel(halves, lags, block_rows, plan_hbm, receiver_hbm, pair_hbm, keep_hbm, *refs):
    plan_ref, receiver_ref, pair_ref, keep_ref, digit_ref, sems = refs[-6:]
    parcel_refs, number_ref = refs[:-7], refs[-7]
    small = []
    for place, (source, target) in enumerate(
        ((plan_hbm, plan_ref), (receiver_hbm, receiver_ref), (pair_hbm, pair_ref), (keep_hbm, keep_ref))
    ):
        small.append(pltpu.make_async_copy(source, target, sems.at[place]))
        small[-1].start()
    r_dev, samples = receiver_ref.shape
    n_chan, cap = pair_ref.shape
    n_win = lax.axis_size("win")
    chan, win, rep = lax.axis_index("chan"), lax.axis_index("win"), lax.axis_index("rep")
    for copy in small:
        copy.wait()

    packed = pair_ref[...] * 2 + keep_ref[...]
    digit_ref[:n_chan, :] = jnp.concatenate([packed // DIGIT, packed % DIGIT], axis=1).astype(F32)
    heard = receiver_ref[...].astype(F32)
    part = 2 * cap // r_dev
    spare = parcel_refs[0].shape[1] - samples - part
    for distance, parcel_ref in enumerate(parcel_refs):
        digits = digit_ref[pl.ds(lax.rem(chan + distance, n_chan), 1), :]
        lists = [digits[:, i * part : (i + 1) * part] for i in range(r_dev)]
        parcel = [heard, jnp.concatenate(lists, axis=0)]
        if spare:
            parcel.append(jnp.zeros((r_dev, spare), F32))
        parcel_ref[...] = jnp.concatenate(parcel, axis=1).astype(BF16)

    one, two = plan_ref[0, 0], plan_ref[0, 1]
    nearer = jnp.where(jnp.abs(one - chan) <= jnp.abs(two - chan), 0, 1)
    sign = jnp.where(chan % 2 == 0, 1, -1)
    number_ref[0] = nearer
    number_ref[1] = block_rows - rep * (block_rows // halves)
    number_ref[2] = sign * (jnp.where(nearer == 0, one, two) - chan)
    number_ref[3] = sign * (jnp.where(nearer == 0, two, one) - chan)
    number_ref[4] = chan
    number_ref[5] = (win * halves + rep) * lags
    number_ref[6] = win


def pack(plan, receivers, pair_index, keep, halves, lags, block_rows, n_chan):
    r_dev, samples = receivers.shape
    cap = pair_index.shape[1]
    beside = -(-2 * cap // r_dev // LANES) * LANES
    vmem, smem = pl.BlockSpec(memory_space=pltpu.VMEM), pl.BlockSpec(memory_space=pltpu.SMEM)
    shapes = [jax.ShapeDtypeStruct((r_dev, samples + beside), BF16)] * n_chan
    shapes.append(jax.ShapeDtypeStruct((7,), jnp.int32))
    *parcels, numbers = pl.pallas_call(
        functools.partial(pack_kernel, halves, lags, block_rows),
        in_specs=[pl.BlockSpec(memory_space=pl.ANY)] * 4,
        out_specs=[vmem] * n_chan + [smem],
        out_shape=shapes,
        scratch_shapes=[
            pltpu.SMEM(plan.shape, plan.dtype),
            pltpu.VMEM(receivers.shape, receivers.dtype),
            pltpu.VMEM(pair_index.shape, pair_index.dtype),
            pltpu.VMEM(keep.shape, keep.dtype),
            pltpu.VMEM((-(-n_chan // SHIFT_ROWS) * SHIFT_ROWS, 2 * cap), F32),
            pltpu.SemaphoreType.DMA((4,)),
        ],
        compiler_params=params(VMEM_BYTES // 2),
        name="pack",
    )(*[in_hbm(a) for a in (plan, receivers, pair_index, keep)])
    return parcels, numbers


def own_kernel(number_ref, source_ref, *refs):
    chain_refs, sems = refs[:-1], refs[-1]
    rows = chain_refs[0].shape[0]
    copies = []
    for chain, chain_ref in enumerate(chain_refs):
        start = pl.multiple_of(source_ref.shape[0] - number_ref[1] + chain * rows, rows)
        copies.append(pltpu.make_async_copy(source_ref.at[pl.ds(start, rows)], chain_ref, sems.at[chain]))
        copies[-1].start()
    for copy in copies:
        copy.wait()


def own_rows(numbers, sources, halves):
    block_rows, samples = sources.shape
    shape = jax.ShapeDtypeStruct((block_rows // halves // CHAINS, samples), BF16)
    return pl.pallas_call(
        own_kernel,
        in_specs=[pl.BlockSpec(memory_space=pltpu.SMEM), pl.BlockSpec(memory_space=pl.ANY)],
        out_specs=[pl.BlockSpec(memory_space=pltpu.VMEM)] * CHAINS,
        out_shape=[shape] * CHAINS,
        scratch_shapes=[pltpu.SemaphoreType.DMA((CHAINS,))],
        compiler_params=params(VMEM_BYTES // 4),
        name="own_rows",
    )(numbers, in_hbm(sources))


def choose_kernel(which, offsets, number_ref, *refs):
    out_ref, sems = refs[-2:]
    rows = out_ref.shape[0] // CHAINS
    where = number_ref[which]
    waits = []
    for chain in range(CHAINS):
        target = out_ref.at[pl.ds(chain * rows, rows)]
        for place, offset in enumerate(offsets):
            copy = pltpu.make_async_copy(refs[chain * len(offsets) + place], target, sems.at[chain])

            @pl.when(where == offset)
            def _():
                copy.start()

        waits.append(copy)
    for copy in waits:
        copy.wait()


def choose(numbers, which, arrived, offsets):
    pieces = [there[offset] for there in arrived for offset in offsets]
    rows, samples = pieces[0].shape
    any_spec = pl.BlockSpec(memory_space=pl.ANY)
    return pl.pallas_call(
        functools.partial(choose_kernel, which, offsets),
        in_specs=[pl.BlockSpec(memory_space=pltpu.SMEM)] + [any_spec] * len(pieces),
        out_specs=pl.BlockSpec(memory_space=pltpu.VMEM),
        out_shape=jax.ShapeDtypeStruct((rows * CHAINS, samples), BF16),
        scratch_shapes=[pltpu.SemaphoreType.DMA((CHAINS,))],
        compiler_params=params(VMEM_BYTES // 4),
        name="choose",
    )(numbers, *pieces)


def column(row):
    return jnp.broadcast_to(row, (SHIFT_ROWS, row.shape[1])).T[:, :1]


def ones_where(condition):
    return jnp.where(condition, 1.0, 0.0).astype(BF16)


def index_kernel(r_dev, samples, cap, tile, block_rows, number_ref, *refs):
    pick_ref, place_ref, pass_ref, count_ref, more_pick_ref, more_place_ref, pick_scratch, place_scratch = refs[-8:]
    parcel_refs = refs[:-8]
    nearer, offset = number_ref[0], number_ref[1]
    slots = 2 * r_dev * tile
    window = tile + SPARE
    part = 2 * cap // r_dev
    below = lax.broadcasted_iota(jnp.int32, (cap, cap), 0) < lax.broadcasted_iota(jnp.int32, (cap, cap), 1)
    below = ones_where(below)
    later = []
    for group, parcel_ref in enumerate(parcel_refs):
        digits = parcel_ref[:, samples:].astype(F32)
        digits = jnp.concatenate([digits[i : i + 1, :part] for i in range(r_dev)], axis=1).astype(jnp.int32)
        packed = digits[:, :cap] * DIGIT + digits[:, cap:]
        pairs, kept = packed // 2, packed % 2 == 1
        source_row, receiver = pairs // r_dev, pairs % r_dev
        turn = jnp.where(source_row // block_rows == nearer, 0, 1)
        row = (source_row + offset) % block_rows
        segment = jnp.where(kept, turn * r_dev + receiver, -1)
        member = lax.broadcasted_iota(jnp.int32, (2 * r_dev, cap), 0) == segment
        earlier = jnp.dot(ones_where(member), below, preferred_element_type=F32)
        of_pair = lambda values: jnp.sum(jnp.where(member, values, 0.0), axis=0, keepdims=True).astype(jnp.int32)
        counts = jnp.sum(jnp.where(member, 1.0, 0.0), axis=1, keepdims=True)
        from_top = jnp.minimum(counts[:r_dev], window)
        from_bottom = jnp.minimum(jnp.minimum(counts[r_dev:], 2.0 * tile - from_top), window)
        first_pass = jnp.concatenate([from_top, from_bottom], axis=0)
        first_slot = jnp.concatenate([jnp.zeros_like(from_top), 2.0 * tile - from_bottom], axis=0)
        rank, limit, begin = of_pair(earlier), of_pair(first_pass), of_pair(first_slot)
        rest = rank - limit
        code = jnp.where(rest < 0, begin + rank, (1 + rest // tile) * slots + turn * tile + rest % tile)
        code = jnp.where(kept, code + receiver * 2 * tile, -1)
        left = counts - first_pass
        which = lax.broadcasted_iota(jnp.int32, left.shape, 0) % r_dev
        passes = 1
        for r in range(r_dev):
            count = jnp.max(jnp.where(which == r, left, 0.0)).astype(jnp.int32)
            count_ref[group * r_dev + r] = count
            passes = jnp.maximum(passes, 1 + (count + tile - 1) // tile)
        pass_ref[group] = passes
        code_column = column(code.astype(F32)).astype(jnp.int32)
        row_column = column(row.astype(F32)).astype(jnp.int32)

        def matrices(number, code=code, turn=turn, code_column=code_column, row_column=row_column):
            start = number * slots
            row_ones = ones_where(row_column == lax.broadcasted_iota(jnp.int32, (cap, block_rows), 1))
            line = lax.broadcasted_iota(jnp.int32, (r_dev * window, 1), 0)
            slot = line // window * (2 * tile) + line % window + start
            of_block = [jnp.where(turn == q, code - q * (2 * tile - window), -1) for q in range(2)]
            by_slot = jnp.concatenate([ones_where(slot == codes) for codes in of_block], axis=0)
            pick = jnp.dot(by_slot, row_ones, preferred_element_type=F32).astype(BF16)
            return pick, ones_where(lax.broadcasted_iota(jnp.int32, (cap, slots), 1) + start == code_column)

        pick_ref[group], place_ref[group] = matrices(0)
        later.append((group, passes, matrices))

    for group, passes, matrices in later:

        @pl.when(passes > 1)
        def _():
            def one_pass(number, carry):
                pick_scratch[...], place_scratch[...] = matrices(number)
                pltpu.sync_copy(pick_scratch, more_pick_ref.at[group, number - 1])
                pltpu.sync_copy(place_scratch, more_place_ref.at[group, number - 1])
                return carry

            lax.fori_loop(1, passes, one_pass, 0)


def index(parcels, numbers, samples, r_dev, cap, tile, block_rows):
    groups = len(parcels)
    slots = 2 * r_dev * tile
    lines = 2 * r_dev * (tile + SPARE)
    more = -(-(min(block_rows, cap) - (tile - SPARE)) // tile)
    vmem, smem = pl.BlockSpec(memory_space=pltpu.VMEM), pl.BlockSpec(memory_space=pltpu.SMEM)
    any_spec = pl.BlockSpec(memory_space=pl.ANY)
    return pl.pallas_call(
        functools.partial(index_kernel, r_dev, samples, cap, tile, block_rows),
        in_specs=[smem] + [vmem] * groups,
        out_specs=[vmem, vmem, smem, smem, any_spec, any_spec],
        out_shape=[
            jax.ShapeDtypeStruct((groups, lines, block_rows), BF16),
            jax.ShapeDtypeStruct((groups, cap, slots), BF16),
            jax.ShapeDtypeStruct((groups,), jnp.int32),
            jax.ShapeDtypeStruct((groups * r_dev,), jnp.int32),
            pltpu.HBM((groups, more, lines, block_rows), BF16),
            pltpu.HBM((groups, more, cap, slots), BF16),
        ],
        scratch_shapes=[pltpu.VMEM((lines, block_rows), BF16), pltpu.VMEM((cap, slots), BF16)],
        compiler_params=params(VMEM_BYTES),
        name="index",
    )(numbers, *parcels)


def lay_out(heard, number_ref, signal_ref):
    n_win = len(heard)
    r_dev, samples = heard[0].shape
    for distance, span in enumerate(heard):
        begin = lax.rem(number_ref[6] + n_win - distance, n_win) * samples
        signal_ref[:r_dev, pl.ds(pl.multiple_of(begin, LANES), samples)] = span.astype(F32)
    tail = signal_ref.shape[1] - n_win * samples
    signal_ref[:r_dev, n_win * samples :] = jnp.zeros((r_dev, tail), F32)


def first_sample(number_ref, v, n_win, samples):
    return lax.rem(number_ref[6] + n_win - v, n_win) * samples + number_ref[5]


def hankel_rows(signal_ref, r, begin, width, out_ref, place):
    length = width + LANES
    signal = signal_ref[r : r + 1, pl.ds(pl.multiple_of(begin, LANES), length)]
    base = jnp.broadcast_to(signal, (SHIFT_ROWS, length))
    sublane = lax.broadcasted_iota(jnp.int32, base.shape, 0)
    for bit in (1, 2, 4):
        base = jnp.where(sublane & bit != 0, pltpu.roll(base, length - bit, 1), base)
    for first in range(0, LANES, 2 * SHIFT_ROWS):
        both = []
        for shift in (first, first + SHIFT_ROWS):
            rolled = pltpu.roll(base, length - shift, 1) if shift else base
            both.append(rolled[:, :width])
        out_ref[place, first : first + 2 * SHIFT_ROWS, :] = jnp.concatenate(both, axis=0).astype(BF16)


def hankel_kernel(v, n_win, samples, number_ref, *refs):
    out_ref, signal_refs = refs[-2:]
    heard_refs = refs[:-2]
    r_dev = heard_refs[0].shape[0]
    begin = first_sample(number_ref, v, n_win, samples)
    for group in range(len(heard_refs) // n_win):
        signal_ref = signal_refs.at[group % 2]
        heard = [ref[:, :samples] for ref in heard_refs[group * n_win : (group + 1) * n_win]]
        lay_out(heard, number_ref, signal_ref)
        for r in range(r_dev):
            hankel_rows(signal_ref, r, begin, out_ref.shape[2], out_ref, group * r_dev + r)


def build_hankel(heard, numbers, v, samples, width):
    groups, n_win, r_dev = len(heard), len(heard[0]), heard[0][0].shape[0]
    shape = (groups * r_dev, LANES, width)
    vmem = pl.BlockSpec(memory_space=pltpu.VMEM)
    return pl.pallas_call(
        functools.partial(hankel_kernel, v, n_win, samples),
        in_specs=[pl.BlockSpec(memory_space=pltpu.SMEM)] + [vmem] * (groups * n_win),
        out_specs=vmem,
        scratch_shapes=[pltpu.VMEM((2, SHIFT_ROWS, n_win * samples + LAGS), F32)],
        out_shape=jax.ShapeDtypeStruct(shape, BF16),
        cost_estimate=pl.CostEstimate(
            flops=math.prod(shape), bytes_accessed=2 * math.prod(shape), transcendentals=0
        ),
        compiler_params=params(VMEM_BYTES // 2),
        name="hankel",
    )(numbers, *[span for spans in heard for span in spans])


def pick_rows(pieces, pick, gathered, tile):
    parts = len(pieces) // 2
    window = tile + SPARE
    shared = tile - SPARE
    r_dev, samples = gathered.shape[0] // (2 * tile), gathered.shape[1]
    for t in range(0, samples, STEP):
        chosen = []
        for q in range(2):
            block = jnp.concatenate([piece[:, t : t + STEP] for piece in pieces[q * parts : (q + 1) * parts]], axis=0)
            ones = pick[q * r_dev * window : (q + 1) * r_dev * window, :]
            chosen.append(jnp.dot(ones, block, preferred_element_type=F32))
        for r in range(r_dev):
            top, bottom = [rows[r * window : (r + 1) * window] for rows in chosen]
            rows = [top[shared:] + bottom[: window - shared]]
            if shared:
                rows = [top[:shared]] + rows + [bottom[window - shared :]]
            for place, part in zip((0, shared, window) if shared else (0,), rows):
                start = r * 2 * tile + place
                gathered[start : start + part.shape[0], t : t + STEP] = part.astype(BF16)


def multiply(gathered, hankel_ref, place, r, tile, lag):
    samples = gathered.shape[1]
    wide = jnp.concatenate(
        [hankel_ref[place, :, t + lag : t + lag + STEP] for t in range(0, samples, LANES)], axis=0
    )
    return jnp.dot(gathered[r * 2 * tile : (r + 1) * 2 * tile, :], wide, preferred_element_type=F32)


def split(total, high, low, slots, lags):
    upper = total.astype(BF16)
    high[slots, lags] = upper
    low[slots, lags] = (total - upper.astype(F32)).astype(BF16)


def placed(place, high, low):
    return jnp.dot(place, high[...], preferred_element_type=F32) + jnp.dot(
        place, low[...], preferred_element_type=F32
    )


def correlate_kernel(parts, v, tile, norming, prebuilt, first, last, pass_ref, count_ref, number_ref, *refs):
    refs = list(refs)
    pieces = [refs.pop(0) for _ in range(2 * parts)]
    signal_ref, pick_ref, place_ref, more_pick_ref, more_place_ref = [refs.pop(0) for _ in range(5)]
    if not first:
        sums_ref, extra_ref = refs.pop(0), refs.pop(0)
    if last:
        out_ref = refs.pop(0)
    else:
        handed_ref, left_ref = refs.pop(0), refs.pop(0)
    gathered, high, low, extra, pick_scratch, place_scratch = refs[:6]
    r_dev = gathered.shape[0] // (2 * tile)
    samples = pieces[0].shape[1]
    lag_dev = extra.shape[1]
    group = pl.program_id(0)

    if prebuilt:
        hankel_ref, hankel_place = signal_ref, group * r_dev
    else:
        hankel_place = 0
        hankel_ref, row_ref = refs[6:]
        n_win = signal_ref.shape[1]
        lay_out([signal_ref[0, w] for w in range(n_win)], number_ref, row_ref)
        begin = first_sample(number_ref, v, n_win, samples)
        for r in range(r_dev):
            hankel_rows(row_ref, r, begin, hankel_ref.shape[2], hankel_ref, r)

    pick_rows(pieces, pick_ref.at[0], gathered, tile)
    for r in range(r_dev):
        slots = slice(r * 2 * tile, (r + 1) * 2 * tile)
        for lag in range(0, lag_dev, STEP):
            lags = slice(lag, lag + STEP)
            total = multiply(gathered, hankel_ref, hankel_place + r, r, tile, lag)
            if not first:
                total += sums_ref[group, slots, lags]
            if last:
                split(total * norming, high, low, slots, lags)
            else:
                handed_ref[group, slots, lags] = total
    if last:
        out_ref[0] = placed(place_ref[0], high, low)

    @pl.when(pass_ref[group] > 1)
    def _():
        if first:
            extra[...] = jnp.zeros(extra.shape, F32)
        else:
            pltpu.sync_copy(extra_ref.at[group], extra)

        def one_pass(number, carry):
            pltpu.sync_copy(more_pick_ref.at[group, number - 1], pick_scratch)
            pltpu.sync_copy(more_place_ref.at[group, number - 1], place_scratch)
            pick_rows(pieces, pick_scratch, gathered, tile)
            for r in range(r_dev):
                needed = count_ref[group * r_dev + r] > (number - 1) * tile
                slots = slice(r * 2 * tile, (r + 1) * 2 * tile)

                @pl.when(needed)
                def _():
                    for lag in range(0, lag_dev, STEP):
                        total = multiply(gathered, hankel_ref, hankel_place + r, r, tile, lag)
                        split(total * norming, high, low, slots, slice(lag, lag + STEP))

                @pl.when(jnp.logical_not(needed))
                def _():
                    high[slots, :] = jnp.zeros((2 * tile, lag_dev), BF16)
                    low[slots, :] = jnp.zeros((2 * tile, lag_dev), BF16)

            extra[...] += placed(place_scratch[...], high, low)
            return carry

        lax.fori_loop(1, pass_ref[group], one_pass, 0)
        if last:
            out_ref[0] += extra[...]
        else:
            pltpu.sync_copy(extra, left_ref.at[group])


def correlate(pieces, signal, prebuilt, numbers, v, matrices, before, last, tile, norming, lag_dev, n_win, r_dev):
    pick, place, passes, counts, more_pick, more_place = matrices
    parts = len(pieces) // 2
    groups, cap, slots = place.shape
    part_rows, samples = pieces[0].shape
    width = samples - LANES + lag_dev
    by_group = lambda shape: pl.BlockSpec(shape, lambda i, *_: (i, 0, 0))
    any_spec = pl.BlockSpec(memory_space=pl.ANY)
    whole_spec = pl.BlockSpec(memory_space=pltpu.VMEM)
    out_spec = pl.BlockSpec(
        (1, cap, lag_dev), lambda i, _, __, number_ref: (lax.rem(number_ref[4] + groups - i, groups), 0, 0)
    )
    sums_shape = jax.ShapeDtypeStruct((groups, slots, lag_dev), F32)
    out_shape = jax.ShapeDtypeStruct((groups, cap, lag_dev), F32)
    in_specs = [whole_spec] * len(pieces)
    in_specs.append(whole_spec if prebuilt else pl.BlockSpec((1,) + signal.shape[1:], lambda i, *_: (i, 0, 0, 0)))
    in_specs += [by_group((1,) + pick.shape[1:]), by_group((1,) + place.shape[1:]), any_spec, any_spec]
    args = pieces + [signal, pick, place, in_hbm(more_pick), in_hbm(more_place)]
    if before is not None:
        in_specs += [whole_spec, any_spec]
        args += [before[0], in_hbm(before[1])]
    scratch = [
        pltpu.VMEM((slots, samples), BF16),
        pltpu.VMEM((slots, lag_dev), BF16),
        pltpu.VMEM((slots, lag_dev), BF16),
        pltpu.VMEM((cap, lag_dev), F32),
        pltpu.VMEM(pick.shape[1:], BF16),
        pltpu.VMEM(place.shape[1:], BF16),
    ]
    if not prebuilt:
        scratch.append(pltpu.VMEM((r_dev, LANES, width), BF16))
        scratch.append(pltpu.VMEM((SHIFT_ROWS, n_win * samples + LAGS), F32))
    body = functools.partial(correlate_kernel, parts, v, tile, norming, prebuilt, before is None, last)
    return pl.pallas_call(
        body,
        grid_spec=pltpu.PrefetchScalarGridSpec(
            num_scalar_prefetch=3,
            grid=(groups,),
            in_specs=in_specs,
            out_specs=out_spec if last else [whole_spec, any_spec],
            scratch_shapes=scratch,
        ),
        out_shape=out_shape if last else [sums_shape, pltpu.HBM(out_shape.shape, F32)],
        cost_estimate=pl.CostEstimate(
            flops=4 * groups * r_dev * tile * samples * (lag_dev + parts * part_rows),
            bytes_accessed=signal.size * signal.dtype.itemsize + 2 * groups * cap * lag_dev * 4,
            transcendentals=0,
        ),
        compiler_params=params(VMEM_BYTES if prebuilt else 2 * VMEM_BYTES),
        name="correlate",
    )(passes, counts, numbers, *args)


def shards(sources, receivers, plan, pair_index, keep):
    _, block_rows, samples = sources.shape
    r_dev = receivers.shape[0]
    n_chan = lax.axis_size("chan")
    n_win = lax.axis_size("win")
    n_rep = lax.axis_size("rep")
    cap = pair_index.shape[3]
    lag_dev = LAGS // (n_win * n_rep)
    tile = max(16, cap // 8)
    norming = 1.0 / math.sqrt(samples * n_win)
    width = samples - LANES + lag_dev
    prebuilt = n_chan * r_dev * n_win * LANES * width * 2 <= HANKEL_BYTES

    parcels, numbers = pack(plan, receivers, pair_index[0, 0], keep[0, 0], n_rep, lag_dev, block_rows, n_chan)
    parcels = [parcels[0]] + [turned(parcels[k], "chan", k) for k in range(1, n_chan)]
    heard = [[parcel] for parcel in parcels]
    for k in range(n_chan):
        heard[k] += [turned_both(receivers, k, v) for v in range(1, n_win)]
    owns = own_rows(numbers, sources[0], n_rep)

    arrived = [{0: own} for own in owns]

    def relay(step):
        for there in arrived:
            there[step] = swapped(there[1 - step], "chan", 0)
            if step < n_chan - 1:
                there[-step] = swapped(there[step - 1], "chan", 1)

    def after_arrival(step, value):
        for there in arrived:
            for key in (step, -step):
                if key in there:
                    value, there[key] = lax.optimization_barrier((value, there[key]))
        return value

    def before_start(step, value):
        for there in arrived:
            for key in (1 - step, step - 1):
                value, there[key] = lax.optimization_barrier((value, there[key]))
        return value

    def halves(piece):
        return [piece] + [turned(piece, "rep", -u) for u in range(1, n_rep)]

    def spans(piece):
        return [piece] + [turned(piece, "win", v) for v in range(1, n_win)]

    relay(1)
    matrices = index(parcels, numbers, samples, r_dev, cap, tile, block_rows)
    if prebuilt:
        signals = [build_hankel(heard, numbers, 0, samples, width)]
        matrices, signals = before_start(2, (matrices, signals))
    else:
        signals = [jnp.stack([jnp.stack([span[:, :samples] for span in spans_of]) for spans_of in heard])] * n_win
    relay(2)
    reach = range(-(n_chan - 2), n_chan - 1)
    near = choose(numbers, 2, arrived, [offset for offset in reach if offset in arrived[0]])
    if prebuilt:
        heard = after_arrival(1, heard)
        signals += [build_hankel(heard, numbers, v, samples, width) for v in range(1, n_win)]
        signals = before_start(3, signals)
    for step in range(3, n_chan):
        relay(step)
    near_halves = [halves(piece) for piece in spans(near)]
    far_spans = spans(choose(numbers, 3, arrived, sorted(arrived[0])))

    result = None
    for v in range(n_win):
        if v:
            far_spans, result = lax.optimization_barrier((far_spans, result))
        result = correlate(
            near_halves[v] + halves(far_spans[v]), signals[v], prebuilt, numbers, v, matrices, result, v == n_win - 1,
            tile, norming, lag_dev, n_win, r_dev,
        )
    return result[None, None]


def solution(mesh):
    placed_at = (
        P(("grp", "chan"), None, "win"),
        P(("grp", "chan"), "win"),
        P("grp", None),
        P("grp", "chan", None, None),
        P("grp", "chan", None, None),
    )
    return jax.shard_map(
        shards,
        mesh=mesh,
        in_specs=placed_at,
        out_specs=P(("grp", "chan"), None, None, None, ("win", "rep")),
        check_vma=False,
    )
```

time: 86 us -> 95.7 us (1.11)
  the two profiles are of different devices: /device:TPU:9 before, /device:TPU:0 now
where the time goes in v1:
time: 95.7 us; the launch traced here: 95.5 us
  Pallas kernels  41.3 us (43%)
  waiting for transfers between devices  27.9 us (29%)
  starting transfers between devices  26.1 us (27%)
    pallas_call x2, Pallas kernels, correlate(): pl.pallas_call(body, grid_spec=pltpu.PrefetchScalarGridSpec(num_scalar_pr...  20.4 us
    ppermute x9, waiting for transfers between devices, turned(): lax.ppermute(block, axis, [(i, (i + distance) % size) for i in range(size)])  18 us
    ppermute x5, starting transfers between devices, swapped(): return lax.ppermute(block, axis, route)  14.2 us
    pallas_call x2, Pallas kernels, build_hankel(): pl.pallas_call(functools.partial(hankel_kernel, v, n_win, samples), in_sp...  12.9 us
    ppermute x5, waiting for transfers between devices, swapped(): return lax.ppermute(block, axis, route)  9.4 us
    ppermute x4, starting transfers between devices, turned_both(): return lax.ppermute(block, ('chan', 'win'), route)  6.74 us
    ppermute x9, starting transfers between devices, turned(): lax.ppermute(block, axis, [(i, (i + distance) % size) for i in range(size)])  5.15 us
    pallas_call x1, Pallas kernels, index(): pl.pallas_call(functools.partial(index_kernel, r_dev, samples, cap, tile,...  3.77 us
  transfers between devices with their start and end apart: 18, of which 7 were waited for; matrix products, arithmetic and copies ran while one was open for 0% of the time, Pallas kernels for 28%

profile of v1, /device:TPU:0, one launch (start us, length us, event | category | flops | bytes accessed | tf_op | source)
XLA Modules:
  0.0 95.5 jit_solution(1164633060498506016)
XLA Ops:
  0.0 1.4 %pack.1 = (bf16[4,2304]{1,0:T(4,128)(2,1)S(1)}, bf16[4,2304]{1,0:T(4,128)(2,1)S(1)}, bf16[4,2304]{1,0:T(4,128)(2,1)S(1)}, bf16[4,2304]{1,0:T(4,128)(2,1)S(1)}, s32[7]{0:T(128)S(1)}) custom-call(s32[1,2]{1,0:T(1,128)} %plan_hbm.1, bf16[4,2048]{1,0:T(4,128)(2,1)} %receiver_hbm.1, s32[4,512]{1,0:T(4,128)} %bitcast.5, s32[4,512]{1,0:T(4,128)} %bitcast.6), custom_call_target="tpu_custom_call" | custom-call | tf_op jit(solution)/shard_map/pack/pallas_call | solution.py:103
  1.4 1.6 %own_rows.1.refs_2_ = bf16[128,2048]{1,0:T(8,128)(2,1)S(1)} custom-call(s32[7]{0:T(128)S(1)} %get-tuple-element.61.number_ref, bf16[256,2048]{1,0:T(8,128)(2,1)} %bitcast.4), custom_call_target="tpu_custom_call" | custom-call | tf_op jit(solution)/shard_map/own_rows/pallas_call | solution.py:137
  3.7 5.9 %collective-permute-start.8 = (bf16[128,2048]{1,0:T(8,128)(2,1)S(1)}, bf16[128,2048]{1,0:T(8,128)(2,1)S(1)}, u32[]{:S(2)}, u32[]{:S(2)}) collective-permute-start(bf16[128,2048]{1,0:T(8,128)(2,1)S(1)} %own_rows.1.refs_2_), channel_id=1, source_target_pairs={{0,4},{4,0},{8,12},{12,8},{1,5},{5,1},{9,13},{13,9},{2,6},{6,2},{1... | collective-permute-start | bytes 1572872 | tf_op jit(solution)/shard_map/ppermute | solution.py:29
  9.6 1.5 %collective-permute-start.3 = (bf16[4,2048]{1,0:T(4,128)(2,1)}, bf16[4,2048]{1,0:T(4,128)(2,1)S(1)}, u32[]{:S(2)}, u32[]{:S(2)}) collective-permute-start(bf16[4,2048]{1,0:T(4,128)(2,1)} %receiver_hbm.1), channel_id=1, source_target_pairs={{0,2},{2,0},{4,6},{6,4},{8,10},{10,8},{12,14},{14,12},{1,3},{3,1},... | collective-permute-start | bytes 49160 | tf_op jit(solution)/shard_map/ppermute | solution.py:44
  11.2 1.8 %collective-permute-start.1 = (bf16[4,2304]{1,0:T(4,128)(2,1)S(1)}, bf16[4,2304]{1,0:T(4,128)(2,1)S(1)}, u32[]{:S(2)}, u32[]{:S(2)}) collective-permute-start(bf16[4,2304]{1,0:T(4,128)(2,1)S(1)} %get-tuple-element.64), channel_id=1, source_target_pairs={{0,8},{4,12},{8,0},{12,4},{1,9},{5,13},{9,1},{13,5},{2,10},{6,14},... | collective-permute-start | bytes 55304 | tf_op jit(solution)/shard_map/ppermute | solution.py:34
  13.5 1.4 %collective-permute-start.2 = (bf16[4,2304]{1,0:T(4,128)(2,1)S(1)}, bf16[4,2304]{1,0:T(4,128)(2,1)S(1)}, u32[]{:S(2)}, u32[]{:S(2)}) collective-permute-start(bf16[4,2304]{1,0:T(4,128)(2,1)S(1)} %get-tuple-element.65), channel_id=1, source_target_pairs={{0,12},{4,0},{8,4},{12,8},{1,13},{5,1},{9,5},{13,9},{2,14},{6,2},{... | collective-permute-start | bytes 55304 | tf_op jit(solution)/shard_map/ppermute | solution.py:34
  14.9 8.2 %collective-permute-done.refs_1_.refs_2_ = bf16[4,2304]{1,0:T(4,128)(2,1)S(1)} collective-permute-done((bf16[4,2304]{1,0:T(4,128)(2,1)S(1)}, bf16[4,2304]{1,0:T(4,128)(2,1)S(1)}, u32[]{:S(2)}, u32[]{:S(2)}) %collective-permute-start) | collective-permute-done | bytes 18464 | tf_op jit(solution)/shard_map/ppermute | solution.py:34
  23.1 1.6 %collective-permute-start.4 = (bf16[4,2048]{1,0:T(4,128)(2,1)}, bf16[4,2048]{1,0:T(4,128)(2,1)S(1)}, u32[]{:S(2)}, u32[]{:S(2)}) collective-permute-start(bf16[4,2048]{1,0:T(4,128)(2,1)} %receiver_hbm.1), channel_id=1, source_target_pairs={{0,6},{2,4},{4,10},{6,8},{8,14},{10,12},{12,2},{14,0},{1,7},{3,5},... | collective-permute-start | bytes 49160 | tf_op jit(solution)/shard_map/ppermute | solution.py:44
  24.7 1.1 %collective-permute-start.5 = (bf16[4,2048]{1,0:T(4,128)(2,1)}, bf16[4,2048]{1,0:T(4,128)(2,1)S(1)}, u32[]{:S(2)}, u32[]{:S(2)}) collective-permute-start(bf16[4,2048]{1,0:T(4,128)(2,1)} %receiver_hbm.1), channel_id=1, source_target_pairs={{0,10},{2,8},{4,14},{6,12},{8,2},{10,0},{12,6},{14,4},{1,11},{3,9}... | collective-permute-start | bytes 49160 | tf_op jit(solution)/shard_map/ppermute | solution.py:44
  25.8 2.5 %collective-permute-start.6 = (bf16[4,2048]{1,0:T(4,128)(2,1)}, bf16[4,2048]{1,0:T(4,128)(2,1)S(1)}, u32[]{:S(2)}, u32[]{:S(2)}) collective-permute-start(bf16[4,2048]{1,0:T(4,128)(2,1)} %receiver_hbm.1), channel_id=1, source_target_pairs={{0,14},{2,12},{4,2},{6,0},{8,6},{10,4},{12,10},{14,8},{1,15},{3,13... | collective-permute-start | bytes 49160 | tf_op jit(solution)/shard_map/ppermute | solution.py:44
  28.3 3.8 %index.1 = (bf16[4,640,256]{2,1,0:T(8,128)(2,1)S(1)}, bf16[4,512,512]{2,1,0:T(8,128)(2,1)S(1)}, s32[4]{0:T(128)S(1)}, s32[16]{0:T(128)S(1)}, bf16[4,4,640,256]{3...) custom-call(s32[7]{0:T(128)S(1)} %get-tuple-element.61.number_ref, bf16[4,2304]{1,0:T(4,128)(2,1)S(1)} %get-tuple-element.92.refs_0_, ...), custom_call_target="tpu_custom_call" | custom-call | tf_op jit(solution)/shard_map/index/pallas_call | solution.py:265
  32.1 6.4 %hankel.2.refs_4_ = bf16[16,128,2432]{2,1,0:T(8,128)(2,1)S(1)} custom-call(s32[7]{0:T(128)S(1)} %get-tuple-element.61.number_ref, bf16[4,2304]{1,0:T(4,128)(2,1)S(1)} %get-tuple-element.92.refs_0_, bf16[4,2048]{1,0:T(4,128)(2,1)S(1)} %collective-permute-done.3.refs_1_, bf16[4,2304]{1,0:T(4,128)(2,1)S(1)} %collective-permute-done.refs_1_.refs_2_, ...), custom_call_target="tpu_custom_call" | custom-call | flops 4980736 | bytes 9961472 | tf_op jit(solution)/shard_map/hankel/pallas_call | solution.py:329
  38.6 0.9 collective-permute-start.9
  39.5 4.3 %collective-permute-start.10 = (bf16[128,2048]{1,0:T(8,128)(2,1)S(1)}, bf16[128,2048]{1,0:T(8,128)(2,1)S(1)}, u32[]{:S(2)}, u32[]{:S(2)}) collective-permute-start(bf16[128,2048]{1,0:T(8,128)(2,1)S(1)} %collective-permute-done.7.refs_1_), channel_id=1, source_target_pairs={{0,4},{4,0},{8,12},{12,8},{1,5},{5,1},{9,13},{13,9},{2,6},{6,2},{1... | collective-permute-start | bytes 1572872 | tf_op jit(solution)/shard_map/ppermute | solution.py:29
  43.8 6.4 %hankel.3.refs_4_ = bf16[16,128,2432]{2,1,0:T(8,128)(2,1)S(1)} custom-call(s32[7]{0:T(128)S(1)} %get-tuple-element.61.number_ref, bf16[4,2304]{1,0:T(4,128)(2,1)S(1)} %get-tuple-element.92.refs_0_, bf16[4,2048]{1,0:T(4,128)(2,1)S(1)} %collective-permute-done.3.refs_1_, bf16[4,2304]{1,0:T(4,128)(2,1)S(1)} %collective-permute-done.refs_1_.refs_2_, ...), custom_call_target="tpu_custom_call" | custom-call | flops 4980736 | bytes 9961472 | tf_op jit(solution)/shard_map/hankel/pallas_call | solution.py:329
  50.2 2.5 %collective-permute-start.13 = (bf16[128,2048]{1,0:T(8,128)(2,1)S(1)}, bf16[128,2048]{1,0:T(8,128)(2,1)S(1)}, u32[]{:S(2)}, u32[]{:S(2)}) collective-permute-start(bf16[128,2048]{1,0:T(8,128)(2,1)S(1)} %collective-permute-done.9.refs_0_), channel_id=1, source_target_pairs={{0,4},{4,0},{8,12},{12,8},{1,5},{5,1},{9,13},{13,9},{2,6},{6,2},{1... | collective-permute-start | bytes 1572872 | tf_op jit(solution)/shard_map/ppermute | solution.py:29
  52.7 2.7 %collective-permute-done.10.refs_4_ = bf16[128,2048]{1,0:T(8,128)(2,1)S(1)} collective-permute-done((bf16[128,2048]{1,0:T(8,128)(2,1)S(1)}, bf16[128,2048]{1,0:T(8,128)(2,1)S(1)}, u32[]{:S(2)}, u32[]{:S(2)}) %collective-permute-start.10) | collective-permute-done | bytes 524320 | tf_op jit(solution)/shard_map/ppermute | solution.py:29
  56.1 1.1 %collective-permute-start.11 = (bf16[128,2048]{1,0:T(8,128)(2,1)S(1)}, bf16[128,2048]{1,0:T(8,128)(2,1)S(1)}, u32[]{:S(2)}, u32[]{:S(2)}) collective-permute-start(bf16[128,2048]{1,0:T(8,128)(2,1)S(1)} %choose.2.refs_0_), channel_id=1, source_target_pairs={{0,2},{2,0},{1,3},{3,1},{4,6},{6,4},{5,7},{7,5},{8,10},{10,8},{9,1... | collective-permute-start | bytes 1572872 | tf_op jit(solution)/shard_map/ppermute | solution.py:34
  57.2 6.7 %collective-permute-done.13.refs_5_ = bf16[128,2048]{1,0:T(8,128)(2,1)S(1)} collective-permute-done((bf16[128,2048]{1,0:T(8,128)(2,1)S(1)}, bf16[128,2048]{1,0:T(8,128)(2,1)S(1)}, u32[]{:S(2)}, u32[]{:S(2)}) %collective-permute-start.13) | collective-permute-done | bytes 524320 | tf_op jit(solution)/shard_map/ppermute | solution.py:29
  65.2 5.6 %collective-permute-done.11.refs_0_ = bf16[128,2048]{1,0:T(8,128)(2,1)S(1)} collective-permute-done((bf16[128,2048]{1,0:T(8,128)(2,1)S(1)}, bf16[128,2048]{1,0:T(8,128)(2,1)S(1)}, u32[]{:S(2)}, u32[]{:S(2)}) %collective-permute-start.11) | collective-permute-done | bytes 524320 | tf_op jit(solution)/shard_map/ppermute | solution.py:34
  70.9 8.5 %correlate.2 = (f32[4,512,512]{2,1,0:T(8,128)S(1)}, f32[4,512,512]{2,1,0:T(8,128)}) custom-call(s32[4]{0:T(128)S(1)} %get-tuple-element.79.pass_ref, s32[16]{0:T(128)S(1)} %get-tuple-element.80.count_ref, s32[7]{0:T(128)S(1)} %get-tuple-element.61.number_ref, bf16[128,2048]{1,0:T(8,128)(2,1)S(1)} %choose.2.refs_0_, ...), custom_call_target="tpu_custom_call" | custom-call | flops 6442450944 | bytes 18350080 | tf_op jit(solution)/shard_map/correlate/pallas_call | solution.py:495
  79.4 2.3 %collective-permute-done.14.refs_2_ = bf16[128,2048]{1,0:T(8,128)(2,1)S(1)} collective-permute-done((bf16[128,2048]{1,0:T(8,128)(2,1)S(1)}, bf16[128,2048]{1,0:T(8,128)(2,1)S(1)}, u32[]{:S(2)}, u32[]{:S(2)}) %collective-permute-start.14) | collective-permute-done | bytes 524320 | tf_op jit(solution)/shard_map/ppermute | solution.py:34
  81.6 1.9 %collective-permute-done.17.refs_3_ = bf16[128,2048]{1,0:T(8,128)(2,1)S(1)} collective-permute-done((bf16[128,2048]{1,0:T(8,128)(2,1)S(1)}, bf16[128,2048]{1,0:T(8,128)(2,1)S(1)}, u32[]{:S(2)}, u32[]{:S(2)}) %collective-permute-start.17) | collective-permute-done | bytes 524320 | tf_op jit(solution)/shard_map/ppermute | solution.py:34
  83.6 11.9 %correlate.3 = f32[4,512,512]{2,1,0:T(8,128)} custom-call(s32[4]{0:T(128)S(1)} %get-tuple-element.79.pass_ref, s32[16]{0:T(128)S(1)} %get-tuple-element.80.count_ref, s32[7]{0:T(128)S(1)} %get-tuple-element.61.number_ref, bf16[128,2048]{1,0:T(8,128)(2,1)S(1)} %collective-permute-done.11.refs_0_, bf16[128,2048]{1,0:T(8,128)(2,1)S(1)} %collective-permute-done.12.refs_1_, ...), custom_call_target="tpu_custom_call" | custom-call | flops 6442450944 | bytes 18350080 | tf_op jit(solution)/shard_map/correlate/pallas_call | solution.py:495
  (21 shorter events, 3.3 us)
Async XLA Ops:
  3.0 35.6 %collective-permute-start.7 = (bf16[128,2048]{1,0:T(8,128)(2,1)S(1)}, bf16[128,2048]{1,0:T(8,128)(2,1)S(1)}, u32[]{:S(2)}, u32[]{:S(2)}) collective-permute-start(bf16[128,2048]{1,0:T(8,128)(2,1)S(1)} %own_rows.1.refs_2_), channel_id=1, source_target_pairs={{4,8},{8,4},{5,9},{9,5},{6,10},{10,6},{7,11},{11,7},{20,24},{24,20... | collective-permute-start | bytes 1572872 | tf_op jit(solution)/shard_map/ppermute | solution.py:29
  3.7 34.9 %collective-permute-start.8 = (bf16[128,2048]{1,0:T(8,128)(2,1)S(1)}, bf16[128,2048]{1,0:T(8,128)(2,1)S(1)}, u32[]{:S(2)}, u32[]{:S(2)}) collective-permute-start(bf16[128,2048]{1,0:T(8,128)(2,1)S(1)} %own_rows.1.refs_2_), channel_id=1, source_target_pairs={{0,4},{4,0},{8,12},{12,8},{1,5},{5,1},{9,13},{13,9},{2,6},{6,2},{1... | collective-permute-start | bytes 1572872 | tf_op jit(solution)/shard_map/ppermute | solution.py:29
  9.6 3.9 %collective-permute-start.3 = (bf16[4,2048]{1,0:T(4,128)(2,1)}, bf16[4,2048]{1,0:T(4,128)(2,1)S(1)}, u32[]{:S(2)}, u32[]{:S(2)}) collective-permute-start(bf16[4,2048]{1,0:T(4,128)(2,1)} %receiver_hbm.1), channel_id=1, source_target_pairs={{0,2},{2,0},{4,6},{6,4},{8,10},{10,8},{12,14},{14,12},{1,3},{3,1},... | collective-permute-start | bytes 49160 | tf_op jit(solution)/shard_map/ppermute | solution.py:44
  11.1 12.0 %collective-permute-start = (bf16[4,2304]{1,0:T(4,128)(2,1)S(1)}, bf16[4,2304]{1,0:T(4,128)(2,1)S(1)}, u32[]{:S(2)}, u32[]{:S(2)}) collective-permute-start(bf16[4,2304]{1,0:T(4,128)(2,1)S(1)} %get-tuple-element.63), channel_id=1, source_target_pairs={{0,4},{4,8},{8,12},{12,0},{1,5},{5,9},{9,13},{13,1},{2,6},{6,10},{... | collective-permute-start | bytes 55304 | tf_op jit(solution)/shard_map/ppermute | solution.py:34
  11.2 13.5 %collective-permute-start.1 = (bf16[4,2304]{1,0:T(4,128)(2,1)S(1)}, bf16[4,2304]{1,0:T(4,128)(2,1)S(1)}, u32[]{:S(2)}, u32[]{:S(2)}) collective-permute-start(bf16[4,2304]{1,0:T(4,128)(2,1)S(1)} %get-tuple-element.64), channel_id=1, source_target_pairs={{0,8},{4,12},{8,0},{12,4},{1,9},{5,13},{9,1},{13,5},{2,10},{6,14},... | collective-permute-start | bytes 55304 | tf_op jit(solution)/shard_map/ppermute | solution.py:34
  13.5 12.3 %collective-permute-start.2 = (bf16[4,2304]{1,0:T(4,128)(2,1)S(1)}, bf16[4,2304]{1,0:T(4,128)(2,1)S(1)}, u32[]{:S(2)}, u32[]{:S(2)}) collective-permute-start(bf16[4,2304]{1,0:T(4,128)(2,1)S(1)} %get-tuple-element.65), channel_id=1, source_target_pairs={{0,12},{4,0},{8,4},{12,8},{1,13},{5,1},{9,5},{13,9},{2,14},{6,2},{... | collective-permute-start | bytes 55304 | tf_op jit(solution)/shard_map/ppermute | solution.py:34
  23.1 9.0 %collective-permute-start.4 = (bf16[4,2048]{1,0:T(4,128)(2,1)}, bf16[4,2048]{1,0:T(4,128)(2,1)S(1)}, u32[]{:S(2)}, u32[]{:S(2)}) collective-permute-start(bf16[4,2048]{1,0:T(4,128)(2,1)} %receiver_hbm.1), channel_id=1, source_target_pairs={{0,6},{2,4},{4,10},{6,8},{8,14},{10,12},{12,2},{14,0},{1,7},{3,5},... | collective-permute-start | bytes 49160 | tf_op jit(solution)/shard_map/ppermute | solution.py:44
  24.7 7.4 %collective-permute-start.5 = (bf16[4,2048]{1,0:T(4,128)(2,1)}, bf16[4,2048]{1,0:T(4,128)(2,1)S(1)}, u32[]{:S(2)}, u32[]{:S(2)}) collective-permute-start(bf16[4,2048]{1,0:T(4,128)(2,1)} %receiver_hbm.1), channel_id=1, source_target_pairs={{0,10},{2,8},{4,14},{6,12},{8,2},{10,0},{12,6},{14,4},{1,11},{3,9}... | collective-permute-start | bytes 49160 | tf_op jit(solution)/shard_map/ppermute | solution.py:44
  25.8 6.3 %collective-permute-start.6 = (bf16[4,2048]{1,0:T(4,128)(2,1)}, bf16[4,2048]{1,0:T(4,128)(2,1)S(1)}, u32[]{:S(2)}, u32[]{:S(2)}) collective-permute-start(bf16[4,2048]{1,0:T(4,128)(2,1)} %receiver_hbm.1), channel_id=1, source_target_pairs={{0,14},{2,12},{4,2},{6,0},{8,6},{10,4},{12,10},{14,8},{1,15},{3,13... | collective-permute-start | bytes 49160 | tf_op jit(solution)/shard_map/ppermute | solution.py:44
  38.6 11.6 %collective-permute-start.9 = (bf16[128,2048]{1,0:T(8,128)(2,1)S(1)}, bf16[128,2048]{1,0:T(8,128)(2,1)S(1)}, u32[]{:S(2)}, u32[]{:S(2)}) collective-permute-start(bf16[128,2048]{1,0:T(8,128)(2,1)S(1)} %collective-permute-done.8.refs_3_), channel_id=1, source_target_pairs={{4,8},{8,4},{5,9},{9,5},{6,10},{10,6},{7,11},{11,7},{20,24},{24,20... | collective-permute-start | bytes 1572872 | tf_op jit(solution)/shard_map/ppermute | solution.py:29
  39.5 15.9 %collective-permute-start.10 = (bf16[128,2048]{1,0:T(8,128)(2,1)S(1)}, bf16[128,2048]{1,0:T(8,128)(2,1)S(1)}, u32[]{:S(2)}, u32[]{:S(2)}) collective-permute-start(bf16[128,2048]{1,0:T(8,128)(2,1)S(1)} %collective-permute-done.7.refs_1_), channel_id=1, source_target_pairs={{0,4},{4,0},{8,12},{12,8},{1,5},{5,1},{9,13},{13,9},{2,6},{6,2},{1... | collective-permute-start | bytes 1572872 | tf_op jit(solution)/shard_map/ppermute | solution.py:29
  50.2 13.7 %collective-permute-start.13 = (bf16[128,2048]{1,0:T(8,128)(2,1)S(1)}, bf16[128,2048]{1,0:T(8,128)(2,1)S(1)}, u32[]{:S(2)}, u32[]{:S(2)}) collective-permute-start(bf16[128,2048]{1,0:T(8,128)(2,1)S(1)} %collective-permute-done.9.refs_0_), channel_id=1, source_target_pairs={{0,4},{4,0},{8,12},{12,8},{1,5},{5,1},{9,13},{13,9},{2,6},{6,2},{1... | collective-permute-start | bytes 1572872 | tf_op jit(solution)/shard_map/ppermute | solution.py:29
  56.0 14.9 %collective-permute-start.15 = (bf16[128,2048]{1,0:T(8,128)(2,1)S(1)}, bf16[128,2048]{1,0:T(8,128)(2,1)S(1)}, u32[]{:S(2)}, u32[]{:S(2)}) collective-permute-start(bf16[128,2048]{1,0:T(8,128)(2,1)S(1)} %choose.2.refs_0_), channel_id=1, source_target_pairs={{0,1},{1,0},{2,3},{3,2},{4,5},{5,4},{6,7},{7,6},{8,9},{9,8},{10,11... | collective-permute-start | bytes 1572872 | tf_op jit(solution)/shard_map/ppermute | solution.py:34
  56.1 14.8 %collective-permute-start.11 = (bf16[128,2048]{1,0:T(8,128)(2,1)S(1)}, bf16[128,2048]{1,0:T(8,128)(2,1)S(1)}, u32[]{:S(2)}, u32[]{:S(2)}) collective-permute-start(bf16[128,2048]{1,0:T(8,128)(2,1)S(1)} %choose.2.refs_0_), channel_id=1, source_target_pairs={{0,2},{2,0},{1,3},{3,1},{4,6},{6,4},{5,7},{7,5},{8,10},{10,8},{9,1... | collective-permute-start | bytes 1572872 | tf_op jit(solution)/shard_map/ppermute | solution.py:34
  64.5 6.3 %collective-permute-start.16 = (bf16[128,2048]{1,0:T(8,128)(2,1)S(1)}, bf16[128,2048]{1,0:T(8,128)(2,1)S(1)}, u32[]{:S(2)}, u32[]{:S(2)}) collective-permute-start(bf16[128,2048]{1,0:T(8,128)(2,1)S(1)} %choose.3.refs_2_), channel_id=1, source_target_pairs={{0,1},{1,0},{2,3},{3,2},{4,5},{5,4},{6,7},{7,6},{8,9},{9,8},{10,11... | collective-permute-start | bytes 1572872 | tf_op jit(solution)/shard_map/ppermute | solution.py:34
  64.6 17.0 %collective-permute-start.14 = (bf16[128,2048]{1,0:T(8,128)(2,1)S(1)}, bf16[128,2048]{1,0:T(8,128)(2,1)S(1)}, u32[]{:S(2)}, u32[]{:S(2)}) collective-permute-start(bf16[128,2048]{1,0:T(8,128)(2,1)S(1)} %choose.3.refs_2_), channel_id=1, source_target_pairs={{0,2},{2,0},{1,3},{3,1},{4,6},{6,4},{5,7},{7,5},{8,10},{10,8},{9,1... | collective-permute-start | bytes 1572872 | tf_op jit(solution)/shard_map/ppermute | solution.py:34
  70.9 10.8 %collective-permute-start.12 = (bf16[128,2048]{1,0:T(8,128)(2,1)S(1)}, bf16[128,2048]{1,0:T(8,128)(2,1)S(1)}, u32[]{:S(2)}, u32[]{:S(2)}) collective-permute-start(bf16[128,2048]{1,0:T(8,128)(2,1)S(1)} %collective-permute-done.11.refs_0_), channel_id=1, source_target_pairs={{0,1},{1,0},{2,3},{3,2},{4,5},{5,4},{6,7},{7,6},{8,9},{9,8},{10,11... | collective-permute-start | bytes 1572872 | tf_op jit(solution)/shard_map/ppermute | solution.py:34
  81.6 1.9 %collective-permute-start.17 = (bf16[128,2048]{1,0:T(8,128)(2,1)S(1)}, bf16[128,2048]{1,0:T(8,128)(2,1)S(1)}, u32[]{:S(2)}, u32[]{:S(2)}) collective-permute-start(bf16[128,2048]{1,0:T(8,128)(2,1)S(1)} %collective-permute-done.14.refs_2_), channel_id=1, source_target_pairs={{0,1},{1,0},{2,3},{3,2},{4,5},{5,4},{6,7},{7,6},{8,9},{9,8},{10,11... | collective-permute-start | bytes 1572872 | tf_op jit(solution)/shard_map/ppermute | solution.py:34

commit v2 on v1

--- a/solution.py
+++ b/solution.py
@@ -530,6 +530,7 @@
     heard = [[parcel] for parcel in parcels]
     for k in range(n_chan):
         heard[k] += [turned_both(receivers, k, v) for v in range(1, n_win)]
+    sources, parcels, heard = lax.optimization_barrier((sources, parcels, heard))
     owns = own_rows(numbers, sources[0], n_rep)
 
     arrived = [{0: own} for own in owns]

time: 95.7 us -> 88.9 us (0.929)
  waiting for transfers between devices: 27.9 us -> 22.3 us
  starting transfers between devices: 26.1 us -> 24.8 us
    ppermute x9, waiting for transfers between devices: 18 us -> 9.71 us  [turned(): lax.ppermute(block, axis, [(i, (i + distance) % size) for i in range(size)])]
    ppermute x4, waiting for transfers between devices: 0.55 us -> 3.68 us  [turned_both(): return lax.ppermute(block, ('chan', 'win'), route)]
    ppermute x5, starting transfers between devices: 14.2 us -> 11.4 us  [swapped(): return lax.ppermute(block, axis, route)]
    ppermute x9, starting transfers between devices: 5.15 us -> 6.39 us  [turned(): lax.ppermute(block, axis, [(i, (i + distance) % size) for i in range(size)])]
  transfers between devices with their start and end apart: 18 -> 18, of which waited for: 7 -> 7; matrix products, arithmetic and copies ran while one was open for 0% -> 0% of each run, Pallas kernels for 28% -> 31%
where the time goes in v2:
time: 88.9 us; the launch traced here: 88.5 us
  Pallas kernels  41.3 us (46%)
  starting transfers between devices  24.8 us (28%)
  waiting for transfers between devices  22.3 us (25%)
    pallas_call x2, Pallas kernels, correlate(): pl.pallas_call(body, grid_spec=pltpu.PrefetchScalarGridSpec(num_scalar_pr...  20.4 us
    pallas_call x2, Pallas kernels, build_hankel(): pl.pallas_call(functools.partial(hankel_kernel, v, n_win, samples), in_sp...  12.9 us
    ppermute x5, starting transfers between devices, swapped(): return lax.ppermute(block, axis, route)  11.4 us
    ppermute x9, waiting for transfers between devices, turned(): lax.ppermute(block, axis, [(i, (i + distance) % size) for i in range(size)])  9.71 us
    ppermute x5, waiting for transfers between devices, swapped(): return lax.ppermute(block, axis, route)  8.95 us
    ppermute x4, starting transfers between devices, turned_both(): return lax.ppermute(block, ('chan', 'win'), route)  6.93 us
    ppermute x9, starting transfers between devices, turned(): lax.ppermute(block, axis, [(i, (i + distance) % size) for i in range(size)])  6.39 us
    pallas_call x1, Pallas kernels, index(): pl.pallas_call(functools.partial(index_kernel, r_dev, samples, cap, tile,...  3.77 us
  transfers between devices with their start and end apart: 18, of which 7 were waited for; matrix products, arithmetic and copies ran while one was open for 0% of the time, Pallas kernels for 31%

profile of v2, /device:TPU:0, one launch (start us, length us, event | category | flops | bytes accessed | tf_op | source)
XLA Modules:
  0.0 88.5 jit_solution(904384189015912571)
XLA Ops:
  0.0 2.9 %collective-permute-start.3 = (bf16[4,2048]{1,0:T(4,128)(2,1)}, bf16[4,2048]{1,0:T(4,128)(2,1)S(1)}, u32[]{:S(2)}, u32[]{:S(2)}) collective-permute-start(bf16[4,2048]{1,0:T(4,128)(2,1)} %receiver_hbm.1), channel_id=1, source_target_pairs={{0,2},{2,0},{4,6},{6,4},{8,10},{10,8},{12,14},{14,12},{1,3},{3,1},... | collective-permute-start | bytes 49160 | tf_op jit(solution)/shard_map/ppermute | solution.py:44
  2.9 1.5 %collective-permute-start.4 = (bf16[4,2048]{1,0:T(4,128)(2,1)}, bf16[4,2048]{1,0:T(4,128)(2,1)S(1)}, u32[]{:S(2)}, u32[]{:S(2)}) collective-permute-start(bf16[4,2048]{1,0:T(4,128)(2,1)} %receiver_hbm.1), channel_id=1, source_target_pairs={{0,6},{2,4},{4,10},{6,8},{8,14},{10,12},{12,2},{14,0},{1,7},{3,5},... | collective-permute-start | bytes 49160 | tf_op jit(solution)/shard_map/ppermute | solution.py:44
  4.5 1.4 %pack.1 = (bf16[4,2304]{1,0:T(4,128)(2,1)S(1)}, bf16[4,2304]{1,0:T(4,128)(2,1)S(1)}, bf16[4,2304]{1,0:T(4,128)(2,1)S(1)}, bf16[4,2304]{1,0:T(4,128)(2,1)S(1)}, s32[7]{0:T(128)S(1)}) custom-call(s32[1,2]{1,0:T(1,128)} %plan_hbm.1, bf16[4,2048]{1,0:T(4,128)(2,1)} %receiver_hbm.1, s32[4,512]{1,0:T(4,128)} %bitcast.5, s32[4,512]{1,0:T(4,128)} %bitcast.6), custom_call_target="tpu_custom_call" | custom-call | tf_op jit(solution)/shard_map/pack/pallas_call | solution.py:103
  5.9 1.6 %collective-permute-start = (bf16[4,2304]{1,0:T(4,128)(2,1)S(1)}, bf16[4,2304]{1,0:T(4,128)(2,1)S(1)}, u32[]{:S(2)}, u32[]{:S(2)}) collective-permute-start(bf16[4,2304]{1,0:T(4,128)(2,1)S(1)} %get-tuple-element.76), channel_id=1, source_target_pairs={{0,4},{4,8},{8,12},{12,0},{1,5},{5,9},{9,13},{13,1},{2,6},{6,10},{... | collective-permute-start | bytes 55304 | tf_op jit(solution)/shard_map/ppermute | solution.py:34
  7.5 1.1 %collective-permute-start.1 = (bf16[4,2304]{1,0:T(4,128)(2,1)S(1)}, bf16[4,2304]{1,0:T(4,128)(2,1)S(1)}, u32[]{:S(2)}, u32[]{:S(2)}) collective-permute-start(bf16[4,2304]{1,0:T(4,128)(2,1)S(1)} %get-tuple-element.77), channel_id=1, source_target_pairs={{0,8},{4,12},{8,0},{12,4},{1,9},{5,13},{9,1},{13,5},{2,10},{6,14},... | collective-permute-start | bytes 55304 | tf_op jit(solution)/shard_map/ppermute | solution.py:34
  8.6 2.8 %collective-permute-start.2 = (bf16[4,2304]{1,0:T(4,128)(2,1)S(1)}, bf16[4,2304]{1,0:T(4,128)(2,1)S(1)}, u32[]{:S(2)}, u32[]{:S(2)}) collective-permute-start(bf16[4,2304]{1,0:T(4,128)(2,1)S(1)} %get-tuple-element.78), channel_id=1, source_target_pairs={{0,12},{4,0},{8,4},{12,8},{1,13},{5,1},{9,5},{13,9},{2,14},{6,2},{... | collective-permute-start | bytes 55304 | tf_op jit(solution)/shard_map/ppermute | solution.py:34
  11.5 1.3 %collective-permute-start.5 = (bf16[4,2048]{1,0:T(4,128)(2,1)}, bf16[4,2048]{1,0:T(4,128)(2,1)S(1)}, u32[]{:S(2)}, u32[]{:S(2)}) collective-permute-start(bf16[4,2048]{1,0:T(4,128)(2,1)} %receiver_hbm.1), channel_id=1, source_target_pairs={{0,10},{2,8},{4,14},{6,12},{8,2},{10,0},{12,6},{14,4},{1,11},{3,9}... | collective-permute-start | bytes 49160 | tf_op jit(solution)/shard_map/ppermute | solution.py:44
  12.7 1.2 %collective-permute-start.6 = (bf16[4,2048]{1,0:T(4,128)(2,1)}, bf16[4,2048]{1,0:T(4,128)(2,1)S(1)}, u32[]{:S(2)}, u32[]{:S(2)}) collective-permute-start(bf16[4,2048]{1,0:T(4,128)(2,1)} %receiver_hbm.1), channel_id=1, source_target_pairs={{0,14},{2,12},{4,2},{6,0},{8,6},{10,4},{12,10},{14,8},{1,15},{3,13... | collective-permute-start | bytes 49160 | tf_op jit(solution)/shard_map/ppermute | solution.py:44
  13.9 3.3 %collective-permute-done.5.refs_5_ = bf16[4,2048]{1,0:T(4,128)(2,1)S(1)} collective-permute-done((bf16[4,2048]{1,0:T(4,128)(2,1)}, bf16[4,2048]{1,0:T(4,128)(2,1)S(1)}, u32[]{:S(2)}, u32[]{:S(2)}) %collective-permute-start.5) | collective-permute-done | bytes 16416 | tf_op jit(solution)/shard_map/ppermute | solution.py:44
  17.6 1.6 %own_rows.1.refs_2_ = bf16[128,2048]{1,0:T(8,128)(2,1)S(1)} custom-call(s32[7]{0:T(128)S(1)} %get-tuple-element.74.number_ref, bf16[256,2048]{1,0:T(8,128)(2,1)} %bitcast.4), custom_call_target="tpu_custom_call" | custom-call | tf_op jit(solution)/shard_map/own_rows/pallas_call | solution.py:137
  19.9 4.4 %collective-permute-start.8 = (bf16[128,2048]{1,0:T(8,128)(2,1)S(1)}, bf16[128,2048]{1,0:T(8,128)(2,1)S(1)}, u32[]{:S(2)}, u32[]{:S(2)}) collective-permute-start(bf16[128,2048]{1,0:T(8,128)(2,1)S(1)} %own_rows.1.refs_2_), channel_id=1, source_target_pairs={{0,4},{4,0},{8,12},{12,8},{1,5},{5,1},{9,13},{13,9},{2,6},{6,2},{1... | collective-permute-start | bytes 1572872 | tf_op jit(solution)/shard_map/ppermute | solution.py:29
  24.3 3.8 %index.1 = (bf16[4,640,256]{2,1,0:T(8,128)(2,1)S(1)}, bf16[4,512,512]{2,1,0:T(8,128)(2,1)S(1)}, s32[4]{0:T(128)S(1)}, s32[16]{0:T(128)S(1)}, bf16[4,4,640,256]{3...) custom-call(s32[7]{0:T(128)S(1)} %get-tuple-element.74.number_ref, bf16[4,2304]{1,0:T(4,128)(2,1)S(1)} %get-tuple-element.118.refs_0_, ...), custom_call_target="tpu_custom_call" | custom-call | tf_op jit(solution)/shard_map/index/pallas_call | solution.py:265
  28.1 6.4 %hankel.2.refs_4_ = bf16[16,128,2432]{2,1,0:T(8,128)(2,1)S(1)} custom-call(s32[7]{0:T(128)S(1)} %get-tuple-element.74.number_ref, bf16[4,2304]{1,0:T(4,128)(2,1)S(1)} %get-tuple-element.118.refs_0_, bf16[4,2048]{1,0:T(4,128)(2,1)S(1)} %collective-permute-done.3.refs_1_, bf16[4,2304]{1,0:T(4,128)(2,1)S(1)} %collective-permute-done.refs_1_.refs_2_, ...), custom_call_target="tpu_custom_call" | custom-call | flops 4980736 | bytes 9961472 | tf_op jit(solution)/shard_map/hankel/pallas_call | solution.py:329
  34.6 0.9 collective-permute-start.9
  35.5 2.2 %collective-permute-start.10 = (bf16[128,2048]{1,0:T(8,128)(2,1)S(1)}, bf16[128,2048]{1,0:T(8,128)(2,1)S(1)}, u32[]{:S(2)}, u32[]{:S(2)}) collective-permute-start(bf16[128,2048]{1,0:T(8,128)(2,1)S(1)} %collective-permute-done.7.refs_1_), channel_id=1, source_target_pairs={{0,4},{4,0},{8,12},{12,8},{1,5},{5,1},{9,13},{13,9},{2,6},{6,2},{1... | collective-permute-start | bytes 1572872 | tf_op jit(solution)/shard_map/ppermute | solution.py:29
  37.6 6.4 %hankel.3.refs_4_ = bf16[16,128,2432]{2,1,0:T(8,128)(2,1)S(1)} custom-call(s32[7]{0:T(128)S(1)} %get-tuple-element.74.number_ref, bf16[4,2304]{1,0:T(4,128)(2,1)S(1)} %get-tuple-element.118.refs_0_, bf16[4,2048]{1,0:T(4,128)(2,1)S(1)} %collective-permute-done.3.refs_1_, bf16[4,2304]{1,0:T(4,128)(2,1)S(1)} %collective-permute-done.refs_1_.refs_2_, ...), custom_call_target="tpu_custom_call" | custom-call | flops 4980736 | bytes 9961472 | tf_op jit(solution)/shard_map/hankel/pallas_call | solution.py:329
  44.1 3.3 %collective-permute-start.13 = (bf16[128,2048]{1,0:T(8,128)(2,1)S(1)}, bf16[128,2048]{1,0:T(8,128)(2,1)S(1)}, u32[]{:S(2)}, u32[]{:S(2)}) collective-permute-start(bf16[128,2048]{1,0:T(8,128)(2,1)S(1)} %collective-permute-done.9.refs_0_), channel_id=1, source_target_pairs={{0,4},{4,0},{8,12},{12,8},{1,5},{5,1},{9,13},{13,9},{2,6},{6,2},{1... | collective-permute-start | bytes 1572872 | tf_op jit(solution)/shard_map/ppermute | solution.py:29
  47.3 1.1 %collective-permute-done.10.refs_4_ = bf16[128,2048]{1,0:T(8,128)(2,1)S(1)} collective-permute-done((bf16[128,2048]{1,0:T(8,128)(2,1)S(1)}, bf16[128,2048]{1,0:T(8,128)(2,1)S(1)}, u32[]{:S(2)}, u32[]{:S(2)}) %collective-permute-start.10) | collective-permute-done | bytes 524320 | tf_op jit(solution)/shard_map/ppermute | solution.py:29
  49.5 7.9 %collective-permute-done.13.refs_5_ = bf16[128,2048]{1,0:T(8,128)(2,1)S(1)} collective-permute-done((bf16[128,2048]{1,0:T(8,128)(2,1)S(1)}, bf16[128,2048]{1,0:T(8,128)(2,1)S(1)}, u32[]{:S(2)}, u32[]{:S(2)}) %collective-permute-start.13) | collective-permute-done | bytes 524320 | tf_op jit(solution)/shard_map/ppermute | solution.py:29
  58.4 5.5 %collective-permute-done.11.refs_0_ = bf16[128,2048]{1,0:T(8,128)(2,1)S(1)} collective-permute-done((bf16[128,2048]{1,0:T(8,128)(2,1)S(1)}, bf16[128,2048]{1,0:T(8,128)(2,1)S(1)}, u32[]{:S(2)}, u32[]{:S(2)}) %collective-permute-start.11) | collective-permute-done | bytes 524320 | tf_op jit(solution)/shard_map/ppermute | solution.py:34
  63.9 8.5 %correlate.2 = (f32[4,512,512]{2,1,0:T(8,128)S(1)}, f32[4,512,512]{2,1,0:T(8,128)}) custom-call(s32[4]{0:T(128)S(1)} %get-tuple-element.105.pass_ref, s32[16]{0:T(128)S(1)} %get-tuple-element.106.count_ref, s32[7]{0:T(128)S(1)} %get-tuple-element.74.number_ref, bf16[128,2048]{1,0:T(8,128)(2,1)S(1)} %choose.2.refs_0_, ...), custom_call_target="tpu_custom_call" | custom-call | flops 6442450944 | bytes 18350080 | tf_op jit(solution)/shard_map/correlate/pallas_call | solution.py:495
  72.4 2.3 %collective-permute-done.14.refs_2_ = bf16[128,2048]{1,0:T(8,128)(2,1)S(1)} collective-permute-done((bf16[128,2048]{1,0:T(8,128)(2,1)S(1)}, bf16[128,2048]{1,0:T(8,128)(2,1)S(1)}, u32[]{:S(2)}, u32[]{:S(2)}) %collective-permute-start.14) | collective-permute-done | bytes 524320 | tf_op jit(solution)/shard_map/ppermute | solution.py:34
  74.7 1.9 %collective-permute-done.17.refs_3_ = bf16[128,2048]{1,0:T(8,128)(2,1)S(1)} collective-permute-done((bf16[128,2048]{1,0:T(8,128)(2,1)S(1)}, bf16[128,2048]{1,0:T(8,128)(2,1)S(1)}, u32[]{:S(2)}, u32[]{:S(2)}) %collective-permute-start.17) | collective-permute-done | bytes 524320 | tf_op jit(solution)/shard_map/ppermute | solution.py:34
  76.6 11.9 %correlate.3 = f32[4,512,512]{2,1,0:T(8,128)} custom-call(s32[4]{0:T(128)S(1)} %get-tuple-element.105.pass_ref, s32[16]{0:T(128)S(1)} %get-tuple-element.106.count_ref, s32[7]{0:T(128)S(1)} %get-tuple-element.74.number_ref, bf16[128,2048]{1,0:T(8,128)(2,1)S(1)} %collective-permute-done.11.refs_0_, bf16[128,2048]{1,0:T(8,128)(2,1)S(1)} %collective-permute-done.12.refs_1_, ...), custom_call_target="tpu_custom_call" | custom-call | flops 6442450944 | bytes 18350080 | tf_op jit(solution)/shard_map/correlate/pallas_call | solution.py:495
  (21 shorter events, 3.1 us)
Async XLA Ops:
  0.0 11.5 %collective-permute-start.3 = (bf16[4,2048]{1,0:T(4,128)(2,1)}, bf16[4,2048]{1,0:T(4,128)(2,1)S(1)}, u32[]{:S(2)}, u32[]{:S(2)}) collective-permute-start(bf16[4,2048]{1,0:T(4,128)(2,1)} %receiver_hbm.1), channel_id=1, source_target_pairs={{0,2},{2,0},{4,6},{6,4},{8,10},{10,8},{12,14},{14,12},{1,3},{3,1},... | collective-permute-start | bytes 49160 | tf_op jit(solution)/shard_map/ppermute | solution.py:44
  2.9 9.8 %collective-permute-start.4 = (bf16[4,2048]{1,0:T(4,128)(2,1)}, bf16[4,2048]{1,0:T(4,128)(2,1)S(1)}, u32[]{:S(2)}, u32[]{:S(2)}) collective-permute-start(bf16[4,2048]{1,0:T(4,128)(2,1)} %receiver_hbm.1), channel_id=1, source_target_pairs={{0,6},{2,4},{4,10},{6,8},{8,14},{10,12},{12,2},{14,0},{1,7},{3,5},... | collective-permute-start | bytes 49160 | tf_op jit(solution)/shard_map/ppermute | solution.py:44
  5.9 11.7 %collective-permute-start = (bf16[4,2304]{1,0:T(4,128)(2,1)S(1)}, bf16[4,2304]{1,0:T(4,128)(2,1)S(1)}, u32[]{:S(2)}, u32[]{:S(2)}) collective-permute-start(bf16[4,2304]{1,0:T(4,128)(2,1)S(1)} %get-tuple-element.76), channel_id=1, source_target_pairs={{0,4},{4,8},{8,12},{12,0},{1,5},{5,9},{9,13},{13,1},{2,6},{6,10},{... | collective-permute-start | bytes 55304 | tf_op jit(solution)/shard_map/ppermute | solution.py:34
  7.5 10.1 %collective-permute-start.1 = (bf16[4,2304]{1,0:T(4,128)(2,1)S(1)}, bf16[4,2304]{1,0:T(4,128)(2,1)S(1)}, u32[]{:S(2)}, u32[]{:S(2)}) collective-permute-start(bf16[4,2304]{1,0:T(4,128)(2,1)S(1)} %get-tuple-element.77), channel_id=1, source_target_pairs={{0,8},{4,12},{8,0},{12,4},{1,9},{5,13},{9,1},{13,5},{2,10},{6,14},... | collective-permute-start | bytes 55304 | tf_op jit(solution)/shard_map/ppermute | solution.py:34
  8.6 9.0 %collective-permute-start.2 = (bf16[4,2304]{1,0:T(4,128)(2,1)S(1)}, bf16[4,2304]{1,0:T(4,128)(2,1)S(1)}, u32[]{:S(2)}, u32[]{:S(2)}) collective-permute-start(bf16[4,2304]{1,0:T(4,128)(2,1)S(1)} %get-tuple-element.78), channel_id=1, source_target_pairs={{0,12},{4,0},{8,4},{12,8},{1,13},{5,1},{9,5},{13,9},{2,14},{6,2},{... | collective-permute-start | bytes 55304 | tf_op jit(solution)/shard_map/ppermute | solution.py:34
  11.5 5.7 %collective-permute-start.5 = (bf16[4,2048]{1,0:T(4,128)(2,1)}, bf16[4,2048]{1,0:T(4,128)(2,1)S(1)}, u32[]{:S(2)}, u32[]{:S(2)}) collective-permute-start(bf16[4,2048]{1,0:T(4,128)(2,1)} %receiver_hbm.1), channel_id=1, source_target_pairs={{0,10},{2,8},{4,14},{6,12},{8,2},{10,0},{12,6},{14,4},{1,11},{3,9}... | collective-permute-start | bytes 49160 | tf_op jit(solution)/shard_map/ppermute | solution.py:44
  12.7 4.8 %collective-permute-start.6 = (bf16[4,2048]{1,0:T(4,128)(2,1)}, bf16[4,2048]{1,0:T(4,128)(2,1)S(1)}, u32[]{:S(2)}, u32[]{:S(2)}) collective-permute-start(bf16[4,2048]{1,0:T(4,128)(2,1)} %receiver_hbm.1), channel_id=1, source_target_pairs={{0,14},{2,12},{4,2},{6,0},{8,6},{10,4},{12,10},{14,8},{1,15},{3,13... | collective-permute-start | bytes 49160 | tf_op jit(solution)/shard_map/ppermute | solution.py:44
  19.2 15.4 %collective-permute-start.7 = (bf16[128,2048]{1,0:T(8,128)(2,1)S(1)}, bf16[128,2048]{1,0:T(8,128)(2,1)S(1)}, u32[]{:S(2)}, u32[]{:S(2)}) collective-permute-start(bf16[128,2048]{1,0:T(8,128)(2,1)S(1)} %own_rows.1.refs_2_), channel_id=1, source_target_pairs={{4,8},{8,4},{5,9},{9,5},{6,10},{10,6},{7,11},{11,7},{20,24},{24,20... | collective-permute-start | bytes 1572872 | tf_op jit(solution)/shard_map/ppermute | solution.py:29
  19.9 14.7 %collective-permute-start.8 = (bf16[128,2048]{1,0:T(8,128)(2,1)S(1)}, bf16[128,2048]{1,0:T(8,128)(2,1)S(1)}, u32[]{:S(2)}, u32[]{:S(2)}) collective-permute-start(bf16[128,2048]{1,0:T(8,128)(2,1)S(1)} %own_rows.1.refs_2_), channel_id=1, source_target_pairs={{0,4},{4,0},{8,12},{12,8},{1,5},{5,1},{9,13},{13,9},{2,6},{6,2},{1... | collective-permute-start | bytes 1572872 | tf_op jit(solution)/shard_map/ppermute | solution.py:29
  34.6 9.5 %collective-permute-start.9 = (bf16[128,2048]{1,0:T(8,128)(2,1)S(1)}, bf16[128,2048]{1,0:T(8,128)(2,1)S(1)}, u32[]{:S(2)}, u32[]{:S(2)}) collective-permute-start(bf16[128,2048]{1,0:T(8,128)(2,1)S(1)} %collective-permute-done.8.refs_3_), channel_id=1, source_target_pairs={{4,8},{8,4},{5,9},{9,5},{6,10},{10,6},{7,11},{11,7},{20,24},{24,20... | collective-permute-start | bytes 1572872 | tf_op jit(solution)/shard_map/ppermute | solution.py:29
  35.5 13.0 %collective-permute-start.10 = (bf16[128,2048]{1,0:T(8,128)(2,1)S(1)}, bf16[128,2048]{1,0:T(8,128)(2,1)S(1)}, u32[]{:S(2)}, u32[]{:S(2)}) collective-permute-start(bf16[128,2048]{1,0:T(8,128)(2,1)S(1)} %collective-permute-done.7.refs_1_), channel_id=1, source_target_pairs={{0,4},{4,0},{8,12},{12,8},{1,5},{5,1},{9,13},{13,9},{2,6},{6,2},{1... | collective-permute-start | bytes 1572872 | tf_op jit(solution)/shard_map/ppermute | solution.py:29
  44.1 13.3 %collective-permute-start.13 = (bf16[128,2048]{1,0:T(8,128)(2,1)S(1)}, bf16[128,2048]{1,0:T(8,128)(2,1)S(1)}, u32[]{:S(2)}, u32[]{:S(2)}) collective-permute-start(bf16[128,2048]{1,0:T(8,128)(2,1)S(1)} %collective-permute-done.9.refs_0_), channel_id=1, source_target_pairs={{0,4},{4,0},{8,12},{12,8},{1,5},{5,1},{9,13},{13,9},{2,6},{6,2},{1... | collective-permute-start | bytes 1572872 | tf_op jit(solution)/shard_map/ppermute | solution.py:29
  49.0 14.9 %collective-permute-start.15 = (bf16[128,2048]{1,0:T(8,128)(2,1)S(1)}, bf16[128,2048]{1,0:T(8,128)(2,1)S(1)}, u32[]{:S(2)}, u32[]{:S(2)}) collective-permute-start(bf16[128,2048]{1,0:T(8,128)(2,1)S(1)} %choose.2.refs_0_), channel_id=1, source_target_pairs={{0,1},{1,0},{2,3},{3,2},{4,5},{5,4},{6,7},{7,6},{8,9},{9,8},{10,11... | collective-permute-start | bytes 1572872 | tf_op jit(solution)/shard_map/ppermute | solution.py:34
  49.1 14.8 %collective-permute-start.11 = (bf16[128,2048]{1,0:T(8,128)(2,1)S(1)}, bf16[128,2048]{1,0:T(8,128)(2,1)S(1)}, u32[]{:S(2)}, u32[]{:S(2)}) collective-permute-start(bf16[128,2048]{1,0:T(8,128)(2,1)S(1)} %choose.2.refs_0_), channel_id=1, source_target_pairs={{0,2},{2,0},{1,3},{3,1},{4,6},{6,4},{5,7},{7,5},{8,10},{10,8},{9,1... | collective-permute-start | bytes 1572872 | tf_op jit(solution)/shard_map/ppermute | solution.py:34
  58.0 6.0 %collective-permute-start.16 = (bf16[128,2048]{1,0:T(8,128)(2,1)S(1)}, bf16[128,2048]{1,0:T(8,128)(2,1)S(1)}, u32[]{:S(2)}, u32[]{:S(2)}) collective-permute-start(bf16[128,2048]{1,0:T(8,128)(2,1)S(1)} %choose.3.refs_2_), channel_id=1, source_target_pairs={{0,1},{1,0},{2,3},{3,2},{4,5},{5,4},{6,7},{7,6},{8,9},{9,8},{10,11... | collective-permute-start | bytes 1572872 | tf_op jit(solution)/shard_map/ppermute | solution.py:34
  58.0 16.7 %collective-permute-start.14 = (bf16[128,2048]{1,0:T(8,128)(2,1)S(1)}, bf16[128,2048]{1,0:T(8,128)(2,1)S(1)}, u32[]{:S(2)}, u32[]{:S(2)}) collective-permute-start(bf16[128,2048]{1,0:T(8,128)(2,1)S(1)} %choose.3.refs_2_), channel_id=1, source_target_pairs={{0,2},{2,0},{1,3},{3,1},{4,6},{6,4},{5,7},{7,5},{8,10},{10,8},{9,1... | collective-permute-start | bytes 1572872 | tf_op jit(solution)/shard_map/ppermute | solution.py:34
  63.9 10.8 %collective-permute-start.12 = (bf16[128,2048]{1,0:T(8,128)(2,1)S(1)}, bf16[128,2048]{1,0:T(8,128)(2,1)S(1)}, u32[]{:S(2)}, u32[]{:S(2)}) collective-permute-start(bf16[128,2048]{1,0:T(8,128)(2,1)S(1)} %collective-permute-done.11.refs_0_), channel_id=1, source_target_pairs={{0,1},{1,0},{2,3},{3,2},{4,5},{5,4},{6,7},{7,6},{8,9},{9,8},{10,11... | collective-permute-start | bytes 1572872 | tf_op jit(solution)/shard_map/ppermute | solution.py:34
  74.7 1.9 %collective-permute-start.17 = (bf16[128,2048]{1,0:T(8,128)(2,1)S(1)}, bf16[128,2048]{1,0:T(8,128)(2,1)S(1)}, u32[]{:S(2)}, u32[]{:S(2)}) collective-permute-start(bf16[128,2048]{1,0:T(8,128)(2,1)S(1)} %collective-permute-done.14.refs_2_), channel_id=1, source_target_pairs={{0,1},{1,0},{2,3},{3,2},{4,5},{5,4},{6,7},{7,6},{8,9},{9,8},{10,11... | collective-permute-start | bytes 1572872 | tf_op jit(solution)/shard_map/ppermute | solution.py:34

commit v3 on v1

--- a/solution.py
+++ b/solution.py
@@ -34,16 +34,6 @@
     return lax.ppermute(block, axis, [(i, (i + distance) % size) for i in range(size)])
 
 
-def turned_both(block, chan_distance, win_distance):
-    n_chan, n_win = lax.axis_size("chan"), lax.axis_size("win")
-    route = []
-    for c in range(n_chan):
-        for w in range(n_win):
-            there = (c + chan_distance) % n_chan * n_win + (w + win_distance) % n_win
-            route.append((c * n_win + w, there))
-    return lax.ppermute(block, ("chan", "win"), route)
-
-
 def in_hbm(array):
     return pltpu.with_memory_space_constraint(array, pltpu.HBM)
 
@@ -52,31 +42,31 @@
     return pltpu.CompilerParams(vmem_limit_bytes=vmem)
 
 
-def pack_kernel(halves, lags, block_rows, plan_hbm, receiver_hbm, pair_hbm, keep_hbm, *refs):
-    plan_ref, receiver_ref, pair_ref, keep_ref, digit_ref, sems = refs[-6:]
+def pack_kernel(halves, lags, block_rows, n_win, plan_hbm, pair_hbm, keep_hbm, *refs):
+    span_hbms, refs = refs[:n_win], refs[n_win:]
+    plan_ref, pair_ref, keep_ref, span_refs, digit_ref, sems = refs[-6:]
     parcel_refs, number_ref = refs[:-7], refs[-7]
     small = []
-    for place, (source, target) in enumerate(
-        ((plan_hbm, plan_ref), (receiver_hbm, receiver_ref), (pair_hbm, pair_ref), (keep_hbm, keep_ref))
-    ):
+    moves = [(plan_hbm, plan_ref), (pair_hbm, pair_ref), (keep_hbm, keep_ref)]
+    moves += [(span, span_refs.at[v]) for v, span in enumerate(span_hbms)]
+    for place, (source, target) in enumerate(moves):
         small.append(pltpu.make_async_copy(source, target, sems.at[place]))
         small[-1].start()
-    r_dev, samples = receiver_ref.shape
+    r_dev, samples = span_refs.shape[1:]
     n_chan, cap = pair_ref.shape
-    n_win = lax.axis_size("win")
     chan, win, rep = lax.axis_index("chan"), lax.axis_index("win"), lax.axis_index("rep")
     for copy in small:
         copy.wait()
 
     packed = pair_ref[...] * 2 + keep_ref[...]
     digit_ref[:n_chan, :] = jnp.concatenate([packed // DIGIT, packed % DIGIT], axis=1).astype(F32)
-    heard = receiver_ref[...].astype(F32)
+    heard = [span_refs[v].astype(F32) for v in range(n_win)]
     part = 2 * cap // r_dev
-    spare = parcel_refs[0].shape[1] - samples - part
+    spare = parcel_refs[0].shape[1] - n_win * samples - part
     for distance, parcel_ref in enumerate(parcel_refs):
         digits = digit_ref[pl.ds(lax.rem(chan + distance, n_chan), 1), :]
         lists = [digits[:, i * part : (i + 1) * part] for i in range(r_dev)]
-        parcel = [heard, jnp.concatenate(lists, axis=0)]
+        parcel = heard + [jnp.concatenate(lists, axis=0)]
         if spare:
             parcel.append(jnp.zeros((r_dev, spare), F32))
         parcel_ref[...] = jnp.concatenate(parcel, axis=1).astype(BF16)
@@ -93,56 +83,57 @@
     number_ref[6] = win
 
 
-def pack(plan, receivers, pair_index, keep, halves, lags, block_rows, n_chan):
-    r_dev, samples = receivers.shape
+def pack(plan, spans, pair_index, keep, halves, lags, block_rows, n_chan):
+    n_win = len(spans)
+    r_dev, samples = spans[0].shape
     cap = pair_index.shape[1]
     beside = -(-2 * cap // r_dev // LANES) * LANES
     vmem, smem = pl.BlockSpec(memory_space=pltpu.VMEM), pl.BlockSpec(memory_space=pltpu.SMEM)
-    shapes = [jax.ShapeDtypeStruct((r_dev, samples + beside), BF16)] * n_chan
+    shapes = [jax.ShapeDtypeStruct((r_dev, n_win * samples + beside), BF16)] * n_chan
     shapes.append(jax.ShapeDtypeStruct((7,), jnp.int32))
     *parcels, numbers = pl.pallas_call(
-        functools.partial(pack_kernel, halves, lags, block_rows),
-        in_specs=[pl.BlockSpec(memory_space=pl.ANY)] * 4,
+        functools.partial(pack_kernel, halves, lags, block_rows, n_win),
+        in_specs=[pl.BlockSpec(memory_space=pl.ANY)] * (3 + n_win),
         out_specs=[vmem] * n_chan + [smem],
         out_shape=shapes,
         scratch_shapes=[
             pltpu.SMEM(plan.shape, plan.dtype),
-            pltpu.VMEM(receivers.shape, receivers.dtype),
             pltpu.VMEM(pair_index.shape, pair_index.dtype),
             pltpu.VMEM(keep.shape, keep.dtype),
+            pltpu.VMEM((n_win, r_dev, samples), BF16),
             pltpu.VMEM((-(-n_chan // SHIFT_ROWS) * SHIFT_ROWS, 2 * cap), F32),
-            pltpu.SemaphoreType.DMA((4,)),
+            pltpu.SemaphoreType.DMA((3 + n_win,)),
         ],
         compiler_params=params(VMEM_BYTES // 2),
         name="pack",
-    )(*[in_hbm(a) for a in (plan, receivers, pair_index, keep)])
+    )(*[in_hbm(a) for a in (plan, pair_index, keep, spans[0])], *spans[1:])
     return parcels, numbers
 
 
-def own_kernel(number_ref, source_ref, *refs):
+def own_kernel(source_ref, *refs):
     chain_refs, sems = refs[:-1], refs[-1]
     rows = chain_refs[0].shape[0]
     copies = []
     for chain, chain_ref in enumerate(chain_refs):
-        start = pl.multiple_of(source_ref.shape[0] - number_ref[1] + chain * rows, rows)
+        start = pl.multiple_of((lax.axis_index("rep") * CHAINS + chain) * rows, rows)
         copies.append(pltpu.make_async_copy(source_ref.at[pl.ds(start, rows)], chain_ref, sems.at[chain]))
         copies[-1].start()
     for copy in copies:
         copy.wait()
 
 
-def own_rows(numbers, sources, halves):
+def own_rows(sources, halves):
     block_rows, samples = sources.shape
     shape = jax.ShapeDtypeStruct((block_rows // halves // CHAINS, samples), BF16)
     return pl.pallas_call(
         own_kernel,
-        in_specs=[pl.BlockSpec(memory_space=pltpu.SMEM), pl.BlockSpec(memory_space=pl.ANY)],
+        in_specs=[pl.BlockSpec(memory_space=pl.ANY)],
         out_specs=[pl.BlockSpec(memory_space=pltpu.VMEM)] * CHAINS,
         out_shape=[shape] * CHAINS,
         scratch_shapes=[pltpu.SemaphoreType.DMA((CHAINS,))],
         compiler_params=params(VMEM_BYTES // 4),
         name="own_rows",
-    )(numbers, in_hbm(sources))
+    )(in_hbm(sources))
 
 
 def choose_kernel(which, offsets, number_ref, *refs):
@@ -187,7 +178,7 @@
     return jnp.where(condition, 1.0, 0.0).astype(BF16)
 
 
-def index_kernel(r_dev, samples, cap, tile, block_rows, number_ref, *refs):
+def index_kernel(r_dev, lists_at, cap, tile, block_rows, number_ref, *refs):
     pick_ref, place_ref, pass_ref, count_ref, more_pick_ref, more_place_ref, pick_scratch, place_scratch = refs[-8:]
     parcel_refs = refs[:-8]
     nearer, offset = number_ref[0], number_ref[1]
@@ -198,7 +189,7 @@
     below = ones_where(below)
     later = []
     for group, parcel_ref in enumerate(parcel_refs):
-        digits = parcel_ref[:, samples:].astype(F32)
+        digits = parcel_ref[:, lists_at:].astype(F32)
         digits = jnp.concatenate([digits[i : i + 1, :part] for i in range(r_dev)], axis=1).astype(jnp.int32)
         packed = digits[:, :cap] * DIGIT + digits[:, cap:]
         pairs, kept = packed // 2, packed % 2 == 1
@@ -255,7 +246,7 @@
             lax.fori_loop(1, passes, one_pass, 0)
 
 
-def index(parcels, numbers, samples, r_dev, cap, tile, block_rows):
+def index(parcels, numbers, lists_at, r_dev, cap, tile, block_rows):
     groups = len(parcels)
     slots = 2 * r_dev * tile
     lines = 2 * r_dev * (tile + SPARE)
@@ -263,7 +254,7 @@
     vmem, smem = pl.BlockSpec(memory_space=pltpu.VMEM), pl.BlockSpec(memory_space=pltpu.SMEM)
     any_spec = pl.BlockSpec(memory_space=pl.ANY)
     return pl.pallas_call(
-        functools.partial(index_kernel, r_dev, samples, cap, tile, block_rows),
+        functools.partial(index_kernel, r_dev, lists_at, cap, tile, block_rows),
         in_specs=[smem] + [vmem] * groups,
         out_specs=[vmem, vmem, smem, smem, any_spec, any_spec],
         out_shape=[
@@ -311,24 +302,24 @@
 
 def hankel_kernel(v, n_win, samples, number_ref, *refs):
     out_ref, signal_refs = refs[-2:]
-    heard_refs = refs[:-2]
-    r_dev = heard_refs[0].shape[0]
+    parcel_refs = refs[:-2]
+    r_dev = parcel_refs[0].shape[0]
     begin = first_sample(number_ref, v, n_win, samples)
-    for group in range(len(heard_refs) // n_win):
+    for group, parcel_ref in enumerate(parcel_refs):
         signal_ref = signal_refs.at[group % 2]
-        heard = [ref[:, :samples] for ref in heard_refs[group * n_win : (group + 1) * n_win]]
+        heard = [parcel_ref[:, w * samples : (w + 1) * samples] for w in range(n_win)]
         lay_out(heard, number_ref, signal_ref)
         for r in range(r_dev):
             hankel_rows(signal_ref, r, begin, out_ref.shape[2], out_ref, group * r_dev + r)
 
 
-def build_hankel(heard, numbers, v, samples, width):
-    groups, n_win, r_dev = len(heard), len(heard[0]), heard[0][0].shape[0]
+def build_hankel(parcels, numbers, v, n_win, samples, width):
+    groups, r_dev = len(parcels), parcels[0].shape[0]
     shape = (groups * r_dev, LANES, width)
     vmem = pl.BlockSpec(memory_space=pltpu.VMEM)
     return pl.pallas_call(
         functools.partial(hankel_kernel, v, n_win, samples),
-        in_specs=[pl.BlockSpec(memory_space=pltpu.SMEM)] + [vmem] * (groups * n_win),
+        in_specs=[pl.BlockSpec(memory_space=pltpu.SMEM)] + [vmem] * groups,
         out_specs=vmem,
         scratch_shapes=[pltpu.VMEM((2, SHIFT_ROWS, n_win * samples + LAGS), F32)],
         out_shape=jax.ShapeDtypeStruct(shape, BF16),
@@ -337,7 +328,7 @@
         ),
         compiler_params=params(VMEM_BYTES // 2),
         name="hankel",
-    )(numbers, *[span for spans in heard for span in spans])
+    )(numbers, *parcels)
 
 
 def pick_rows(pieces, pick, gathered, tile):
@@ -402,8 +393,8 @@
     else:
         hankel_place = 0
         hankel_ref, row_ref = refs[6:]
-        n_win = signal_ref.shape[1]
-        lay_out([signal_ref[0, w] for w in range(n_win)], number_ref, row_ref)
+        n_win = signal_ref.shape[2] // samples
+        lay_out([signal_ref[0, :, w * samples : (w + 1) * samples] for w in range(n_win)], number_ref, row_ref)
         begin = first_sample(number_ref, v, n_win, samples)
         for r in range(r_dev):
             hankel_rows(row_ref, r, begin, hankel_ref.shape[2], hankel_ref, r)
@@ -474,7 +465,7 @@
     sums_shape = jax.ShapeDtypeStruct((groups, slots, lag_dev), F32)
     out_shape = jax.ShapeDtypeStruct((groups, cap, lag_dev), F32)
     in_specs = [whole_spec] * len(pieces)
-    in_specs.append(whole_spec if prebuilt else pl.BlockSpec((1,) + signal.shape[1:], lambda i, *_: (i, 0, 0, 0)))
+    in_specs.append(whole_spec if prebuilt else by_group((1,) + signal.shape[1:]))
     in_specs += [by_group((1,) + pick.shape[1:]), by_group((1,) + place.shape[1:]), any_spec, any_spec]
     args = pieces + [signal, pick, place, in_hbm(more_pick), in_hbm(more_place)]
     if before is not None:
@@ -525,12 +516,10 @@
     width = samples - LANES + lag_dev
     prebuilt = n_chan * r_dev * n_win * LANES * width * 2 <= HANKEL_BYTES
 
-    parcels, numbers = pack(plan, receivers, pair_index[0, 0], keep[0, 0], n_rep, lag_dev, block_rows, n_chan)
+    heard = [receivers] + [turned(receivers, "win", v) for v in range(1, n_win)]
+    owns = own_rows(sources[0], n_rep)
+    parcels, numbers = pack(plan, heard, pair_index[0, 0], keep[0, 0], n_rep, lag_dev, block_rows, n_chan)
     parcels = [parcels[0]] + [turned(parcels[k], "chan", k) for k in range(1, n_chan)]
-    heard = [[parcel] for parcel in parcels]
-    for k in range(n_chan):
-        heard[k] += [turned_both(receivers, k, v) for v in range(1, n_win)]
-    owns = own_rows(numbers, sources[0], n_rep)
 
     arrived = [{0: own} for own in owns]
 
@@ -560,30 +549,33 @@
         return [piece] + [turned(piece, "win", v) for v in range(1, n_win)]
 
     relay(1)
-    matrices = index(parcels, numbers, samples, r_dev, cap, tile, block_rows)
+    parcels = after_arrival(1, parcels)
+    relay(2)
+    matrices = index(parcels, numbers, n_win * samples, r_dev, cap, tile, block_rows)
     if prebuilt:
-        signals = [build_hankel(heard, numbers, 0, samples, width)]
-        matrices, signals = before_start(2, (matrices, signals))
+        signals = [build_hankel(parcels, numbers, 0, n_win, samples, width)]
+        matrices, signals = before_start(3, (matrices, signals))
     else:
-        signals = [jnp.stack([jnp.stack([span[:, :samples] for span in spans_of]) for spans_of in heard])] * n_win
-    relay(2)
+        signals = [jnp.stack(parcels)[:, :, : n_win * samples]] * n_win
     reach = range(-(n_chan - 2), n_chan - 1)
     near = choose(numbers, 2, arrived, [offset for offset in reach if offset in arrived[0]])
     if prebuilt:
-        heard = after_arrival(1, heard)
-        signals += [build_hankel(heard, numbers, v, samples, width) for v in range(1, n_win)]
-        signals = before_start(3, signals)
+        parcels = after_arrival(2, parcels)
+        parcels, near = lax.optimization_barrier((parcels, near))
+        signals += [build_hankel(parcels, numbers, v, n_win, samples, width) for v in range(1, n_win)]
     for step in range(3, n_chan):
         relay(step)
-    near_halves = [halves(piece) for piece in spans(near)]
+    near_spans = spans(near)
+    if prebuilt:
+        signals, near_spans = after_arrival(n_chan - 1, (signals, near_spans))
     far_spans = spans(choose(numbers, 3, arrived, sorted(arrived[0])))
 
     result = None
     for v in range(n_win):
         if v:
-            far_spans, result = lax.optimization_barrier((far_spans, result))
+            near_spans, far_spans, result = lax.optimization_barrier((near_spans, far_spans, result))
         result = correlate(
-            near_halves[v] + halves(far_spans[v]), signals[v], prebuilt, numbers, v, matrices, result, v == n_win - 1,
+            halves(near_spans[v]) + halves(far_spans[v]), signals[v], prebuilt, numbers, v, matrices, result, v == n_win - 1,
             tile, norming, lag_dev, n_win, r_dev,
         )
     return result[None, None]

time: 95.7 us -> 81 us (0.85)
  waiting for transfers between devices: 27.9 us -> 18.5 us
  starting transfers between devices: 26.1 us -> 21.2 us
    ppermute x5, waiting for transfers between devices: 9.4 us -> 1.22 us  [swapped(): return lax.ppermute(block, axis, route)]
    ppermute x4 -> x0, starting transfers between devices: 6.74 us -> none  [turned_both(): return lax.ppermute(block, ('chan', 'win'), route)]
    ppermute x9 -> x10, starting transfers between devices: 5.15 us -> 11.6 us  [turned(): lax.ppermute(block, axis, [(i, (i + distance) % size) for i in range(size)])]
    ppermute x5, starting transfers between devices: 14.2 us -> 9.63 us  [swapped(): return lax.ppermute(block, axis, route)]
    ppermute x9 -> x10, waiting for transfers between devices: 18 us -> 17.2 us  [turned(): lax.ppermute(block, axis, [(i, (i + distance) % size) for i in range(size)])]
  transfers between devices with their start and end apart: 18 -> 15, of which waited for: 7 -> 10; matrix products, arithmetic and copies ran while one was open for 0% -> 0% of each run, Pallas kernels for 28% -> 33%
where the time goes in v3:
time: 81 us; the launch traced here: 80.7 us
  Pallas kernels  40.9 us (50%)
  starting transfers between devices  21.2 us (26%)
  waiting for transfers between devices  18.5 us (23%)
    pallas_call x2, Pallas kernels, correlate(): pl.pallas_call(body, grid_spec=pltpu.PrefetchScalarGridSpec(num_scalar_pr...  20.4 us
    ppermute x10, waiting for transfers between devices, turned(): lax.ppermute(block, axis, [(i, (i + distance) % size) for i in range(size)])  17.2 us
    pallas_call x2, Pallas kernels, build_hankel(): pl.pallas_call(functools.partial(hankel_kernel, v, n_win, samples), in_sp...  12.9 us
    ppermute x10, starting transfers between devices, turned(): lax.ppermute(block, axis, [(i, (i + distance) % size) for i in range(size)])  11.6 us
    ppermute x5, starting transfers between devices, swapped(): return lax.ppermute(block, axis, route)  9.63 us
    pallas_call x1, Pallas kernels, index(): pl.pallas_call(functools.partial(index_kernel, r_dev, lists_at, cap, tile...  3.77 us
  transfers between devices with their start and end apart: 15, of which 10 were waited for; matrix products, arithmetic and copies ran while one was open for 0% of the time, Pallas kernels for 33%

profile of v3, /device:TPU:0, one launch (start us, length us, event | category | flops | bytes accessed | tf_op | source)
XLA Modules:
  0.0 80.7 jit_solution(12131998916828652981)
XLA Ops:
  0.0 1.0 %own_rows.1.refs_2_ = bf16[128,2048]{1,0:T(8,128)(2,1)S(1)} custom-call(bf16[256,2048]{1,0:T(8,128)(2,1)} %bitcast.4), custom_call_target="tpu_custom_call" | custom-call | tf_op jit(solution)/shard_map/own_rows/pallas_call | solution.py:128
  1.1 3.1 %collective-permute-start.4 = (bf16[128,2048]{1,0:T(8,128)(2,1)S(1)}, bf16[128,2048]{1,0:T(8,128)(2,1)S(1)}, u32[]{:S(2)}, u32[]{:S(2)}) collective-permute-start(bf16[128,2048]{1,0:T(8,128)(2,1)S(1)} %own_rows.1.refs_2_), channel_id=1, source_target_pairs={{0,4},{4,0},{8,12},{12,8},{1,5},{5,1},{9,13},{13,9},{2,6},{6,2},{1... | collective-permute-start | bytes 1572872 | tf_op jit(solution)/shard_map/ppermute | solution.py:29
  4.8 1.6 %collective-permute-start = (bf16[4,2048]{1,0:T(4,128)(2,1)}, bf16[4,2048]{1,0:T(4,128)(2,1)S(1)}, u32[]{:S(2)}, u32[]{:S(2)}) collective-permute-start(bf16[4,2048]{1,0:T(4,128)(2,1)} %refs_0_.1), channel_id=1, source_target_pairs={{0,2},{2,0},{1,3},{3,1},{4,6},{6,4},{5,7},{7,5},{8,10},{10,8},{9,1... | collective-permute-start | bytes 49160 | tf_op jit(solution)/shard_map/ppermute | solution.py:34
  6.4 2.5 %collective-permute-done.refs_1_ = bf16[4,2048]{1,0:T(4,128)(2,1)S(1)} collective-permute-done((bf16[4,2048]{1,0:T(4,128)(2,1)}, bf16[4,2048]{1,0:T(4,128)(2,1)S(1)}, u32[]{:S(2)}, u32[]{:S(2)}) %collective-permute-start) | collective-permute-done | bytes 16416 | tf_op jit(solution)/shard_map/ppermute | solution.py:34
  8.9 1.4 %pack.1 = (bf16[4,4352]{1,0:T(4,128)(2,1)S(1)}, bf16[4,4352]{1,0:T(4,128)(2,1)S(1)}, bf16[4,4352]{1,0:T(4,128)(2,1)S(1)}, bf16[4,4352]{1,0:T(4,128)(2,1)S(1)}, s32[7]{0:T(128)S(1)}) custom-call(s32[1,2]{1,0:T(1,128)} %plan_hbm.1, s32[4,512]{1,0:T(4,128)} %bitcast.5, s32[4,512]{1,0:T(4,128)} %bitcast.6, bf16[4,2048]{1,0:T(4,128)(2,1)} %refs_0_.1, ...), custom_call_target="tpu_custom_call" | custom-call | tf_op jit(solution)/shard_map/pack/pallas_call | solution.py:94
  10.3 4.4 %collective-permute-start.1 = (bf16[4,4352]{1,0:T(4,128)(2,1)S(1)}, bf16[4,4352]{1,0:T(4,128)(2,1)S(1)}, u32[]{:S(2)}, u32[]{:S(2)}) collective-permute-start(bf16[4,4352]{1,0:T(4,128)(2,1)S(1)} %get-tuple-element.70), channel_id=1, source_target_pairs={{0,4},{4,8},{8,12},{12,0},{1,5},{5,9},{9,13},{13,1},{2,6},{6,10},{... | collective-permute-start | bytes 104456 | tf_op jit(solution)/shard_map/ppermute | solution.py:34
  14.7 2.4 %collective-permute-start.3 = (bf16[4,4352]{1,0:T(4,128)(2,1)S(1)}, bf16[4,4352]{1,0:T(4,128)(2,1)S(1)}, u32[]{:S(2)}, u32[]{:S(2)}) collective-permute-start(bf16[4,4352]{1,0:T(4,128)(2,1)S(1)} %get-tuple-element.72), channel_id=1, source_target_pairs={{0,12},{4,0},{8,4},{12,8},{1,13},{5,1},{9,5},{13,9},{2,14},{6,2},{... | collective-permute-start | bytes 104456 | tf_op jit(solution)/shard_map/ppermute | solution.py:34
  17.1 2.7 %collective-permute-done.1.refs_1_ = bf16[4,4352]{1,0:T(4,128)(2,1)S(1)} collective-permute-done((bf16[4,4352]{1,0:T(4,128)(2,1)S(1)}, bf16[4,4352]{1,0:T(4,128)(2,1)S(1)}, u32[]{:S(2)}, u32[]{:S(2)}) %collective-permute-start.1) | collective-permute-done | bytes 34848 | tf_op jit(solution)/shard_map/ppermute | solution.py:34
  19.9 3.0 %collective-permute-done.2.refs_2_ = bf16[4,4352]{1,0:T(4,128)(2,1)S(1)} collective-permute-done((bf16[4,4352]{1,0:T(4,128)(2,1)S(1)}, bf16[4,4352]{1,0:T(4,128)(2,1)S(1)}, u32[]{:S(2)}, u32[]{:S(2)}) %collective-permute-start.2) | collective-permute-done | bytes 34848 | tf_op jit(solution)/shard_map/ppermute | solution.py:34
  23.6 3.6 %collective-permute-start.7 = (bf16[128,2048]{1,0:T(8,128)(2,1)S(1)}, bf16[128,2048]{1,0:T(8,128)(2,1)S(1)}, u32[]{:S(2)}, u32[]{:S(2)}) collective-permute-start(bf16[128,2048]{1,0:T(8,128)(2,1)S(1)} %collective-permute-done.5.refs_1_), channel_id=1, source_target_pairs={{0,4},{4,0},{8,12},{12,8},{1,5},{5,1},{9,13},{13,9},{2,6},{6,2},{1... | collective-permute-start | bytes 1572872 | tf_op jit(solution)/shard_map/ppermute | solution.py:29
  27.2 3.8 %index.1 = (bf16[4,640,256]{2,1,0:T(8,128)(2,1)S(1)}, bf16[4,512,512]{2,1,0:T(8,128)(2,1)S(1)}, s32[4]{0:T(128)S(1)}, s32[16]{0:T(128)S(1)}, bf16[4,4,640,256]{3...) custom-call(s32[7]{0:T(128)S(1)} %get-tuple-element.68.number_ref, bf16[4,4352]{1,0:T(4,128)(2,1)S(1)} %get-tuple-element.109.refs_0_, ...), custom_call_target="tpu_custom_call" | custom-call | tf_op jit(solution)/shard_map/index/pallas_call | solution.py:256
  31.0 6.4 %hankel.2.refs_4_ = bf16[16,128,2432]{2,1,0:T(8,128)(2,1)S(1)} custom-call(s32[7]{0:T(128)S(1)} %get-tuple-element.68.number_ref, bf16[4,4352]{1,0:T(4,128)(2,1)S(1)} %get-tuple-element.109.refs_0_, bf16[4,4352]{1,0:T(4,128)(2,1)S(1)} %collective-permute-done.1.refs_1_, bf16[4,4352]{1,0:T(4,128)(2,1)S(1)} %collective-permute-done.2.refs_2_, ...), custom_call_target="tpu_custom_call" | custom-call | flops 4980736 | bytes 9961472 | tf_op jit(solution)/shard_map/hankel/pallas_call | solution.py:320
  37.4 0.8 choose.2.refs_0_
  38.2 1.6 %collective-permute-start.8 = (bf16[128,2048]{1,0:T(8,128)(2,1)S(1)}, bf16[128,2048]{1,0:T(8,128)(2,1)S(1)}, u32[]{:S(2)}, u32[]{:S(2)}) collective-permute-start(bf16[128,2048]{1,0:T(8,128)(2,1)S(1)} %choose.2.refs_0_), channel_id=1, source_target_pairs={{0,2},{2,0},{1,3},{3,1},{4,6},{6,4},{5,7},{7,5},{8,10},{10,8},{9,1... | collective-permute-start | bytes 1572872 | tf_op jit(solution)/shard_map/ppermute | solution.py:34
  39.8 1.6 %collective-permute-start.9 = (bf16[128,2048]{1,0:T(8,128)(2,1)S(1)}, bf16[128,2048]{1,0:T(8,128)(2,1)S(1)}, u32[]{:S(2)}, u32[]{:S(2)}) collective-permute-start(bf16[128,2048]{1,0:T(8,128)(2,1)S(1)} %collective-permute-done.6.refs_0_), channel_id=1, source_target_pairs={{0,4},{4,0},{8,12},{12,8},{1,5},{5,1},{9,13},{13,9},{2,6},{6,2},{1... | collective-permute-start | bytes 1572872 | tf_op jit(solution)/shard_map/ppermute | solution.py:29
  41.4 6.4 %hankel.3.refs_4_ = bf16[16,128,2432]{2,1,0:T(8,128)(2,1)S(1)} custom-call(s32[7]{0:T(128)S(1)} %get-tuple-element.68.number_ref, bf16[4,4352]{1,0:T(4,128)(2,1)S(1)} %get-tuple-element.109.refs_0_, bf16[4,4352]{1,0:T(4,128)(2,1)S(1)} %collective-permute-done.1.refs_1_, bf16[4,4352]{1,0:T(4,128)(2,1)S(1)} %collective-permute-done.2.refs_2_, ...), custom_call_target="tpu_custom_call" | custom-call | flops 4980736 | bytes 9961472 | tf_op jit(solution)/shard_map/hankel/pallas_call | solution.py:320
  47.8 2.0 %collective-permute-done.8.refs_0_ = bf16[128,2048]{1,0:T(8,128)(2,1)S(1)} collective-permute-done((bf16[128,2048]{1,0:T(8,128)(2,1)S(1)}, bf16[128,2048]{1,0:T(8,128)(2,1)S(1)}, u32[]{:S(2)}, u32[]{:S(2)}) %collective-permute-start.8) | collective-permute-done | bytes 524320 | tf_op jit(solution)/shard_map/ppermute | solution.py:34
  49.8 1.2 %collective-permute-done.9.refs_5_ = bf16[128,2048]{1,0:T(8,128)(2,1)S(1)} collective-permute-done((bf16[128,2048]{1,0:T(8,128)(2,1)S(1)}, bf16[128,2048]{1,0:T(8,128)(2,1)S(1)}, u32[]{:S(2)}, u32[]{:S(2)}) %collective-permute-start.9) | collective-permute-done | bytes 524320 | tf_op jit(solution)/shard_map/ppermute | solution.py:29
  52.8 0.9 %collective-permute-done.12.refs_3_ = bf16[128,2048]{1,0:T(8,128)(2,1)S(1)} collective-permute-done((bf16[128,2048]{1,0:T(8,128)(2,1)S(1)}, bf16[128,2048]{1,0:T(8,128)(2,1)S(1)}, u32[]{:S(2)}, u32[]{:S(2)}) %collective-permute-start.12) | collective-permute-done | bytes 524320 | tf_op jit(solution)/shard_map/ppermute | solution.py:34
  53.6 0.7 collective-permute-done.11.refs_1_
  54.4 8.5 %correlate.2 = (f32[4,512,512]{2,1,0:T(8,128)S(1)}, f32[4,512,512]{2,1,0:T(8,128)}) custom-call(s32[4]{0:T(128)S(1)} %get-tuple-element.96.pass_ref, s32[16]{0:T(128)S(1)} %get-tuple-element.97.count_ref, s32[7]{0:T(128)S(1)} %get-tuple-element.68.number_ref, bf16[128,2048]{1,0:T(8,128)(2,1)S(1)} %choose.2.refs_0_, ...), custom_call_target="tpu_custom_call" | custom-call | flops 6442450944 | bytes 18350080 | tf_op jit(solution)/shard_map/correlate/pallas_call | solution.py:486
  62.9 3.3 %collective-permute-done.10.refs_2_ = bf16[128,2048]{1,0:T(8,128)(2,1)S(1)} collective-permute-done((bf16[128,2048]{1,0:T(8,128)(2,1)S(1)}, bf16[128,2048]{1,0:T(8,128)(2,1)S(1)}, u32[]{:S(2)}, u32[]{:S(2)}) %collective-permute-start.10) | collective-permute-done | bytes 524320 | tf_op jit(solution)/shard_map/ppermute | solution.py:34
  66.7 1.4 %collective-permute-done.13.refs_1_ = bf16[128,2048]{1,0:T(8,128)(2,1)S(1)} collective-permute-done((bf16[128,2048]{1,0:T(8,128)(2,1)S(1)}, bf16[128,2048]{1,0:T(8,128)(2,1)S(1)}, u32[]{:S(2)}, u32[]{:S(2)}) %collective-permute-start.13) | collective-permute-done | bytes 524320 | tf_op jit(solution)/shard_map/ppermute | solution.py:34
  68.8 11.9 %correlate.3 = f32[4,512,512]{2,1,0:T(8,128)} custom-call(s32[4]{0:T(128)S(1)} %get-tuple-element.96.pass_ref, s32[16]{0:T(128)S(1)} %get-tuple-element.97.count_ref, s32[7]{0:T(128)S(1)} %get-tuple-element.68.number_ref, bf16[128,2048]{1,0:T(8,128)(2,1)S(1)} %collective-permute-done.8.refs_0_, bf16[128,2048]{1,0:T(8,128)(2,1)S(1)} %collective-permute-done.13.refs_1_, ...), custom_call_target="tpu_custom_call" | custom-call | flops 6442450944 | bytes 18350080 | tf_op jit(solution)/shard_map/correlate/pallas_call | solution.py:486
  (15 shorter events, 4.4 us)
Async XLA Ops:
  1.1 21.8 %collective-permute-start.4 = (bf16[128,2048]{1,0:T(8,128)(2,1)S(1)}, bf16[128,2048]{1,0:T(8,128)(2,1)S(1)}, u32[]{:S(2)}, u32[]{:S(2)}) collective-permute-start(bf16[128,2048]{1,0:T(8,128)(2,1)S(1)} %own_rows.1.refs_2_), channel_id=1, source_target_pairs={{0,4},{4,0},{8,12},{12,8},{1,5},{5,1},{9,13},{13,9},{2,6},{6,2},{1... | collective-permute-start | bytes 1572872 | tf_op jit(solution)/shard_map/ppermute | solution.py:29
  4.1 19.4 %collective-permute-start.5 = (bf16[128,2048]{1,0:T(8,128)(2,1)S(1)}, bf16[128,2048]{1,0:T(8,128)(2,1)S(1)}, u32[]{:S(2)}, u32[]{:S(2)}) collective-permute-start(bf16[128,2048]{1,0:T(8,128)(2,1)S(1)} %own_rows.1.refs_2_), channel_id=1, source_target_pairs={{4,8},{8,4},{5,9},{9,5},{6,10},{10,6},{7,11},{11,7},{20,24},{24,20... | collective-permute-start | bytes 1572872 | tf_op jit(solution)/shard_map/ppermute | solution.py:29
  4.8 4.0 %collective-permute-start = (bf16[4,2048]{1,0:T(4,128)(2,1)}, bf16[4,2048]{1,0:T(4,128)(2,1)S(1)}, u32[]{:S(2)}, u32[]{:S(2)}) collective-permute-start(bf16[4,2048]{1,0:T(4,128)(2,1)} %refs_0_.1), channel_id=1, source_target_pairs={{0,2},{2,0},{1,3},{3,1},{4,6},{6,4},{5,7},{7,5},{8,10},{10,8},{9,1... | collective-permute-start | bytes 49160 | tf_op jit(solution)/shard_map/ppermute | solution.py:34
  10.3 9.6 %collective-permute-start.1 = (bf16[4,4352]{1,0:T(4,128)(2,1)S(1)}, bf16[4,4352]{1,0:T(4,128)(2,1)S(1)}, u32[]{:S(2)}, u32[]{:S(2)}) collective-permute-start(bf16[4,4352]{1,0:T(4,128)(2,1)S(1)} %get-tuple-element.70), channel_id=1, source_target_pairs={{0,4},{4,8},{8,12},{12,0},{1,5},{5,9},{9,13},{13,1},{2,6},{6,10},{... | collective-permute-start | bytes 104456 | tf_op jit(solution)/shard_map/ppermute | solution.py:34
  14.7 8.2 %collective-permute-start.2 = (bf16[4,4352]{1,0:T(4,128)(2,1)S(1)}, bf16[4,4352]{1,0:T(4,128)(2,1)S(1)}, u32[]{:S(2)}, u32[]{:S(2)}) collective-permute-start(bf16[4,4352]{1,0:T(4,128)(2,1)S(1)} %get-tuple-element.71), channel_id=1, source_target_pairs={{0,8},{4,12},{8,0},{12,4},{1,9},{5,13},{9,1},{13,5},{2,10},{6,14},... | collective-permute-start | bytes 104456 | tf_op jit(solution)/shard_map/ppermute | solution.py:34
  14.7 8.2 %collective-permute-start.3 = (bf16[4,4352]{1,0:T(4,128)(2,1)S(1)}, bf16[4,4352]{1,0:T(4,128)(2,1)S(1)}, u32[]{:S(2)}, u32[]{:S(2)}) collective-permute-start(bf16[4,4352]{1,0:T(4,128)(2,1)S(1)} %get-tuple-element.72), channel_id=1, source_target_pairs={{0,12},{4,0},{8,4},{12,8},{1,13},{5,1},{9,5},{13,9},{2,14},{6,2},{... | collective-permute-start | bytes 104456 | tf_op jit(solution)/shard_map/ppermute | solution.py:34
  22.9 14.5 %collective-permute-start.6 = (bf16[128,2048]{1,0:T(8,128)(2,1)S(1)}, bf16[128,2048]{1,0:T(8,128)(2,1)S(1)}, u32[]{:S(2)}, u32[]{:S(2)}) collective-permute-start(bf16[128,2048]{1,0:T(8,128)(2,1)S(1)} %collective-permute-done.4.refs_3_), channel_id=1, source_target_pairs={{4,8},{8,4},{5,9},{9,5},{6,10},{10,6},{7,11},{11,7},{20,24},{24,20... | collective-permute-start | bytes 1572872 | tf_op jit(solution)/shard_map/ppermute | solution.py:29
  23.6 13.8 %collective-permute-start.7 = (bf16[128,2048]{1,0:T(8,128)(2,1)S(1)}, bf16[128,2048]{1,0:T(8,128)(2,1)S(1)}, u32[]{:S(2)}, u32[]{:S(2)}) collective-permute-start(bf16[128,2048]{1,0:T(8,128)(2,1)S(1)} %collective-permute-done.5.refs_1_), channel_id=1, source_target_pairs={{0,4},{4,0},{8,12},{12,8},{1,5},{5,1},{9,13},{13,9},{2,6},{6,2},{1... | collective-permute-start | bytes 1572872 | tf_op jit(solution)/shard_map/ppermute | solution.py:29
  38.2 11.6 %collective-permute-start.8 = (bf16[128,2048]{1,0:T(8,128)(2,1)S(1)}, bf16[128,2048]{1,0:T(8,128)(2,1)S(1)}, u32[]{:S(2)}, u32[]{:S(2)}) collective-permute-start(bf16[128,2048]{1,0:T(8,128)(2,1)S(1)} %choose.2.refs_0_), channel_id=1, source_target_pairs={{0,2},{2,0},{1,3},{3,1},{4,6},{6,4},{5,7},{7,5},{8,10},{10,8},{9,1... | collective-permute-start | bytes 1572872 | tf_op jit(solution)/shard_map/ppermute | solution.py:34
  39.8 11.3 %collective-permute-start.9 = (bf16[128,2048]{1,0:T(8,128)(2,1)S(1)}, bf16[128,2048]{1,0:T(8,128)(2,1)S(1)}, u32[]{:S(2)}, u32[]{:S(2)}) collective-permute-start(bf16[128,2048]{1,0:T(8,128)(2,1)S(1)} %collective-permute-done.6.refs_0_), channel_id=1, source_target_pairs={{0,4},{4,0},{8,12},{12,8},{1,5},{5,1},{9,13},{13,9},{2,6},{6,2},{1... | collective-permute-start | bytes 1572872 | tf_op jit(solution)/shard_map/ppermute | solution.py:29
  51.7 2.0 %collective-permute-start.12 = (bf16[128,2048]{1,0:T(8,128)(2,1)S(1)}, bf16[128,2048]{1,0:T(8,128)(2,1)S(1)}, u32[]{:S(2)}, u32[]{:S(2)}) collective-permute-start(bf16[128,2048]{1,0:T(8,128)(2,1)S(1)} %choose.3.refs_2_), channel_id=1, source_target_pairs={{0,1},{1,0},{2,3},{3,2},{4,5},{5,4},{6,7},{7,6},{8,9},{9,8},{10,11... | collective-permute-start | bytes 1572872 | tf_op jit(solution)/shard_map/ppermute | solution.py:34
  51.7 2.6 %collective-permute-start.11 = (bf16[128,2048]{1,0:T(8,128)(2,1)S(1)}, bf16[128,2048]{1,0:T(8,128)(2,1)S(1)}, u32[]{:S(2)}, u32[]{:S(2)}) collective-permute-start(bf16[128,2048]{1,0:T(8,128)(2,1)S(1)} %choose.2.refs_0_), channel_id=1, source_target_pairs={{0,1},{1,0},{2,3},{3,2},{4,5},{5,4},{6,7},{7,6},{8,9},{9,8},{10,11... | collective-permute-start | bytes 1572872 | tf_op jit(solution)/shard_map/ppermute | solution.py:34
  52.2 13.9 %collective-permute-start.10 = (bf16[128,2048]{1,0:T(8,128)(2,1)S(1)}, bf16[128,2048]{1,0:T(8,128)(2,1)S(1)}, u32[]{:S(2)}, u32[]{:S(2)}) collective-permute-start(bf16[128,2048]{1,0:T(8,128)(2,1)S(1)} %choose.3.refs_2_), channel_id=1, source_target_pairs={{0,2},{2,0},{1,3},{3,1},{4,6},{6,4},{5,7},{7,5},{8,10},{10,8},{9,1... | collective-permute-start | bytes 1572872 | tf_op jit(solution)/shard_map/ppermute | solution.py:34
  66.2 1.9 %collective-permute-start.13 = (bf16[128,2048]{1,0:T(8,128)(2,1)S(1)}, bf16[128,2048]{1,0:T(8,128)(2,1)S(1)}, u32[]{:S(2)}, u32[]{:S(2)}) collective-permute-start(bf16[128,2048]{1,0:T(8,128)(2,1)S(1)} %collective-permute-done.8.refs_0_), channel_id=1, source_target_pairs={{0,1},{1,0},{2,3},{3,2},{4,5},{5,4},{6,7},{7,6},{8,9},{9,8},{10,11... | collective-permute-start | bytes 1572872 | tf_op jit(solution)/shard_map/ppermute | solution.py:34
  66.2 2.7 %collective-permute-start.14 = (bf16[128,2048]{1,0:T(8,128)(2,1)S(1)}, bf16[128,2048]{1,0:T(8,128)(2,1)S(1)}, u32[]{:S(2)}, u32[]{:S(2)}) collective-permute-start(bf16[128,2048]{1,0:T(8,128)(2,1)S(1)} %collective-permute-done.10.refs_2_), channel_id=1, source_target_pairs={{0,1},{1,0},{2,3},{3,2},{4,5},{5,4},{6,7},{7,6},{8,9},{9,8},{10,11... | collective-permute-start | bytes 1572872 | tf_op jit(solution)/shard_map/ppermute | solution.py:34

commit v4 on v3

--- a/solution.py
+++ b/solution.py
@@ -178,9 +178,15 @@
     return jnp.where(condition, 1.0, 0.0).astype(BF16)
 
 
-def index_kernel(r_dev, lists_at, cap, tile, block_rows, number_ref, *refs):
+def index_kernel(r_dev, lists_at, cap, tile, block_rows, done, number_ref, *refs):
     pick_ref, place_ref, pass_ref, count_ref, more_pick_ref, more_place_ref, pick_scratch, place_scratch = refs[-8:]
     parcel_refs = refs[:-8]
+    if done:
+        parcel_refs, (_, _, earlier_pass_ref, earlier_count_ref, _, _) = parcel_refs[:-6], parcel_refs[-6:]
+        for group in range(done):
+            pass_ref[group] = earlier_pass_ref[group]
+            for r in range(r_dev):
+                count_ref[group * r_dev + r] = earlier_count_ref[group * r_dev + r]
     nearer, offset = number_ref[0], number_ref[1]
     slots = 2 * r_dev * tile
     window = tile + SPARE
@@ -188,7 +194,7 @@
     below = lax.broadcasted_iota(jnp.int32, (cap, cap), 0) < lax.broadcasted_iota(jnp.int32, (cap, cap), 1)
     below = ones_where(below)
     later = []
-    for group, parcel_ref in enumerate(parcel_refs):
+    for group, parcel_ref in enumerate(parcel_refs, done):
         digits = parcel_ref[:, lists_at:].astype(F32)
         digits = jnp.concatenate([digits[i : i + 1, :part] for i in range(r_dev)], axis=1).astype(jnp.int32)
         packed = digits[:, :cap] * DIGIT + digits[:, cap:]
@@ -246,17 +252,23 @@
             lax.fori_loop(1, passes, one_pass, 0)
 
 
-def index(parcels, numbers, lists_at, r_dev, cap, tile, block_rows):
-    groups = len(parcels)
+def index(parcels, numbers, earlier, groups, lists_at, r_dev, cap, tile, block_rows):
     slots = 2 * r_dev * tile
     lines = 2 * r_dev * (tile + SPARE)
     more = -(-(min(block_rows, cap) - (tile - SPARE)) // tile)
     vmem, smem = pl.BlockSpec(memory_space=pltpu.VMEM), pl.BlockSpec(memory_space=pltpu.SMEM)
     any_spec = pl.BlockSpec(memory_space=pl.ANY)
+    specs = [vmem, vmem, smem, smem, any_spec, any_spec]
+    args = list(parcels)
+    done, aliases = 0, {}
+    if earlier is not None:
+        done = groups - len(parcels)
+        aliases = {1 + len(parcels) + place: place for place in (0, 1, 4, 5)}
+        args += list(earlier[:4]) + [in_hbm(array) for array in earlier[4:]]
     return pl.pallas_call(
-        functools.partial(index_kernel, r_dev, lists_at, cap, tile, block_rows),
-        in_specs=[smem] + [vmem] * groups,
-        out_specs=[vmem, vmem, smem, smem, any_spec, any_spec],
+        functools.partial(index_kernel, r_dev, lists_at, cap, tile, block_rows, done),
+        in_specs=[smem] + [vmem] * len(parcels) + (specs if done else []),
+        out_specs=specs,
         out_shape=[
             jax.ShapeDtypeStruct((groups, lines, block_rows), BF16),
             jax.ShapeDtypeStruct((groups, cap, slots), BF16),
@@ -266,9 +278,10 @@
             pltpu.HBM((groups, more, cap, slots), BF16),
         ],
         scratch_shapes=[pltpu.VMEM((lines, block_rows), BF16), pltpu.VMEM((cap, slots), BF16)],
+        input_output_aliases=aliases,
         compiler_params=params(VMEM_BYTES),
         name="index",
-    )(numbers, *parcels)
+    )(numbers, *args)
 
 
 def lay_out(heard, number_ref, signal_ref):
@@ -300,12 +313,12 @@
         out_ref[place, first : first + 2 * SHIFT_ROWS, :] = jnp.concatenate(both, axis=0).astype(BF16)
 
 
-def hankel_kernel(v, n_win, samples, number_ref, *refs):
+def hankel_kernel(v, n_win, samples, done, number_ref, *refs):
     out_ref, signal_refs = refs[-2:]
-    parcel_refs = refs[:-2]
+    parcel_refs = refs[: -3 if done else -2]
     r_dev = parcel_refs[0].shape[0]
     begin = first_sample(number_ref, v, n_win, samples)
-    for group, parcel_ref in enumerate(parcel_refs):
+    for group, parcel_ref in enumerate(parcel_refs, done):
         signal_ref = signal_refs.at[group % 2]
         heard = [parcel_ref[:, w * samples : (w + 1) * samples] for w in range(n_win)]
         lay_out(heard, number_ref, signal_ref)
@@ -313,22 +326,23 @@
             hankel_rows(signal_ref, r, begin, out_ref.shape[2], out_ref, group * r_dev + r)
 
 
-def build_hankel(parcels, numbers, v, n_win, samples, width):
-    groups, r_dev = len(parcels), parcels[0].shape[0]
+def build_hankel(parcels, numbers, earlier, groups, v, n_win, samples, width):
+    r_dev = parcels[0].shape[0]
     shape = (groups * r_dev, LANES, width)
     vmem = pl.BlockSpec(memory_space=pltpu.VMEM)
+    done = 0 if earlier is None else groups - len(parcels)
+    copies = len(parcels) * r_dev * LANES * width
     return pl.pallas_call(
-        functools.partial(hankel_kernel, v, n_win, samples),
-        in_specs=[pl.BlockSpec(memory_space=pltpu.SMEM)] + [vmem] * groups,
+        functools.partial(hankel_kernel, v, n_win, samples, done),
+        in_specs=[pl.BlockSpec(memory_space=pltpu.SMEM)] + [vmem] * (len(parcels) + (1 if done else 0)),
         out_specs=vmem,
         scratch_shapes=[pltpu.VMEM((2, SHIFT_ROWS, n_win * samples + LAGS), F32)],
         out_shape=jax.ShapeDtypeStruct(shape, BF16),
-        cost_estimate=pl.CostEstimate(
-            flops=math.prod(shape), bytes_accessed=2 * math.prod(shape), transcendentals=0
-        ),
+        input_output_aliases={1 + len(parcels): 0} if done else {},
+        cost_estimate=pl.CostEstimate(flops=copies, bytes_accessed=2 * copies, transcendentals=0),
         compiler_params=params(VMEM_BYTES // 2),
         name="hankel",
-    )(numbers, *parcels)
+    )(numbers, *parcels, *([earlier] if done else []))
 
 
 def pick_rows(pieces, pick, gathered, tile):
@@ -519,7 +533,11 @@
     heard = [receivers] + [turned(receivers, "win", v) for v in range(1, n_win)]
     owns = own_rows(sources[0], n_rep)
     parcels, numbers = pack(plan, heard, pair_index[0, 0], keep[0, 0], n_rep, lag_dev, block_rows, n_chan)
-    parcels = [parcels[0]] + [turned(parcels[k], "chan", k) for k in range(1, n_chan)]
+    own_parcel = parcels[0]
+    parcels = [turned(parcels[k], "chan", k) for k in range(1, n_chan)]
+    matrices = index([own_parcel], numbers, None, n_chan, n_win * samples, r_dev, cap, tile, block_rows)
+    if prebuilt:
+        signals = [build_hankel([own_parcel], numbers, None, n_chan, v, n_win, samples, width) for v in range(n_win)]
 
     arrived = [{0: own} for own in owns]
 
@@ -533,14 +551,13 @@
         for there in arrived:
             for key in (step, -step):
                 if key in there:
-                    value, there[key] = lax.optimization_barrier((value, there[key]))
+                    value = lax.optimization_barrier((value, there[key]))[0]
         return value
 
     def before_start(step, value):
         for there in arrived:
             for key in (1 - step, step - 1):
-                value, there[key] = lax.optimization_barrier((value, there[key]))
-        return value
+                there[key] = lax.optimization_barrier((value, there[key]))[1]
 
     def halves(piece):
         return [piece] + [turned(piece, "rep", -u) for u in range(1, n_rep)]
@@ -549,20 +566,22 @@
         return [piece] + [turned(piece, "win", v) for v in range(1, n_win)]
 
     relay(1)
+    before_start(2, (matrices, parcels, signals) if prebuilt else (matrices, parcels))
     parcels = after_arrival(1, parcels)
     relay(2)
-    matrices = index(parcels, numbers, n_win * samples, r_dev, cap, tile, block_rows)
+    matrices = index(parcels, numbers, matrices, n_chan, n_win * samples, r_dev, cap, tile, block_rows)
     if prebuilt:
-        signals = [build_hankel(parcels, numbers, 0, n_win, samples, width)]
-        matrices, signals = before_start(3, (matrices, signals))
+        signals[0] = build_hankel(parcels, numbers, signals[0], n_chan, 0, n_win, samples, width)
+        before_start(3, (matrices, signals[0]))
     else:
-        signals = [jnp.stack(parcels)[:, :, : n_win * samples]] * n_win
+        signals = [jnp.stack([own_parcel] + parcels)[:, :, : n_win * samples]] * n_win
     reach = range(-(n_chan - 2), n_chan - 1)
     near = choose(numbers, 2, arrived, [offset for offset in reach if offset in arrived[0]])
     if prebuilt:
         parcels = after_arrival(2, parcels)
         parcels, near = lax.optimization_barrier((parcels, near))
-        signals += [build_hankel(parcels, numbers, v, n_win, samples, width) for v in range(1, n_win)]
+        for v in range(1, n_win):
+            signals[v] = build_hankel(parcels, numbers, signals[v], n_chan, v, n_win, samples, width)
     for step in range(3, n_chan):
         relay(step)
     near_spans = spans(near)

time: 81 us -> 80.9 us (level)
  waiting for transfers between devices: 18.5 us -> 13.7 us
  Pallas kernels: 40.9 us -> 43.3 us
  starting transfers between devices: 21.2 us -> 23.5 us
    ppermute x10, waiting for transfers between devices: 17.2 us -> 10.9 us  [turned(): lax.ppermute(block, axis, [(i, (i + distance) % size) for i in range(size)])]
    ppermute x5, waiting for transfers between devices: 1.22 us -> 2.84 us  [swapped(): return lax.ppermute(block, axis, route)]
    pallas_call x1 -> x2, Pallas kernels: 3.77 us -> 5.29 us  [index(): pl.pallas_call(functools.partial(index_kernel, r_dev, lists_at, cap, tile...]
    ppermute x5, starting transfers between devices: 9.63 us -> 10.9 us  [swapped(): return lax.ppermute(block, axis, route)]
    ppermute x10, starting transfers between devices: 11.6 us -> 12.5 us  [turned(): lax.ppermute(block, axis, [(i, (i + distance) % size) for i in range(size)])]
    pallas_call x2 -> x4, Pallas kernels: 12.9 us -> 13.7 us  [build_hankel(): pl.pallas_call(functools.partial(hankel_kernel, v, n_win, samples, done),...]
  transfers between devices with their start and end apart: 15 -> 15, of which waited for: 10 -> 6; matrix products, arithmetic and copies ran while one was open for 0% -> 0% of each run, Pallas kernels for 33% -> 38%
where the time goes in v4:
time: 80.9 us; the launch traced here: 80.6 us
  Pallas kernels  43.3 us (54%)
  starting transfers between devices  23.5 us (29%)
  waiting for transfers between devices  13.7 us (17%)
    pallas_call x2, Pallas kernels, correlate(): pl.pallas_call(body, grid_spec=pltpu.PrefetchScalarGridSpec(num_scalar_pr...  20.4 us
    pallas_call x4, Pallas kernels, build_hankel(): pl.pallas_call(functools.partial(hankel_kernel, v, n_win, samples, done),...  13.7 us
    ppermute x10, starting transfers between devices, turned(): lax.ppermute(block, axis, [(i, (i + distance) % size) for i in range(size)])  12.5 us
    ppermute x5, starting transfers between devices, swapped(): return lax.ppermute(block, axis, route)  10.9 us
    ppermute x10, waiting for transfers between devices, turned(): lax.ppermute(block, axis, [(i, (i + distance) % size) for i in range(size)])  10.9 us
    pallas_call x2, Pallas kernels, index(): pl.pallas_call(functools.partial(index_kernel, r_dev, lists_at, cap, tile...  5.29 us
    ppermute x5, waiting for transfers between devices, swapped(): return lax.ppermute(block, axis, route)  2.84 us
  transfers between devices with their start and end apart: 15, of which 6 were waited for; matrix products, arithmetic and copies ran while one was open for 0% of the time, Pallas kernels for 38%

profile of v4, /device:TPU:0, one launch (start us, length us, event | category | flops | bytes accessed | tf_op | source)
XLA Modules:
  0.0 80.6 jit_solution(10381074082795052660)
XLA Ops:
  0.0 1.0 %own_rows.1.refs_2_ = bf16[128,2048]{1,0:T(8,128)(2,1)S(1)} custom-call(bf16[256,2048]{1,0:T(8,128)(2,1)} %bitcast.4), custom_call_target="tpu_custom_call" | custom-call | tf_op jit(solution)/shard_map/own_rows/pallas_call | solution.py:128
  1.1 3.1 %collective-permute-start.4 = (bf16[128,2048]{1,0:T(8,128)(2,1)S(1)}, bf16[128,2048]{1,0:T(8,128)(2,1)S(1)}, u32[]{:S(2)}, u32[]{:S(2)}) collective-permute-start(bf16[128,2048]{1,0:T(8,128)(2,1)S(1)} %own_rows.1.refs_2_), channel_id=1, source_target_pairs={{0,4},{4,0},{8,12},{12,8},{1,5},{5,1},{9,13},{13,9},{2,6},{6,2},{1... | collective-permute-start | bytes 1572872 | tf_op jit(solution)/shard_map/ppermute | solution.py:29
  4.8 1.6 %collective-permute-start = (bf16[4,2048]{1,0:T(4,128)(2,1)}, bf16[4,2048]{1,0:T(4,128)(2,1)S(1)}, u32[]{:S(2)}, u32[]{:S(2)}) collective-permute-start(bf16[4,2048]{1,0:T(4,128)(2,1)} %refs_0_.1), channel_id=1, source_target_pairs={{0,2},{2,0},{1,3},{3,1},{4,6},{6,4},{5,7},{7,5},{8,10},{10,8},{9,1... | collective-permute-start | bytes 49160 | tf_op jit(solution)/shard_map/ppermute | solution.py:34
  6.4 2.5 %collective-permute-done.refs_1_ = bf16[4,2048]{1,0:T(4,128)(2,1)S(1)} collective-permute-done((bf16[4,2048]{1,0:T(4,128)(2,1)}, bf16[4,2048]{1,0:T(4,128)(2,1)S(1)}, u32[]{:S(2)}, u32[]{:S(2)}) %collective-permute-start) | collective-permute-done | bytes 16416 | tf_op jit(solution)/shard_map/ppermute | solution.py:34
  8.9 1.4 %pack.1 = (bf16[4,4352]{1,0:T(4,128)(2,1)S(1)}, bf16[4,4352]{1,0:T(4,128)(2,1)S(1)}, bf16[4,4352]{1,0:T(4,128)(2,1)S(1)}, bf16[4,4352]{1,0:T(4,128)(2,1)S(1)}, s32[7]{0:T(128)S(1)}) custom-call(s32[1,2]{1,0:T(1,128)} %plan_hbm.1, s32[4,512]{1,0:T(4,128)} %bitcast.5, s32[4,512]{1,0:T(4,128)} %bitcast.6, bf16[4,2048]{1,0:T(4,128)(2,1)} %refs_0_.1, ...), custom_call_target="tpu_custom_call" | custom-call | tf_op jit(solution)/shard_map/pack/pallas_call | solution.py:94
  10.3 4.4 %collective-permute-start.1 = (bf16[4,4352]{1,0:T(4,128)(2,1)S(1)}, bf16[4,4352]{1,0:T(4,128)(2,1)S(1)}, u32[]{:S(2)}, u32[]{:S(2)}) collective-permute-start(bf16[4,4352]{1,0:T(4,128)(2,1)S(1)} %get-tuple-element.53), channel_id=1, source_target_pairs={{0,4},{4,8},{8,12},{12,0},{1,5},{5,9},{9,13},{13,1},{2,6},{6,10},{... | collective-permute-start | bytes 104456 | tf_op jit(solution)/shard_map/ppermute | solution.py:34
  14.7 2.4 %collective-permute-start.3 = (bf16[4,4352]{1,0:T(4,128)(2,1)S(1)}, bf16[4,4352]{1,0:T(4,128)(2,1)S(1)}, u32[]{:S(2)}, u32[]{:S(2)}) collective-permute-start(bf16[4,4352]{1,0:T(4,128)(2,1)S(1)} %get-tuple-element.55), channel_id=1, source_target_pairs={{0,12},{4,0},{8,4},{12,8},{1,13},{5,1},{9,5},{13,9},{2,14},{6,2},{... | collective-permute-start | bytes 104456 | tf_op jit(solution)/shard_map/ppermute | solution.py:34
  17.1 2.0 %index.2 = (bf16[4,640,256]{2,1,0:T(8,128)(2,1)S(1)}, bf16[4,512,512]{2,1,0:T(8,128)(2,1)S(1)}, s32[4]{0:T(128)S(1)}, s32[16]{0:T(128)S(1)}, bf16[4,4,640,256]{3...) custom-call(s32[7]{0:T(128)S(1)} %get-tuple-element.52.number_ref, bf16[4,4352]{1,0:T(4,128)(2,1)S(1)} %get-tuple-element.56.refs_0_), custom_call_target="tpu_custom_call" | custom-call | tf_op jit(solution)/shard_map/index/pallas_call | solution.py:268
  19.2 1.9 %hankel.5.refs_3_ = bf16[16,128,2432]{2,1,0:T(8,128)(2,1)S(1)} custom-call(s32[7]{0:T(128)S(1)} %get-tuple-element.52.number_ref, bf16[4,4352]{1,0:T(4,128)(2,1)S(1)} %get-tuple-element.56.refs_0_), custom_call_target="tpu_custom_call" | custom-call | flops 1245184 | bytes 2490368 | tf_op jit(solution)/shard_map/hankel/pallas_call | solution.py:335
  21.1 1.9 %hankel.4.refs_3_ = bf16[16,128,2432]{2,1,0:T(8,128)(2,1)S(1)} custom-call(s32[7]{0:T(128)S(1)} %get-tuple-element.52.number_ref, bf16[4,4352]{1,0:T(4,128)(2,1)S(1)} %get-tuple-element.56.refs_0_), custom_call_target="tpu_custom_call" | custom-call | flops 1245184 | bytes 2490368 | tf_op jit(solution)/shard_map/hankel/pallas_call | solution.py:335
  23.8 3.3 %collective-permute-start.6 = (bf16[128,2048]{1,0:T(8,128)(2,1)S(1)}, bf16[128,2048]{1,0:T(8,128)(2,1)S(1)}, u32[]{:S(2)}, u32[]{:S(2)}) collective-permute-start(bf16[128,2048]{1,0:T(8,128)(2,1)S(1)} %collective-permute-done.5.refs_1_), channel_id=1, source_target_pairs={{0,4},{4,0},{8,12},{12,8},{1,5},{5,1},{9,13},{13,9},{2,6},{6,2},{1... | collective-permute-start | bytes 1572872 | tf_op jit(solution)/shard_map/ppermute | solution.py:29
  27.2 3.2 %index.3 = (bf16[4,640,256]{2,1,0:T(8,128)(2,1)S(1)}, bf16[4,512,512]{2,1,0:T(8,128)(2,1)S(1)}, s32[4]{0:T(128)S(1)}, s32[16]{0:T(128)S(1)}, bf16[4,4,640,256]{3...) custom-call(s32[7]{0:T(128)S(1)} %get-tuple-element.52.number_ref, ...), custom_call_target="tpu_custom_call", output_to_operand_aliasing={{0}: (4, {}), {1}: (5, {}), {4}: (8, {}), {5}: (9, {})} | custom-call | tf_op jit(solution)/shard_map/index/pallas_call | solution.py:268
  30.4 4.9 %hankel.6.refs_4_ = bf16[16,128,2432]{2,1,0:T(8,128)(2,1)S(1)} custom-call(s32[7]{0:T(128)S(1)} %get-tuple-element.52.number_ref, bf16[4,4352]{1,0:T(4,128)(2,1)S(1)} %collective-permute-done.1.refs_0_, bf16[4,4352]{1,0:T(4,128)(2,1)S(1)} %collective-permute-done.2.refs_1_, ...), custom_call_target="tpu_custom_call", output_to_operand_aliasing={{}: (4, {})} | custom-call | flops 3735552 | bytes 7471104 | tf_op jit(solution)/shard_map/hankel/pallas_call | solution.py:335
  35.4 3.1 %collective-permute-start.9 = (bf16[128,2048]{1,0:T(8,128)(2,1)S(1)}, bf16[128,2048]{1,0:T(8,128)(2,1)S(1)}, u32[]{:S(2)}, u32[]{:S(2)}) collective-permute-start(bf16[128,2048]{1,0:T(8,128)(2,1)S(1)} %collective-permute-done.7.refs_0_), channel_id=1, source_target_pairs={{0,4},{4,0},{8,12},{12,8},{1,5},{5,1},{9,13},{13,9},{2,6},{6,2},{1... | collective-permute-start | bytes 1572872 | tf_op jit(solution)/shard_map/ppermute | solution.py:29
  38.5 0.8 choose.2.refs_0_
  39.3 1.6 %collective-permute-start.8 = (bf16[128,2048]{1,0:T(8,128)(2,1)S(1)}, bf16[128,2048]{1,0:T(8,128)(2,1)S(1)}, u32[]{:S(2)}, u32[]{:S(2)}) collective-permute-start(bf16[128,2048]{1,0:T(8,128)(2,1)S(1)} %choose.2.refs_0_), channel_id=1, source_target_pairs={{0,2},{2,0},{1,3},{3,1},{4,6},{6,4},{5,7},{7,5},{8,10},{10,8},{9,1... | collective-permute-start | bytes 1572872 | tf_op jit(solution)/shard_map/ppermute | solution.py:34
  40.9 4.9 %hankel.7.refs_4_ = bf16[16,128,2432]{2,1,0:T(8,128)(2,1)S(1)} custom-call(s32[7]{0:T(128)S(1)} %get-tuple-element.52.number_ref, bf16[4,4352]{1,0:T(4,128)(2,1)S(1)} %collective-permute-done.1.refs_0_, bf16[4,4352]{1,0:T(4,128)(2,1)S(1)} %collective-permute-done.2.refs_1_, ...), custom_call_target="tpu_custom_call", output_to_operand_aliasing={{}: (4, {})} | custom-call | flops 3735552 | bytes 7471104 | tf_op jit(solution)/shard_map/hankel/pallas_call | solution.py:335
  45.8 2.8 %collective-permute-done.9.refs_5_ = bf16[128,2048]{1,0:T(8,128)(2,1)S(1)} collective-permute-done((bf16[128,2048]{1,0:T(8,128)(2,1)S(1)}, bf16[128,2048]{1,0:T(8,128)(2,1)S(1)}, u32[]{:S(2)}, u32[]{:S(2)}) %collective-permute-start.9) | collective-permute-done | bytes 524320 | tf_op jit(solution)/shard_map/ppermute | solution.py:29
  48.6 2.3 %collective-permute-done.8.refs_0_ = bf16[128,2048]{1,0:T(8,128)(2,1)S(1)} collective-permute-done((bf16[128,2048]{1,0:T(8,128)(2,1)S(1)}, bf16[128,2048]{1,0:T(8,128)(2,1)S(1)}, u32[]{:S(2)}, u32[]{:S(2)}) %collective-permute-start.8) | collective-permute-done | bytes 524320 | tf_op jit(solution)/shard_map/ppermute | solution.py:34
  52.2 1.5 %collective-permute-start.10 = (bf16[128,2048]{1,0:T(8,128)(2,1)S(1)}, bf16[128,2048]{1,0:T(8,128)(2,1)S(1)}, u32[]{:S(2)}, u32[]{:S(2)}) collective-permute-start(bf16[128,2048]{1,0:T(8,128)(2,1)S(1)} %choose.3.refs_2_), channel_id=1, source_target_pairs={{0,2},{2,0},{1,3},{3,1},{4,6},{6,4},{5,7},{7,5},{8,10},{10,8},{9,1... | collective-permute-start | bytes 1572872 | tf_op jit(solution)/shard_map/ppermute | solution.py:34
  53.7 8.5 %correlate.2 = (f32[4,512,512]{2,1,0:T(8,128)S(1)}, f32[4,512,512]{2,1,0:T(8,128)}) custom-call(s32[4]{0:T(128)S(1)} %get-tuple-element.71.pass_ref, s32[16]{0:T(128)S(1)} %get-tuple-element.72.count_ref, s32[7]{0:T(128)S(1)} %get-tuple-element.52.number_ref, bf16[128,2048]{1,0:T(8,128)(2,1)S(1)} %choose.2.refs_0_, ...), custom_call_target="tpu_custom_call" | custom-call | flops 6442450944 | bytes 18350080 | tf_op jit(solution)/shard_map/correlate/pallas_call | solution.py:500
  62.2 3.9 %collective-permute-done.10.refs_2_ = bf16[128,2048]{1,0:T(8,128)(2,1)S(1)} collective-permute-done((bf16[128,2048]{1,0:T(8,128)(2,1)S(1)}, bf16[128,2048]{1,0:T(8,128)(2,1)S(1)}, u32[]{:S(2)}, u32[]{:S(2)}) %collective-permute-start.10) | collective-permute-done | bytes 524320 | tf_op jit(solution)/shard_map/ppermute | solution.py:34
  66.6 1.4 %collective-permute-done.13.refs_1_ = bf16[128,2048]{1,0:T(8,128)(2,1)S(1)} collective-permute-done((bf16[128,2048]{1,0:T(8,128)(2,1)S(1)}, bf16[128,2048]{1,0:T(8,128)(2,1)S(1)}, u32[]{:S(2)}, u32[]{:S(2)}) %collective-permute-start.13) | collective-permute-done | bytes 524320 | tf_op jit(solution)/shard_map/ppermute | solution.py:34
  68.7 11.9 %correlate.3 = f32[4,512,512]{2,1,0:T(8,128)} custom-call(s32[4]{0:T(128)S(1)} %get-tuple-element.71.pass_ref, s32[16]{0:T(128)S(1)} %get-tuple-element.72.count_ref, s32[7]{0:T(128)S(1)} %get-tuple-element.52.number_ref, bf16[128,2048]{1,0:T(8,128)(2,1)S(1)} %collective-permute-done.8.refs_0_, bf16[128,2048]{1,0:T(8,128)(2,1)S(1)} %collective-permute-done.13.refs_1_, ...), custom_call_target="tpu_custom_call" | custom-call | flops 6442450944 | bytes 18350080 | tf_op jit(solution)/shard_map/correlate/pallas_call | solution.py:500
  (18 shorter events, 3.9 us)
Async XLA Ops:
  1.1 22.1 %collective-permute-start.4 = (bf16[128,2048]{1,0:T(8,128)(2,1)S(1)}, bf16[128,2048]{1,0:T(8,128)(2,1)S(1)}, u32[]{:S(2)}, u32[]{:S(2)}) collective-permute-start(bf16[128,2048]{1,0:T(8,128)(2,1)S(1)} %own_rows.1.refs_2_), channel_id=1, source_target_pairs={{0,4},{4,0},{8,12},{12,8},{1,5},{5,1},{9,13},{13,9},{2,6},{6,2},{1... | collective-permute-start | bytes 1572872 | tf_op jit(solution)/shard_map/ppermute | solution.py:29
  4.1 19.7 %collective-permute-start.5 = (bf16[128,2048]{1,0:T(8,128)(2,1)S(1)}, bf16[128,2048]{1,0:T(8,128)(2,1)S(1)}, u32[]{:S(2)}, u32[]{:S(2)}) collective-permute-start(bf16[128,2048]{1,0:T(8,128)(2,1)S(1)} %own_rows.1.refs_2_), channel_id=1, source_target_pairs={{4,8},{8,4},{5,9},{9,5},{6,10},{10,6},{7,11},{11,7},{20,24},{24,20... | collective-permute-start | bytes 1572872 | tf_op jit(solution)/shard_map/ppermute | solution.py:29
  4.8 4.0 %collective-permute-start = (bf16[4,2048]{1,0:T(4,128)(2,1)}, bf16[4,2048]{1,0:T(4,128)(2,1)S(1)}, u32[]{:S(2)}, u32[]{:S(2)}) collective-permute-start(bf16[4,2048]{1,0:T(4,128)(2,1)} %refs_0_.1), channel_id=1, source_target_pairs={{0,2},{2,0},{1,3},{3,1},{4,6},{6,4},{5,7},{7,5},{8,10},{10,8},{9,1... | collective-permute-start | bytes 49160 | tf_op jit(solution)/shard_map/ppermute | solution.py:34
  10.3 12.8 %collective-permute-start.1 = (bf16[4,4352]{1,0:T(4,128)(2,1)S(1)}, bf16[4,4352]{1,0:T(4,128)(2,1)S(1)}, u32[]{:S(2)}, u32[]{:S(2)}) collective-permute-start(bf16[4,4352]{1,0:T(4,128)(2,1)S(1)} %get-tuple-element.53), channel_id=1, source_target_pairs={{0,4},{4,8},{8,12},{12,0},{1,5},{5,9},{9,13},{13,1},{2,6},{6,10},{... | collective-permute-start | bytes 104456 | tf_op jit(solution)/shard_map/ppermute | solution.py:34
  14.7 8.4 %collective-permute-start.2 = (bf16[4,4352]{1,0:T(4,128)(2,1)S(1)}, bf16[4,4352]{1,0:T(4,128)(2,1)S(1)}, u32[]{:S(2)}, u32[]{:S(2)}) collective-permute-start(bf16[4,4352]{1,0:T(4,128)(2,1)S(1)} %get-tuple-element.54), channel_id=1, source_target_pairs={{0,8},{4,12},{8,0},{12,4},{1,9},{5,13},{9,1},{13,5},{2,10},{6,14},... | collective-permute-start | bytes 104456 | tf_op jit(solution)/shard_map/ppermute | solution.py:34
  14.7 8.4 %collective-permute-start.3 = (bf16[4,4352]{1,0:T(4,128)(2,1)S(1)}, bf16[4,4352]{1,0:T(4,128)(2,1)S(1)}, u32[]{:S(2)}, u32[]{:S(2)}) collective-permute-start(bf16[4,4352]{1,0:T(4,128)(2,1)S(1)} %get-tuple-element.55), channel_id=1, source_target_pairs={{0,12},{4,0},{8,4},{12,8},{1,13},{5,1},{9,5},{13,9},{2,14},{6,2},{... | collective-permute-start | bytes 104456 | tf_op jit(solution)/shard_map/ppermute | solution.py:34
  23.1 12.3 %collective-permute-start.7 = (bf16[128,2048]{1,0:T(8,128)(2,1)S(1)}, bf16[128,2048]{1,0:T(8,128)(2,1)S(1)}, u32[]{:S(2)}, u32[]{:S(2)}) collective-permute-start(bf16[128,2048]{1,0:T(8,128)(2,1)S(1)} %collective-permute-done.4.refs_3_), channel_id=1, source_target_pairs={{4,8},{8,4},{5,9},{9,5},{6,10},{10,6},{7,11},{11,7},{20,24},{24,20... | collective-permute-start | bytes 1572872 | tf_op jit(solution)/shard_map/ppermute | solution.py:29
  23.8 14.7 %collective-permute-start.6 = (bf16[128,2048]{1,0:T(8,128)(2,1)S(1)}, bf16[128,2048]{1,0:T(8,128)(2,1)S(1)}, u32[]{:S(2)}, u32[]{:S(2)}) collective-permute-start(bf16[128,2048]{1,0:T(8,128)(2,1)S(1)} %collective-permute-done.5.refs_1_), channel_id=1, source_target_pairs={{0,4},{4,0},{8,12},{12,8},{1,5},{5,1},{9,13},{13,9},{2,6},{6,2},{1... | collective-permute-start | bytes 1572872 | tf_op jit(solution)/shard_map/ppermute | solution.py:29
  35.4 13.2 %collective-permute-start.9 = (bf16[128,2048]{1,0:T(8,128)(2,1)S(1)}, bf16[128,2048]{1,0:T(8,128)(2,1)S(1)}, u32[]{:S(2)}, u32[]{:S(2)}) collective-permute-start(bf16[128,2048]{1,0:T(8,128)(2,1)S(1)} %collective-permute-done.7.refs_0_), channel_id=1, source_target_pairs={{0,4},{4,0},{8,12},{12,8},{1,5},{5,1},{9,13},{13,9},{2,6},{6,2},{1... | collective-permute-start | bytes 1572872 | tf_op jit(solution)/shard_map/ppermute | solution.py:29
  39.3 11.7 %collective-permute-start.8 = (bf16[128,2048]{1,0:T(8,128)(2,1)S(1)}, bf16[128,2048]{1,0:T(8,128)(2,1)S(1)}, u32[]{:S(2)}, u32[]{:S(2)}) collective-permute-start(bf16[128,2048]{1,0:T(8,128)(2,1)S(1)} %choose.2.refs_0_), channel_id=1, source_target_pairs={{0,2},{2,0},{1,3},{3,1},{4,6},{6,4},{5,7},{7,5},{8,10},{10,8},{9,1... | collective-permute-start | bytes 1572872 | tf_op jit(solution)/shard_map/ppermute | solution.py:34
  51.0 2.7 %collective-permute-start.11 = (bf16[128,2048]{1,0:T(8,128)(2,1)S(1)}, bf16[128,2048]{1,0:T(8,128)(2,1)S(1)}, u32[]{:S(2)}, u32[]{:S(2)}) collective-permute-start(bf16[128,2048]{1,0:T(8,128)(2,1)S(1)} %choose.2.refs_0_), channel_id=1, source_target_pairs={{0,1},{1,0},{2,3},{3,2},{4,5},{5,4},{6,7},{7,6},{8,9},{9,8},{10,11... | collective-permute-start | bytes 1572872 | tf_op jit(solution)/shard_map/ppermute | solution.py:34
  51.6 2.1 %collective-permute-start.12 = (bf16[128,2048]{1,0:T(8,128)(2,1)S(1)}, bf16[128,2048]{1,0:T(8,128)(2,1)S(1)}, u32[]{:S(2)}, u32[]{:S(2)}) collective-permute-start(bf16[128,2048]{1,0:T(8,128)(2,1)S(1)} %choose.3.refs_2_), channel_id=1, source_target_pairs={{0,1},{1,0},{2,3},{3,2},{4,5},{5,4},{6,7},{7,6},{8,9},{9,8},{10,11... | collective-permute-start | bytes 1572872 | tf_op jit(solution)/shard_map/ppermute | solution.py:34
  52.2 13.9 %collective-permute-start.10 = (bf16[128,2048]{1,0:T(8,128)(2,1)S(1)}, bf16[128,2048]{1,0:T(8,128)(2,1)S(1)}, u32[]{:S(2)}, u32[]{:S(2)}) collective-permute-start(bf16[128,2048]{1,0:T(8,128)(2,1)S(1)} %choose.3.refs_2_), channel_id=1, source_target_pairs={{0,2},{2,0},{1,3},{3,1},{4,6},{6,4},{5,7},{7,5},{8,10},{10,8},{9,1... | collective-permute-start | bytes 1572872 | tf_op jit(solution)/shard_map/ppermute | solution.py:34
  66.1 1.9 %collective-permute-start.13 = (bf16[128,2048]{1,0:T(8,128)(2,1)S(1)}, bf16[128,2048]{1,0:T(8,128)(2,1)S(1)}, u32[]{:S(2)}, u32[]{:S(2)}) collective-permute-start(bf16[128,2048]{1,0:T(8,128)(2,1)S(1)} %collective-permute-done.8.refs_0_), channel_id=1, source_target_pairs={{0,1},{1,0},{2,3},{3,2},{4,5},{5,4},{6,7},{7,6},{8,9},{9,8},{10,11... | collective-permute-start | bytes 1572872 | tf_op jit(solution)/shard_map/ppermute | solution.py:34
  66.1 2.7 %collective-permute-start.14 = (bf16[128,2048]{1,0:T(8,128)(2,1)S(1)}, bf16[128,2048]{1,0:T(8,128)(2,1)S(1)}, u32[]{:S(2)}, u32[]{:S(2)}) collective-permute-start(bf16[128,2048]{1,0:T(8,128)(2,1)S(1)} %collective-permute-done.10.refs_2_), channel_id=1, source_target_pairs={{0,1},{1,0},{2,3},{3,2},{4,5},{5,4},{6,7},{7,6},{8,9},{9,8},{10,11... | collective-permute-start | bytes 1572872 | tf_op jit(solution)/shard_map/ppermute | solution.py:34

commit v5 on v4

--- a/solution.py
+++ b/solution.py
@@ -345,17 +345,27 @@
     )(numbers, *parcels, *([earlier] if done else []))
 
 
-def pick_rows(pieces, pick, gathered, tile):
-    parts = len(pieces) // 2
+def window_of(blocks, tile):
+    if len(blocks) == 2:
+        return 0, 2 * tile
+    return (tile - SPARE if blocks[0] else 0), tile + SPARE
+
+
+def pick_rows(blocks, pieces, pick, gathered, tile):
+    parts = len(pieces) // len(blocks)
     window = tile + SPARE
     shared = tile - SPARE
-    r_dev, samples = gathered.shape[0] // (2 * tile), gathered.shape[1]
+    rows_of_channel = window_of(blocks, tile)[1]
+    r_dev, samples = gathered.shape[0] // rows_of_channel, gathered.shape[1]
     for t in range(0, samples, STEP):
         chosen = []
-        for q in range(2):
-            block = jnp.concatenate([piece[:, t : t + STEP] for piece in pieces[q * parts : (q + 1) * parts]], axis=0)
+        for place, q in enumerate(blocks):
+            block = [piece[:, t : t + STEP] for piece in pieces[place * parts : (place + 1) * parts]]
             ones = pick[q * r_dev * window : (q + 1) * r_dev * window, :]
-            chosen.append(jnp.dot(ones, block, preferred_element_type=F32))
+            chosen.append(jnp.dot(ones, jnp.concatenate(block, axis=0), preferred_element_type=F32))
+        if len(blocks) == 1:
+            gathered[:, t : t + STEP] = chosen[0].astype(BF16)
+            continue
         for r in range(r_dev):
             top, bottom = [rows[r * window : (r + 1) * window] for rows in chosen]
             rows = [top[shared:] + bottom[: window - shared]]
@@ -366,29 +376,28 @@
                 gathered[start : start + part.shape[0], t : t + STEP] = part.astype(BF16)
 
 
-def multiply(gathered, hankel_ref, place, r, tile, lag):
+def multiply(gathered, hankel_ref, place, r, rows, lag):
     samples = gathered.shape[1]
     wide = jnp.concatenate(
         [hankel_ref[place, :, t + lag : t + lag + STEP] for t in range(0, samples, LANES)], axis=0
     )
-    return jnp.dot(gathered[r * 2 * tile : (r + 1) * 2 * tile, :], wide, preferred_element_type=F32)
-
-
-def split(total, high, low, slots, lags):
+    return jnp.dot(gathered[r * rows : (r + 1) * rows, :], wide, preferred_element_type=F32)
+
+
+def split(total, terms, slots, lags):
+    count = terms.shape[0] // 2
     upper = total.astype(BF16)
-    high[slots, lags] = upper
-    low[slots, lags] = (total - upper.astype(F32)).astype(BF16)
-
-
-def placed(place, high, low):
-    return jnp.dot(place, high[...], preferred_element_type=F32) + jnp.dot(
-        place, low[...], preferred_element_type=F32
-    )
-
-
-def correlate_kernel(parts, v, tile, norming, prebuilt, first, last, pass_ref, count_ref, number_ref, *refs):
+    terms[slots, lags] = upper
+    terms[slice(count + slots.start, count + slots.stop), lags] = (total - upper.astype(F32)).astype(BF16)
+
+
+def placed(place, terms):
+    return jnp.dot(jnp.concatenate([place, place], axis=1), terms[...], preferred_element_type=F32)
+
+
+def correlate_kernel(blocks, parts, v, tile, norming, prebuilt, first, last, pass_ref, count_ref, number_ref, *refs):
     refs = list(refs)
-    pieces = [refs.pop(0) for _ in range(2 * parts)]
+    pieces = [refs.pop(0) for _ in range(len(blocks) * parts)]
     signal_ref, pick_ref, place_ref, more_pick_ref, more_place_ref = [refs.pop(0) for _ in range(5)]
     if not first:
         sums_ref, extra_ref = refs.pop(0), refs.pop(0)
@@ -396,8 +405,9 @@
         out_ref = refs.pop(0)
     else:
         handed_ref, left_ref = refs.pop(0), refs.pop(0)
-    gathered, high, low, extra, pick_scratch, place_scratch = refs[:6]
-    r_dev = gathered.shape[0] // (2 * tile)
+    gathered, terms, extra, pick_scratch, place_scratch = refs[:5]
+    begin, rows = window_of(blocks, tile)
+    r_dev = gathered.shape[0] // rows
     samples = pieces[0].shape[1]
     lag_dev = extra.shape[1]
     group = pl.program_id(0)
@@ -406,27 +416,31 @@
         hankel_ref, hankel_place = signal_ref, group * r_dev
     else:
         hankel_place = 0
-        hankel_ref, row_ref = refs[6:]
+        hankel_ref, row_ref = refs[5:]
         n_win = signal_ref.shape[2] // samples
         lay_out([signal_ref[0, :, w * samples : (w + 1) * samples] for w in range(n_win)], number_ref, row_ref)
-        begin = first_sample(number_ref, v, n_win, samples)
+        start = first_sample(number_ref, v, n_win, samples)
         for r in range(r_dev):
-            hankel_rows(row_ref, r, begin, hankel_ref.shape[2], hankel_ref, r)
-
-    pick_rows(pieces, pick_ref.at[0], gathered, tile)
+            hankel_rows(row_ref, r, start, hankel_ref.shape[2], hankel_ref, r)
+
+    pick_rows(blocks, pieces, pick_ref.at[0], gathered, tile)
     for r in range(r_dev):
-        slots = slice(r * 2 * tile, (r + 1) * 2 * tile)
+        slots = slice(r * 2 * tile + begin, r * 2 * tile + begin + rows)
+        others = [slice(r * 2 * tile, slots.start), slice(slots.stop, (r + 1) * 2 * tile)]
         for lag in range(0, lag_dev, STEP):
             lags = slice(lag, lag + STEP)
-            total = multiply(gathered, hankel_ref, hankel_place + r, r, tile, lag)
+            total = multiply(gathered, hankel_ref, hankel_place + r, r, rows, lag)
             if not first:
                 total += sums_ref[group, slots, lags]
             if last:
-                split(total * norming, high, low, slots, lags)
+                split(total * norming, terms, slots, lags)
+                for other in others:
+                    if other.start < other.stop:
+                        split(sums_ref[group, other, lags] * norming, terms, other, lags)
             else:
                 handed_ref[group, slots, lags] = total
     if last:
-        out_ref[0] = placed(place_ref[0], high, low)
+        out_ref[0] = placed(place_ref[0], terms)
 
     @pl.when(pass_ref[group] > 1)
     def _():
@@ -438,23 +452,19 @@
         def one_pass(number, carry):
             pltpu.sync_copy(more_pick_ref.at[group, number - 1], pick_scratch)
             pltpu.sync_copy(more_place_ref.at[group, number - 1], place_scratch)
-            pick_rows(pieces, pick_scratch, gathered, tile)
+            pick_rows(blocks, pieces, pick_scratch, gathered, tile)
+            terms[...] = jnp.zeros(terms.shape, BF16)
             for r in range(r_dev):
                 needed = count_ref[group * r_dev + r] > (number - 1) * tile
-                slots = slice(r * 2 * tile, (r + 1) * 2 * tile)
+                slots = slice(r * 2 * tile + begin, r * 2 * tile + begin + rows)
 
                 @pl.when(needed)
                 def _():
                     for lag in range(0, lag_dev, STEP):
-                        total = multiply(gathered, hankel_ref, hankel_place + r, r, tile, lag)
-                        split(total * norming, high, low, slots, slice(lag, lag + STEP))
-
-                @pl.when(jnp.logical_not(needed))
-                def _():
-                    high[slots, :] = jnp.zeros((2 * tile, lag_dev), BF16)
-                    low[slots, :] = jnp.zeros((2 * tile, lag_dev), BF16)
-
-            extra[...] += placed(place_scratch[...], high, low)
+                        total = multiply(gathered, hankel_ref, hankel_place + r, r, rows, lag)
+                        split(total * norming, terms, slots, slice(lag, lag + STEP))
+
+            extra[...] += placed(place_scratch[...], terms)
             return carry
 
         lax.fori_loop(1, pass_ref[group], one_pass, 0)
@@ -464,12 +474,13 @@
             pltpu.sync_copy(extra, left_ref.at[group])
 
 
-def correlate(pieces, signal, prebuilt, numbers, v, matrices, before, last, tile, norming, lag_dev, n_win, r_dev):
+def correlate(blocks, pieces, signal, prebuilt, numbers, v, matrices, before, last, tile, norming, lag_dev, n_win, r_dev):
     pick, place, passes, counts, more_pick, more_place = matrices
-    parts = len(pieces) // 2
+    parts = len(pieces) // len(blocks)
     groups, cap, slots = place.shape
-    part_rows, samples = pieces[0].shape
+    samples = pieces[0].shape[1]
     width = samples - LANES + lag_dev
+    rows = window_of(blocks, tile)[1]
     by_group = lambda shape: pl.BlockSpec(shape, lambda i, *_: (i, 0, 0))
     any_spec = pl.BlockSpec(memory_space=pl.ANY)
     whole_spec = pl.BlockSpec(memory_space=pltpu.VMEM)
@@ -482,13 +493,15 @@
     in_specs.append(whole_spec if prebuilt else by_group((1,) + signal.shape[1:]))
     in_specs += [by_group((1,) + pick.shape[1:]), by_group((1,) + place.shape[1:]), any_spec, any_spec]
     args = pieces + [signal, pick, place, in_hbm(more_pick), in_hbm(more_place)]
+    aliases = {}
     if before is not None:
         in_specs += [whole_spec, any_spec]
         args += [before[0], in_hbm(before[1])]
+        if not last:
+            aliases = {3 + len(args) - 2: 0}
     scratch = [
-        pltpu.VMEM((slots, samples), BF16),
-        pltpu.VMEM((slots, lag_dev), BF16),
-        pltpu.VMEM((slots, lag_dev), BF16),
+        pltpu.VMEM((r_dev * rows, samples), BF16),
+        pltpu.VMEM((2 * slots, lag_dev), BF16),
         pltpu.VMEM((cap, lag_dev), F32),
         pltpu.VMEM(pick.shape[1:], BF16),
         pltpu.VMEM(place.shape[1:], BF16),
@@ -496,7 +509,9 @@
     if not prebuilt:
         scratch.append(pltpu.VMEM((r_dev, LANES, width), BF16))
         scratch.append(pltpu.VMEM((SHIFT_ROWS, n_win * samples + LAGS), F32))
-    body = functools.partial(correlate_kernel, parts, v, tile, norming, prebuilt, before is None, last)
+    body = functools.partial(
+        correlate_kernel, blocks, parts, v, tile, norming, prebuilt, before is None, last
+    )
     return pl.pallas_call(
         body,
         grid_spec=pltpu.PrefetchScalarGridSpec(
@@ -507,9 +522,10 @@
             scratch_shapes=scratch,
         ),
         out_shape=out_shape if last else [sums_shape, pltpu.HBM(out_shape.shape, F32)],
+        input_output_aliases=aliases,
         cost_estimate=pl.CostEstimate(
-            flops=4 * groups * r_dev * tile * samples * (lag_dev + parts * part_rows),
-            bytes_accessed=signal.size * signal.dtype.itemsize + 2 * groups * cap * lag_dev * 4,
+            flops=2 * groups * r_dev * rows * samples * (lag_dev + pick.shape[2]),
+            bytes_accessed=2 * groups * slots * lag_dev * 4,
             transcendentals=0,
         ),
         compiler_params=params(VMEM_BYTES if prebuilt else 2 * VMEM_BYTES),
@@ -589,13 +605,15 @@
         signals, near_spans = after_arrival(n_chan - 1, (signals, near_spans))
     far_spans = spans(choose(numbers, 3, arrived, sorted(arrived[0])))
 
+    calls = [(0, (0, 1))] + [(v, (q,)) for q in range(2) for v in range(1, n_win)]
     result = None
-    for v in range(n_win):
-        if v:
-            near_spans, far_spans, result = lax.optimization_barrier((near_spans, far_spans, result))
+    for v, blocks in calls:
+        if blocks == (1,):
+            far_spans, result = lax.optimization_barrier((far_spans, result))
+        pieces = [half for q in blocks for half in halves((near_spans, far_spans)[q][v])]
         result = correlate(
-            halves(near_spans[v]) + halves(far_spans[v]), signals[v], prebuilt, numbers, v, matrices, result, v == n_win - 1,
-            tile, norming, lag_dev, n_win, r_dev,
+            blocks, pieces, signals[v], prebuilt, numbers, v, matrices, result, (v, blocks) == calls[-1], tile, norming,
+            lag_dev, n_win, r_dev,
         )
     return result[None, None]
 

time: 80.9 us -> 85 us (1.051)
  Pallas kernels: 43.3 us -> 51.8 us
  waiting for transfers between devices: 13.7 us -> 9.22 us
    pallas_call x2 -> x3, Pallas kernels: 20.4 us -> 28.9 us  [correlate(): pl.pallas_call(body, grid_spec=pltpu.PrefetchScalarGridSpec(num_scalar_pr...]
    ppermute x10, waiting for transfers between devices: 10.9 us -> 6.38 us  [turned(): lax.ppermute(block, axis, [(i, (i + distance) % size) for i in range(size)])]
  transfers between devices with their start and end apart: 15 -> 15, of which waited for: 6 -> 4; matrix products, arithmetic and copies ran while one was open for 0% -> 0% of each run, Pallas kernels for 38% -> 46%
where the time goes in v5:
time: 85 us; the launch traced here: 84.7 us
  Pallas kernels  51.8 us (61%)
  starting transfers between devices  23.5 us (28%)
  waiting for transfers between devices  9.22 us (11%)
    pallas_call x3, Pallas kernels, correlate(): pl.pallas_call(body, grid_spec=pltpu.PrefetchScalarGridSpec(num_scalar_pr...  28.9 us
    pallas_call x4, Pallas kernels, build_hankel(): pl.pallas_call(functools.partial(hankel_kernel, v, n_win, samples, done),...  13.7 us
    ppermute x10, starting transfers between devices, turned(): lax.ppermute(block, axis, [(i, (i + distance) % size) for i in range(size)])  12.6 us
    ppermute x5, starting transfers between devices, swapped(): return lax.ppermute(block, axis, route)  10.9 us
    ppermute x10, waiting for transfers between devices, turned(): lax.ppermute(block, axis, [(i, (i + distance) % size) for i in range(size)])  6.38 us
    pallas_call x2, Pallas kernels, index(): pl.pallas_call(functools.partial(index_kernel, r_dev, lists_at, cap, tile...  5.29 us
    ppermute x5, waiting for transfers between devices, swapped(): return lax.ppermute(block, axis, route)  2.84 us
  transfers between devices with their start and end apart: 15, of which 4 were waited for; matrix products, arithmetic and copies ran while one was open for 0% of the time, Pallas kernels for 46%

profile of v5, /device:TPU:0, one launch (start us, length us, event | category | flops | bytes accessed | tf_op | source)
XLA Modules:
  0.0 84.7 jit_solution(5590327722916184305)
XLA Ops:
  0.0 1.0 %own_rows.1.refs_2_ = bf16[128,2048]{1,0:T(8,128)(2,1)S(1)} custom-call(bf16[256,2048]{1,0:T(8,128)(2,1)} %bitcast.4), custom_call_target="tpu_custom_call" | custom-call | tf_op jit(solution)/shard_map/own_rows/pallas_call | solution.py:128
  1.1 3.1 %collective-permute-start.4 = (bf16[128,2048]{1,0:T(8,128)(2,1)S(1)}, bf16[128,2048]{1,0:T(8,128)(2,1)S(1)}, u32[]{:S(2)}, u32[]{:S(2)}) collective-permute-start(bf16[128,2048]{1,0:T(8,128)(2,1)S(1)} %own_rows.1.refs_2_), channel_id=1, source_target_pairs={{0,4},{4,0},{8,12},{12,8},{1,5},{5,1},{9,13},{13,9},{2,6},{6,2},{1... | collective-permute-start | bytes 1572872 | tf_op jit(solution)/shard_map/ppermute | solution.py:29
  4.8 1.6 %collective-permute-start = (bf16[4,2048]{1,0:T(4,128)(2,1)}, bf16[4,2048]{1,0:T(4,128)(2,1)S(1)}, u32[]{:S(2)}, u32[]{:S(2)}) collective-permute-start(bf16[4,2048]{1,0:T(4,128)(2,1)} %refs_0_.1), channel_id=1, source_target_pairs={{0,2},{2,0},{1,3},{3,1},{4,6},{6,4},{5,7},{7,5},{8,10},{10,8},{9,1... | collective-permute-start | bytes 49160 | tf_op jit(solution)/shard_map/ppermute | solution.py:34
  6.4 2.5 %collective-permute-done.refs_1_ = bf16[4,2048]{1,0:T(4,128)(2,1)S(1)} collective-permute-done((bf16[4,2048]{1,0:T(4,128)(2,1)}, bf16[4,2048]{1,0:T(4,128)(2,1)S(1)}, u32[]{:S(2)}, u32[]{:S(2)}) %collective-permute-start) | collective-permute-done | bytes 16416 | tf_op jit(solution)/shard_map/ppermute | solution.py:34
  8.9 1.4 %pack.1 = (bf16[4,4352]{1,0:T(4,128)(2,1)S(1)}, bf16[4,4352]{1,0:T(4,128)(2,1)S(1)}, bf16[4,4352]{1,0:T(4,128)(2,1)S(1)}, bf16[4,4352]{1,0:T(4,128)(2,1)S(1)}, s32[7]{0:T(128)S(1)}) custom-call(s32[1,2]{1,0:T(1,128)} %plan_hbm.1, s32[4,512]{1,0:T(4,128)} %bitcast.5, s32[4,512]{1,0:T(4,128)} %bitcast.6, bf16[4,2048]{1,0:T(4,128)(2,1)} %refs_0_.1, ...), custom_call_target="tpu_custom_call" | custom-call | tf_op jit(solution)/shard_map/pack/pallas_call | solution.py:94
  10.3 4.4 %collective-permute-start.1 = (bf16[4,4352]{1,0:T(4,128)(2,1)S(1)}, bf16[4,4352]{1,0:T(4,128)(2,1)S(1)}, u32[]{:S(2)}, u32[]{:S(2)}) collective-permute-start(bf16[4,4352]{1,0:T(4,128)(2,1)S(1)} %get-tuple-element.54), channel_id=1, source_target_pairs={{0,4},{4,8},{8,12},{12,0},{1,5},{5,9},{9,13},{13,1},{2,6},{6,10},{... | collective-permute-start | bytes 104456 | tf_op jit(solution)/shard_map/ppermute | solution.py:34
  14.7 2.4 %collective-permute-start.3 = (bf16[4,4352]{1,0:T(4,128)(2,1)S(1)}, bf16[4,4352]{1,0:T(4,128)(2,1)S(1)}, u32[]{:S(2)}, u32[]{:S(2)}) collective-permute-start(bf16[4,4352]{1,0:T(4,128)(2,1)S(1)} %get-tuple-element.56), channel_id=1, source_target_pairs={{0,12},{4,0},{8,4},{12,8},{1,13},{5,1},{9,5},{13,9},{2,14},{6,2},{... | collective-permute-start | bytes 104456 | tf_op jit(solution)/shard_map/ppermute | solution.py:34
  17.1 2.0 %index.2 = (bf16[4,640,256]{2,1,0:T(8,128)(2,1)S(1)}, bf16[4,512,512]{2,1,0:T(8,128)(2,1)S(1)}, s32[4]{0:T(128)S(1)}, s32[16]{0:T(128)S(1)}, bf16[4,4,640,256]{3...) custom-call(s32[7]{0:T(128)S(1)} %get-tuple-element.53.number_ref, bf16[4,4352]{1,0:T(4,128)(2,1)S(1)} %get-tuple-element.57.refs_0_), custom_call_target="tpu_custom_call" | custom-call | tf_op jit(solution)/shard_map/index/pallas_call | solution.py:268
  19.2 1.9 %hankel.5.refs_3_ = bf16[16,128,2432]{2,1,0:T(8,128)(2,1)S(1)} custom-call(s32[7]{0:T(128)S(1)} %get-tuple-element.53.number_ref, bf16[4,4352]{1,0:T(4,128)(2,1)S(1)} %get-tuple-element.57.refs_0_), custom_call_target="tpu_custom_call" | custom-call | flops 1245184 | bytes 2490368 | tf_op jit(solution)/shard_map/hankel/pallas_call | solution.py:335
  21.1 1.9 %hankel.4.refs_3_ = bf16[16,128,2432]{2,1,0:T(8,128)(2,1)S(1)} custom-call(s32[7]{0:T(128)S(1)} %get-tuple-element.53.number_ref, bf16[4,4352]{1,0:T(4,128)(2,1)S(1)} %get-tuple-element.57.refs_0_), custom_call_target="tpu_custom_call" | custom-call | flops 1245184 | bytes 2490368 | tf_op jit(solution)/shard_map/hankel/pallas_call | solution.py:335
  23.8 3.3 %collective-permute-start.7 = (bf16[128,2048]{1,0:T(8,128)(2,1)S(1)}, bf16[128,2048]{1,0:T(8,128)(2,1)S(1)}, u32[]{:S(2)}, u32[]{:S(2)}) collective-permute-start(bf16[128,2048]{1,0:T(8,128)(2,1)S(1)} %collective-permute-done.5.refs_1_), channel_id=1, source_target_pairs={{0,4},{4,0},{8,12},{12,8},{1,5},{5,1},{9,13},{13,9},{2,6},{6,2},{1... | collective-permute-start | bytes 1572872 | tf_op jit(solution)/shard_map/ppermute | solution.py:29
  27.2 3.2 %index.3 = (bf16[4,640,256]{2,1,0:T(8,128)(2,1)S(1)}, bf16[4,512,512]{2,1,0:T(8,128)(2,1)S(1)}, s32[4]{0:T(128)S(1)}, s32[16]{0:T(128)S(1)}, bf16[4,4,640,256]{3...) custom-call(s32[7]{0:T(128)S(1)} %get-tuple-element.53.number_ref, ...), custom_call_target="tpu_custom_call", output_to_operand_aliasing={{0}: (4, {}), {1}: (5, {}), {4}: (8, {}), {5}: (9, {})} | custom-call | tf_op jit(solution)/shard_map/index/pallas_call | solution.py:268
  30.4 4.9 %hankel.6.refs_4_ = bf16[16,128,2432]{2,1,0:T(8,128)(2,1)S(1)} custom-call(s32[7]{0:T(128)S(1)} %get-tuple-element.53.number_ref, bf16[4,4352]{1,0:T(4,128)(2,1)S(1)} %collective-permute-done.1.refs_0_, bf16[4,4352]{1,0:T(4,128)(2,1)S(1)} %collective-permute-done.2.refs_1_, ...), custom_call_target="tpu_custom_call", output_to_operand_aliasing={{}: (4, {})} | custom-call | flops 3735552 | bytes 7471104 | tf_op jit(solution)/shard_map/hankel/pallas_call | solution.py:335
  35.4 3.1 %collective-permute-start.8 = (bf16[128,2048]{1,0:T(8,128)(2,1)S(1)}, bf16[128,2048]{1,0:T(8,128)(2,1)S(1)}, u32[]{:S(2)}, u32[]{:S(2)}) collective-permute-start(bf16[128,2048]{1,0:T(8,128)(2,1)S(1)} %collective-permute-done.6.refs_0_), channel_id=1, source_target_pairs={{0,4},{4,0},{8,12},{12,8},{1,5},{5,1},{9,13},{13,9},{2,6},{6,2},{1... | collective-permute-start | bytes 1572872 | tf_op jit(solution)/shard_map/ppermute | solution.py:29
  38.5 0.8 choose.3.refs_0_
  39.3 1.6 %collective-permute-start.10 = (bf16[128,2048]{1,0:T(8,128)(2,1)S(1)}, bf16[128,2048]{1,0:T(8,128)(2,1)S(1)}, u32[]{:S(2)}, u32[]{:S(2)}) collective-permute-start(bf16[128,2048]{1,0:T(8,128)(2,1)S(1)} %choose.3.refs_0_), channel_id=1, source_target_pairs={{0,2},{2,0},{1,3},{3,1},{4,6},{6,4},{5,7},{7,5},{8,10},{10,8},{9,1... | collective-permute-start | bytes 1572872 | tf_op jit(solution)/shard_map/ppermute | solution.py:34
  40.9 4.9 %hankel.7.refs_2_ = bf16[16,128,2432]{2,1,0:T(8,128)(2,1)S(1)} custom-call(s32[7]{0:T(128)S(1)} %get-tuple-element.53.number_ref, bf16[4,4352]{1,0:T(4,128)(2,1)S(1)} %collective-permute-done.1.refs_0_, bf16[4,4352]{1,0:T(4,128)(2,1)S(1)} %collective-permute-done.2.refs_1_, ...), custom_call_target="tpu_custom_call", output_to_operand_aliasing={{}: (4, {})} | custom-call | flops 3735552 | bytes 7471104 | tf_op jit(solution)/shard_map/hankel/pallas_call | solution.py:335
  45.8 2.8 %collective-permute-done.8.refs_5_ = bf16[128,2048]{1,0:T(8,128)(2,1)S(1)} collective-permute-done((bf16[128,2048]{1,0:T(8,128)(2,1)S(1)}, bf16[128,2048]{1,0:T(8,128)(2,1)S(1)}, u32[]{:S(2)}, u32[]{:S(2)}) %collective-permute-start.8) | collective-permute-done | bytes 524320 | tf_op jit(solution)/shard_map/ppermute | solution.py:29
  48.6 2.3 %collective-permute-done.10.refs_0_ = bf16[128,2048]{1,0:T(8,128)(2,1)S(1)} collective-permute-done((bf16[128,2048]{1,0:T(8,128)(2,1)S(1)}, bf16[128,2048]{1,0:T(8,128)(2,1)S(1)}, u32[]{:S(2)}, u32[]{:S(2)}) %collective-permute-start.10) | collective-permute-done | bytes 524320 | tf_op jit(solution)/shard_map/ppermute | solution.py:34
  52.2 1.5 %collective-permute-start.9 = (bf16[128,2048]{1,0:T(8,128)(2,1)S(1)}, bf16[128,2048]{1,0:T(8,128)(2,1)S(1)}, u32[]{:S(2)}, u32[]{:S(2)}) collective-permute-start(bf16[128,2048]{1,0:T(8,128)(2,1)S(1)} %choose.2.refs_2_), channel_id=1, source_target_pairs={{0,2},{2,0},{1,3},{3,1},{4,6},{6,4},{5,7},{7,5},{8,10},{10,8},{9,1... | collective-permute-start | bytes 1572872 | tf_op jit(solution)/shard_map/ppermute | solution.py:34
  53.7 8.5 %correlate.3 = (f32[4,512,512]{2,1,0:T(8,128)S(1)}, f32[4,512,512]{2,1,0:T(8,128)}) custom-call(s32[4]{0:T(128)S(1)} %get-tuple-element.72.pass_ref, s32[16]{0:T(128)S(1)} %get-tuple-element.73.count_ref, s32[7]{0:T(128)S(1)} %get-tuple-element.53.number_ref, bf16[128,2048]{1,0:T(8,128)(2,1)S(1)} %choose.3.refs_0_, ...), custom_call_target="tpu_custom_call" | custom-call | flops 6442450944 | bytes 8388608 | tf_op jit(solution)/shard_map/correlate/pallas_call | solution.py:515
  62.2 8.5 %correlate.4 = (f32[4,512,512]{2,1,0:T(8,128)S(1)}, f32[4,512,512]{2,1,0:T(8,128)}) custom-call(s32[4]{0:T(128)S(1)} %get-tuple-element.72.pass_ref, s32[16]{0:T(128)S(1)} %get-tuple-element.73.count_ref, s32[7]{0:T(128)S(1)} %get-tuple-element.53.number_ref, ...), custom_call_target="tpu_custom_call", output_to_operand_aliasing={{0}: (10, {})} | custom-call | flops 4026531840 | bytes 8388608 | tf_op jit(solution)/shard_map/correlate/pallas_call | solution.py:515
  71.3 1.5 %collective-permute-done.14.refs_1_ = bf16[128,2048]{1,0:T(8,128)(2,1)S(1)} collective-permute-done((bf16[128,2048]{1,0:T(8,128)(2,1)S(1)}, bf16[128,2048]{1,0:T(8,128)(2,1)S(1)}, u32[]{:S(2)}, u32[]{:S(2)}) %collective-permute-start.14) | collective-permute-done | bytes 524320 | tf_op jit(solution)/shard_map/ppermute | solution.py:34
  72.8 11.9 %correlate.5 = f32[4,512,512]{2,1,0:T(8,128)} custom-call(s32[4]{0:T(128)S(1)} %get-tuple-element.72.pass_ref, s32[16]{0:T(128)S(1)} %get-tuple-element.73.count_ref, s32[7]{0:T(128)S(1)} %get-tuple-element.53.number_ref, bf16[128,2048]{1,0:T(8,128)(2,1)S(1)} %collective-permute-done.9.refs_0_, bf16[128,2048]{1,0:T(8,128)(2,1)S(1)} %collective-permute-done.14.refs_1_, ...), custom_call_target="tpu_custom_call" | custom-call | flops 4026531840 | bytes 8388608 | tf_op jit(solution)/shard_map/correlate/pallas_call | solution.py:515
  (19 shorter events, 3.2 us)
Async XLA Ops:
  1.1 22.1 %collective-permute-start.4 = (bf16[128,2048]{1,0:T(8,128)(2,1)S(1)}, bf16[128,2048]{1,0:T(8,128)(2,1)S(1)}, u32[]{:S(2)}, u32[]{:S(2)}) collective-permute-start(bf16[128,2048]{1,0:T(8,128)(2,1)S(1)} %own_rows.1.refs_2_), channel_id=1, source_target_pairs={{0,4},{4,0},{8,12},{12,8},{1,5},{5,1},{9,13},{13,9},{2,6},{6,2},{1... | collective-permute-start | bytes 1572872 | tf_op jit(solution)/shard_map/ppermute | solution.py:29
  4.1 19.7 %collective-permute-start.5 = (bf16[128,2048]{1,0:T(8,128)(2,1)S(1)}, bf16[128,2048]{1,0:T(8,128)(2,1)S(1)}, u32[]{:S(2)}, u32[]{:S(2)}) collective-permute-start(bf16[128,2048]{1,0:T(8,128)(2,1)S(1)} %own_rows.1.refs_2_), channel_id=1, source_target_pairs={{4,8},{8,4},{5,9},{9,5},{6,10},{10,6},{7,11},{11,7},{20,24},{24,20... | collective-permute-start | bytes 1572872 | tf_op jit(solution)/shard_map/ppermute | solution.py:29
  4.8 4.0 %collective-permute-start = (bf16[4,2048]{1,0:T(4,128)(2,1)}, bf16[4,2048]{1,0:T(4,128)(2,1)S(1)}, u32[]{:S(2)}, u32[]{:S(2)}) collective-permute-start(bf16[4,2048]{1,0:T(4,128)(2,1)} %refs_0_.1), channel_id=1, source_target_pairs={{0,2},{2,0},{1,3},{3,1},{4,6},{6,4},{5,7},{7,5},{8,10},{10,8},{9,1... | collective-permute-start | bytes 49160 | tf_op jit(solution)/shard_map/ppermute | solution.py:34
  10.3 12.8 %collective-permute-start.1 = (bf16[4,4352]{1,0:T(4,128)(2,1)S(1)}, bf16[4,4352]{1,0:T(4,128)(2,1)S(1)}, u32[]{:S(2)}, u32[]{:S(2)}) collective-permute-start(bf16[4,4352]{1,0:T(4,128)(2,1)S(1)} %get-tuple-element.54), channel_id=1, source_target_pairs={{0,4},{4,8},{8,12},{12,0},{1,5},{5,9},{9,13},{13,1},{2,6},{6,10},{... | collective-permute-start | bytes 104456 | tf_op jit(solution)/shard_map/ppermute | solution.py:34
  14.7 8.4 %collective-permute-start.2 = (bf16[4,4352]{1,0:T(4,128)(2,1)S(1)}, bf16[4,4352]{1,0:T(4,128)(2,1)S(1)}, u32[]{:S(2)}, u32[]{:S(2)}) collective-permute-start(bf16[4,4352]{1,0:T(4,128)(2,1)S(1)} %get-tuple-element.55), channel_id=1, source_target_pairs={{0,8},{4,12},{8,0},{12,4},{1,9},{5,13},{9,1},{13,5},{2,10},{6,14},... | collective-permute-start | bytes 104456 | tf_op jit(solution)/shard_map/ppermute | solution.py:34
  14.7 8.4 %collective-permute-start.3 = (bf16[4,4352]{1,0:T(4,128)(2,1)S(1)}, bf16[4,4352]{1,0:T(4,128)(2,1)S(1)}, u32[]{:S(2)}, u32[]{:S(2)}) collective-permute-start(bf16[4,4352]{1,0:T(4,128)(2,1)S(1)} %get-tuple-element.56), channel_id=1, source_target_pairs={{0,12},{4,0},{8,4},{12,8},{1,13},{5,1},{9,5},{13,9},{2,14},{6,2},{... | collective-permute-start | bytes 104456 | tf_op jit(solution)/shard_map/ppermute | solution.py:34
  23.1 12.3 %collective-permute-start.6 = (bf16[128,2048]{1,0:T(8,128)(2,1)S(1)}, bf16[128,2048]{1,0:T(8,128)(2,1)S(1)}, u32[]{:S(2)}, u32[]{:S(2)}) collective-permute-start(bf16[128,2048]{1,0:T(8,128)(2,1)S(1)} %collective-permute-done.4.refs_3_), channel_id=1, source_target_pairs={{4,8},{8,4},{5,9},{9,5},{6,10},{10,6},{7,11},{11,7},{20,24},{24,20... | collective-permute-start | bytes 1572872 | tf_op jit(solution)/shard_map/ppermute | solution.py:29
  23.8 14.7 %collective-permute-start.7 = (bf16[128,2048]{1,0:T(8,128)(2,1)S(1)}, bf16[128,2048]{1,0:T(8,128)(2,1)S(1)}, u32[]{:S(2)}, u32[]{:S(2)}) collective-permute-start(bf16[128,2048]{1,0:T(8,128)(2,1)S(1)} %collective-permute-done.5.refs_1_), channel_id=1, source_target_pairs={{0,4},{4,0},{8,12},{12,8},{1,5},{5,1},{9,13},{13,9},{2,6},{6,2},{1... | collective-permute-start | bytes 1572872 | tf_op jit(solution)/shard_map/ppermute | solution.py:29
  35.4 13.2 %collective-permute-start.8 = (bf16[128,2048]{1,0:T(8,128)(2,1)S(1)}, bf16[128,2048]{1,0:T(8,128)(2,1)S(1)}, u32[]{:S(2)}, u32[]{:S(2)}) collective-permute-start(bf16[128,2048]{1,0:T(8,128)(2,1)S(1)} %collective-permute-done.6.refs_0_), channel_id=1, source_target_pairs={{0,4},{4,0},{8,12},{12,8},{1,5},{5,1},{9,13},{13,9},{2,6},{6,2},{1... | collective-permute-start | bytes 1572872 | tf_op jit(solution)/shard_map/ppermute | solution.py:29
  39.3 11.7 %collective-permute-start.10 = (bf16[128,2048]{1,0:T(8,128)(2,1)S(1)}, bf16[128,2048]{1,0:T(8,128)(2,1)S(1)}, u32[]{:S(2)}, u32[]{:S(2)}) collective-permute-start(bf16[128,2048]{1,0:T(8,128)(2,1)S(1)} %choose.3.refs_0_), channel_id=1, source_target_pairs={{0,2},{2,0},{1,3},{3,1},{4,6},{6,4},{5,7},{7,5},{8,10},{10,8},{9,1... | collective-permute-start | bytes 1572872 | tf_op jit(solution)/shard_map/ppermute | solution.py:34
  51.0 2.7 %collective-permute-start.12 = (bf16[128,2048]{1,0:T(8,128)(2,1)S(1)}, bf16[128,2048]{1,0:T(8,128)(2,1)S(1)}, u32[]{:S(2)}, u32[]{:S(2)}) collective-permute-start(bf16[128,2048]{1,0:T(8,128)(2,1)S(1)} %choose.3.refs_0_), channel_id=1, source_target_pairs={{0,1},{1,0},{2,3},{3,2},{4,5},{5,4},{6,7},{7,6},{8,9},{9,8},{10,11... | collective-permute-start | bytes 1572872 | tf_op jit(solution)/shard_map/ppermute | solution.py:34
  51.6 2.1 %collective-permute-start.13 = (bf16[128,2048]{1,0:T(8,128)(2,1)S(1)}, bf16[128,2048]{1,0:T(8,128)(2,1)S(1)}, u32[]{:S(2)}, u32[]{:S(2)}) collective-permute-start(bf16[128,2048]{1,0:T(8,128)(2,1)S(1)} %choose.2.refs_2_), channel_id=1, source_target_pairs={{0,1},{1,0},{2,3},{3,2},{4,5},{5,4},{6,7},{7,6},{8,9},{9,8},{10,11... | collective-permute-start | bytes 1572872 | tf_op jit(solution)/shard_map/ppermute | solution.py:34
  52.2 18.6 %collective-permute-start.9 = (bf16[128,2048]{1,0:T(8,128)(2,1)S(1)}, bf16[128,2048]{1,0:T(8,128)(2,1)S(1)}, u32[]{:S(2)}, u32[]{:S(2)}) collective-permute-start(bf16[128,2048]{1,0:T(8,128)(2,1)S(1)} %choose.2.refs_2_), channel_id=1, source_target_pairs={{0,2},{2,0},{1,3},{3,1},{4,6},{6,4},{5,7},{7,5},{8,10},{10,8},{9,1... | collective-permute-start | bytes 1572872 | tf_op jit(solution)/shard_map/ppermute | solution.py:34
  53.7 8.6 %collective-permute-start.11 = (bf16[128,2048]{1,0:T(8,128)(2,1)S(1)}, bf16[128,2048]{1,0:T(8,128)(2,1)S(1)}, u32[]{:S(2)}, u32[]{:S(2)}) collective-permute-start(bf16[128,2048]{1,0:T(8,128)(2,1)S(1)} %collective-permute-done.10.refs_0_), channel_id=1, source_target_pairs={{0,1},{1,0},{2,3},{3,2},{4,5},{5,4},{6,7},{7,6},{8,9},{9,8},{10,11... | collective-permute-start | bytes 1572872 | tf_op jit(solution)/shard_map/ppermute | solution.py:34
  70.8 2.1 %collective-permute-start.14 = (bf16[128,2048]{1,0:T(8,128)(2,1)S(1)}, bf16[128,2048]{1,0:T(8,128)(2,1)S(1)}, u32[]{:S(2)}, u32[]{:S(2)}) collective-permute-start(bf16[128,2048]{1,0:T(8,128)(2,1)S(1)} %collective-permute-done.9.refs_0_), channel_id=1, source_target_pairs={{0,1},{1,0},{2,3},{3,2},{4,5},{5,4},{6,7},{7,6},{8,9},{9,8},{10,11... | collective-permute-start | bytes 1572872 | tf_op jit(solution)/shard_map/ppermute | solution.py:34

commit v6 on v4

--- a/solution.py
+++ b/solution.py
@@ -12,7 +12,6 @@
 LANES = 128
 SHIFT_ROWS = 8
 STEP = 2 * LANES
-CHAINS = 1
 SPARE = 16
 DIGIT = 64
 HANKEL_BYTES = 24 * 2**20
@@ -110,64 +109,50 @@
     return parcels, numbers
 
 
-def own_kernel(source_ref, *refs):
-    chain_refs, sems = refs[:-1], refs[-1]
-    rows = chain_refs[0].shape[0]
-    copies = []
-    for chain, chain_ref in enumerate(chain_refs):
-        start = pl.multiple_of((lax.axis_index("rep") * CHAINS + chain) * rows, rows)
-        copies.append(pltpu.make_async_copy(source_ref.at[pl.ds(start, rows)], chain_ref, sems.at[chain]))
-        copies[-1].start()
-    for copy in copies:
-        copy.wait()
+def own_kernel(source_ref, own_ref, sem):
+    rows = own_ref.shape[0]
+    start = pl.multiple_of(lax.axis_index("rep") * rows, rows)
+    copy = pltpu.make_async_copy(source_ref.at[pl.ds(start, rows)], own_ref, sem)
+    copy.start()
+    copy.wait()
 
 
 def own_rows(sources, halves):
     block_rows, samples = sources.shape
-    shape = jax.ShapeDtypeStruct((block_rows // halves // CHAINS, samples), BF16)
     return pl.pallas_call(
         own_kernel,
         in_specs=[pl.BlockSpec(memory_space=pl.ANY)],
-        out_specs=[pl.BlockSpec(memory_space=pltpu.VMEM)] * CHAINS,
-        out_shape=[shape] * CHAINS,
-        scratch_shapes=[pltpu.SemaphoreType.DMA((CHAINS,))],
+        out_specs=pl.BlockSpec(memory_space=pltpu.VMEM),
+        out_shape=jax.ShapeDtypeStruct((block_rows // halves, samples), BF16),
+        scratch_shapes=[pltpu.SemaphoreType.DMA],
         compiler_params=params(VMEM_BYTES // 4),
         name="own_rows",
     )(in_hbm(sources))
 
 
 def choose_kernel(which, offsets, number_ref, *refs):
-    out_ref, sems = refs[-2:]
-    rows = out_ref.shape[0] // CHAINS
-    where = number_ref[which]
-    waits = []
-    for chain in range(CHAINS):
-        target = out_ref.at[pl.ds(chain * rows, rows)]
-        for place, offset in enumerate(offsets):
-            copy = pltpu.make_async_copy(refs[chain * len(offsets) + place], target, sems.at[chain])
-
-            @pl.when(where == offset)
-            def _():
-                copy.start()
-
-        waits.append(copy)
-    for copy in waits:
-        copy.wait()
+    out_ref, sem = refs[-2:]
+    for offset, block_ref in zip(offsets, refs):
+        copy = pltpu.make_async_copy(block_ref, out_ref, sem)
+
+        @pl.when(number_ref[which] == offset)
+        def _():
+            copy.start()
+
+    copy.wait()
 
 
 def choose(numbers, which, arrived, offsets):
-    pieces = [there[offset] for there in arrived for offset in offsets]
-    rows, samples = pieces[0].shape
-    any_spec = pl.BlockSpec(memory_space=pl.ANY)
+    blocks = [arrived[offset] for offset in offsets]
     return pl.pallas_call(
         functools.partial(choose_kernel, which, offsets),
-        in_specs=[pl.BlockSpec(memory_space=pltpu.SMEM)] + [any_spec] * len(pieces),
+        in_specs=[pl.BlockSpec(memory_space=pltpu.SMEM)] + [pl.BlockSpec(memory_space=pl.ANY)] * len(blocks),
         out_specs=pl.BlockSpec(memory_space=pltpu.VMEM),
-        out_shape=jax.ShapeDtypeStruct((rows * CHAINS, samples), BF16),
-        scratch_shapes=[pltpu.SemaphoreType.DMA((CHAINS,))],
+        out_shape=jax.ShapeDtypeStruct(blocks[0].shape, BF16),
+        scratch_shapes=[pltpu.SemaphoreType.DMA],
         compiler_params=params(VMEM_BYTES // 4),
         name="choose",
-    )(numbers, *pieces)
+    )(numbers, *blocks)
 
 
 def column(row):
@@ -345,15 +330,14 @@
     )(numbers, *parcels, *([earlier] if done else []))
 
 
-def pick_rows(pieces, pick, gathered, tile):
-    parts = len(pieces) // 2
+def pick_rows(pieces, pick, gathered, margin, tile):
     window = tile + SPARE
     shared = tile - SPARE
-    r_dev, samples = gathered.shape[0] // (2 * tile), gathered.shape[1]
+    r_dev, samples = gathered.shape[0] // (2 * tile), pieces[0][0].shape[1]
     for t in range(0, samples, STEP):
         chosen = []
         for q in range(2):
-            block = jnp.concatenate([piece[:, t : t + STEP] for piece in pieces[q * parts : (q + 1) * parts]], axis=0)
+            block = jnp.concatenate([piece[:, t : t + STEP] for piece in pieces[q]], axis=0)
             ones = pick[q * r_dev * window : (q + 1) * r_dev * window, :]
             chosen.append(jnp.dot(ones, block, preferred_element_type=F32))
         for r in range(r_dev):
@@ -363,15 +347,21 @@
                 rows = [top[:shared]] + rows + [bottom[window - shared :]]
             for place, part in zip((0, shared, window) if shared else (0,), rows):
                 start = r * 2 * tile + place
-                gathered[start : start + part.shape[0], t : t + STEP] = part.astype(BF16)
-
-
-def multiply(gathered, hankel_ref, place, r, tile, lag):
-    samples = gathered.shape[1]
-    wide = jnp.concatenate(
-        [hankel_ref[place, :, t + lag : t + lag + STEP] for t in range(0, samples, LANES)], axis=0
-    )
-    return jnp.dot(gathered[r * 2 * tile : (r + 1) * 2 * tile, :], wide, preferred_element_type=F32)
+                gathered[start : start + part.shape[0], margin + t : margin + t + STEP] = part.astype(BF16)
+
+
+def margin_of(lag_dev):
+    return lag_dev - STEP
+
+
+def multiply(gathered, hankel_ref, place, r, tile, lag_dev):
+    margin = margin_of(lag_dev)
+    length = gathered.shape[1] - margin
+    rows = slice(r * 2 * tile, (r + 1) * 2 * tile)
+    shifted = [gathered[rows, margin - lag : margin - lag + length] for lag in range(0, lag_dev, STEP)]
+    tiles = [hankel_ref[place, :, t : t + STEP] for t in range(0, length, LANES)]
+    both = jnp.dot(jnp.concatenate(shifted, axis=0), jnp.concatenate(tiles, axis=0), preferred_element_type=F32)
+    return [(slice(lag, lag + STEP), both[lag // STEP * 2 * tile :][: 2 * tile]) for lag in range(0, lag_dev, STEP)]
 
 
 def split(total, high, low, slots, lags):
@@ -386,9 +376,9 @@
     )
 
 
-def correlate_kernel(parts, v, tile, norming, prebuilt, first, last, pass_ref, count_ref, number_ref, *refs):
+def correlate_kernel(counts, v, tile, norming, prebuilt, first, last, pass_ref, count_ref, number_ref, *refs):
     refs = list(refs)
-    pieces = [refs.pop(0) for _ in range(2 * parts)]
+    pieces = [[refs.pop(0) for _ in range(count)] for count in counts]
     signal_ref, pick_ref, place_ref, more_pick_ref, more_place_ref = [refs.pop(0) for _ in range(5)]
     if not first:
         sums_ref, extra_ref = refs.pop(0), refs.pop(0)
@@ -398,7 +388,7 @@
         handed_ref, left_ref = refs.pop(0), refs.pop(0)
     gathered, high, low, extra, pick_scratch, place_scratch = refs[:6]
     r_dev = gathered.shape[0] // (2 * tile)
-    samples = pieces[0].shape[1]
+    samples = pieces[0][0].shape[1]
     lag_dev = extra.shape[1]
     group = pl.program_id(0)
 
@@ -413,12 +403,18 @@
         for r in range(r_dev):
             hankel_rows(row_ref, r, begin, hankel_ref.shape[2], hankel_ref, r)
 
-    pick_rows(pieces, pick_ref.at[0], gathered, tile)
+    margin = margin_of(lag_dev)
+    if margin:
+
+        @pl.when(group == 0)
+        def _():
+            for start in (0, margin + samples):
+                gathered[:, start : start + margin] = jnp.zeros((gathered.shape[0], margin), BF16)
+
+    pick_rows(pieces, pick_ref.at[0], gathered, margin, tile)
     for r in range(r_dev):
         slots = slice(r * 2 * tile, (r + 1) * 2 * tile)
-        for lag in range(0, lag_dev, STEP):
-            lags = slice(lag, lag + STEP)
-            total = multiply(gathered, hankel_ref, hankel_place + r, r, tile, lag)
+        for lags, total in multiply(gathered, hankel_ref, hankel_place + r, r, tile, lag_dev):
             if not first:
                 total += sums_ref[group, slots, lags]
             if last:
@@ -438,16 +434,15 @@
         def one_pass(number, carry):
             pltpu.sync_copy(more_pick_ref.at[group, number - 1], pick_scratch)
             pltpu.sync_copy(more_place_ref.at[group, number - 1], place_scratch)
-            pick_rows(pieces, pick_scratch, gathered, tile)
+            pick_rows(pieces, pick_scratch, gathered, margin, tile)
             for r in range(r_dev):
                 needed = count_ref[group * r_dev + r] > (number - 1) * tile
                 slots = slice(r * 2 * tile, (r + 1) * 2 * tile)
 
                 @pl.when(needed)
                 def _():
-                    for lag in range(0, lag_dev, STEP):
-                        total = multiply(gathered, hankel_ref, hankel_place + r, r, tile, lag)
-                        split(total * norming, high, low, slots, slice(lag, lag + STEP))
+                    for lags, total in multiply(gathered, hankel_ref, hankel_place + r, r, tile, lag_dev):
+                        split(total * norming, high, low, slots, lags)
 
                 @pl.when(jnp.logical_not(needed))
                 def _():
@@ -466,9 +461,10 @@
 
 def correlate(pieces, signal, prebuilt, numbers, v, matrices, before, last, tile, norming, lag_dev, n_win, r_dev):
     pick, place, passes, counts, more_pick, more_place = matrices
-    parts = len(pieces) // 2
     groups, cap, slots = place.shape
-    part_rows, samples = pieces[0].shape
+    counts_of_blocks = [len(of_block) for of_block in pieces]
+    pieces = [piece for of_block in pieces for piece in of_block]
+    samples = pieces[0].shape[1]
     width = samples - LANES + lag_dev
     by_group = lambda shape: pl.BlockSpec(shape, lambda i, *_: (i, 0, 0))
     any_spec = pl.BlockSpec(memory_space=pl.ANY)
@@ -486,7 +482,7 @@
         in_specs += [whole_spec, any_spec]
         args += [before[0], in_hbm(before[1])]
     scratch = [
-        pltpu.VMEM((slots, samples), BF16),
+        pltpu.VMEM((slots, samples + 2 * margin_of(lag_dev)), BF16),
         pltpu.VMEM((slots, lag_dev), BF16),
         pltpu.VMEM((slots, lag_dev), BF16),
         pltpu.VMEM((cap, lag_dev), F32),
@@ -496,7 +492,7 @@
     if not prebuilt:
         scratch.append(pltpu.VMEM((r_dev, LANES, width), BF16))
         scratch.append(pltpu.VMEM((SHIFT_ROWS, n_win * samples + LAGS), F32))
-    body = functools.partial(correlate_kernel, parts, v, tile, norming, prebuilt, before is None, last)
+    body = functools.partial(correlate_kernel, counts_of_blocks, v, tile, norming, prebuilt, before is None, last)
     return pl.pallas_call(
         body,
         grid_spec=pltpu.PrefetchScalarGridSpec(
@@ -508,7 +504,7 @@
         ),
         out_shape=out_shape if last else [sums_shape, pltpu.HBM(out_shape.shape, F32)],
         cost_estimate=pl.CostEstimate(
-            flops=4 * groups * r_dev * tile * samples * (lag_dev + parts * part_rows),
+            flops=4 * groups * r_dev * tile * samples * (lag_dev + pick.shape[2]),
             bytes_accessed=signal.size * signal.dtype.itemsize + 2 * groups * cap * lag_dev * 4,
             transcendentals=0,
         ),
@@ -531,7 +527,7 @@
     prebuilt = n_chan * r_dev * n_win * LANES * width * 2 <= HANKEL_BYTES
 
     heard = [receivers] + [turned(receivers, "win", v) for v in range(1, n_win)]
-    owns = own_rows(sources[0], n_rep)
+    own = own_rows(sources[0], n_rep)
     parcels, numbers = pack(plan, heard, pair_index[0, 0], keep[0, 0], n_rep, lag_dev, block_rows, n_chan)
     own_parcel = parcels[0]
     parcels = [turned(parcels[k], "chan", k) for k in range(1, n_chan)]
@@ -539,25 +535,20 @@
     if prebuilt:
         signals = [build_hankel([own_parcel], numbers, None, n_chan, v, n_win, samples, width) for v in range(n_win)]
 
-    arrived = [{0: own} for own in owns]
+    arrived = {0: own}
 
     def relay(step):
-        for there in arrived:
-            there[step] = swapped(there[1 - step], "chan", 0)
-            if step < n_chan - 1:
-                there[-step] = swapped(there[step - 1], "chan", 1)
+        arrived[step] = swapped(arrived[1 - step], "chan", 0)
+        if step < n_chan - 1:
+            arrived[-step] = swapped(arrived[step - 1], "chan", 1)
 
     def after_arrival(step, value):
-        for there in arrived:
-            for key in (step, -step):
-                if key in there:
-                    value = lax.optimization_barrier((value, there[key]))[0]
-        return value
+        keys = [key for key in (step, -step) if key in arrived]
+        return lax.optimization_barrier((value, [arrived[key] for key in keys]))[0]
 
     def before_start(step, value):
-        for there in arrived:
-            for key in (1 - step, step - 1):
-                there[key] = lax.optimization_barrier((value, there[key]))[1]
+        for key in (1 - step, step - 1):
+            arrived[key] = lax.optimization_barrier((value, arrived[key]))[1]
 
     def halves(piece):
         return [piece] + [turned(piece, "rep", -u) for u in range(1, n_rep)]
@@ -575,8 +566,9 @@
         before_start(3, (matrices, signals[0]))
     else:
         signals = [jnp.stack([own_parcel] + parcels)[:, :, : n_win * samples]] * n_win
-    reach = range(-(n_chan - 2), n_chan - 1)
-    near = choose(numbers, 2, arrived, [offset for offset in reach if offset in arrived[0]])
+    reach = [offset for offset in range(-(n_chan - 2), n_chan - 1) if offset in arrived]
+    near = choose(numbers, 2, arrived, reach)
+    before_start(3, near)
     if prebuilt:
         parcels = after_arrival(2, parcels)
         parcels, near = lax.optimization_barrier((parcels, near))
@@ -587,15 +579,17 @@
     near_spans = spans(near)
     if prebuilt:
         signals, near_spans = after_arrival(n_chan - 1, (signals, near_spans))
-    far_spans = spans(choose(numbers, 3, arrived, sorted(arrived[0])))
+        arrived[n_chan - 1] = lax.optimization_barrier((near_spans, arrived[n_chan - 1]))[1]
+    far_spans = spans(choose(numbers, 3, arrived, sorted(arrived)))
 
     result = None
     for v in range(n_win):
         if v:
             near_spans, far_spans, result = lax.optimization_barrier((near_spans, far_spans, result))
+        pieces = halves(near_spans[v]), halves(far_spans[v])
         result = correlate(
-            halves(near_spans[v]) + halves(far_spans[v]), signals[v], prebuilt, numbers, v, matrices, result, v == n_win - 1,
-            tile, norming, lag_dev, n_win, r_dev,
+            pieces, signals[v], prebuilt, numbers, v, matrices, result, v == n_win - 1, tile, norming, lag_dev, n_win,
+            r_dev,
         )
     return result[None, None]
 

time: 80.9 us -> 81.4 us (level)
  starting transfers between devices: 23.5 us -> 21.1 us
  waiting for transfers between devices: 13.7 us -> 15.2 us
  Pallas kernels: 43.3 us -> 44.7 us
    pallas_call x2, Pallas kernels: 20.4 us -> 21.8 us  [correlate(): pl.pallas_call(body, grid_spec=pltpu.PrefetchScalarGridSpec(num_scalar_pr...]
    ppermute x5, starting transfers between devices: 10.9 us -> 9.55 us  [swapped(): return lax.ppermute(block, axis, route)]
    ppermute x10, waiting for transfers between devices: 10.9 us -> 11.9 us  [turned(): lax.ppermute(block, axis, [(i, (i + distance) % size) for i in range(size)])]
    ppermute x10, starting transfers between devices: 12.5 us -> 11.6 us  [turned(): lax.ppermute(block, axis, [(i, (i + distance) % size) for i in range(size)])]
  transfers between devices with their start and end apart: 15 -> 15, of which waited for: 6 -> 9; matrix products, arithmetic and copies ran while one was open for 0% -> 0% of each run, Pallas kernels for 38% -> 36%
where the time goes in v6:
time: 81.4 us; the launch traced here: 81.2 us
  Pallas kernels  44.7 us (55%)
  starting transfers between devices  21.1 us (26%)
  waiting for transfers between devices  15.2 us (19%)
    pallas_call x2, Pallas kernels, correlate(): pl.pallas_call(body, grid_spec=pltpu.PrefetchScalarGridSpec(num_scalar_pr...  21.8 us
    pallas_call x4, Pallas kernels, build_hankel(): pl.pallas_call(functools.partial(hankel_kernel, v, n_win, samples, done),...  13.7 us
    ppermute x10, waiting for transfers between devices, turned(): lax.ppermute(block, axis, [(i, (i + distance) % size) for i in range(size)])  11.9 us
    ppermute x10, starting transfers between devices, turned(): lax.ppermute(block, axis, [(i, (i + distance) % size) for i in range(size)])  11.6 us
    ppermute x5, starting transfers between devices, swapped(): return lax.ppermute(block, axis, route)  9.55 us
    pallas_call x2, Pallas kernels, index(): pl.pallas_call(functools.partial(index_kernel, r_dev, lists_at, cap, tile...  5.29 us
    ppermute x5, waiting for transfers between devices, swapped(): return lax.ppermute(block, axis, route)  3.28 us
  transfers between devices with their start and end apart: 15, of which 9 were waited for; matrix products, arithmetic and copies ran while one was open for 0% of the time, Pallas kernels for 36%

profile of v6, /device:TPU:0, one launch (start us, length us, event | category | flops | bytes accessed | tf_op | source)
XLA Modules:
  0.0 81.2 jit_solution(13951540293023751649)
XLA Ops:
  0.0 1.0 %own_rows.1.refs_2_ = bf16[128,2048]{1,0:T(8,128)(2,1)S(1)} custom-call(bf16[256,2048]{1,0:T(8,128)(2,1)} %bitcast.4), custom_call_target="tpu_custom_call" | custom-call | tf_op jit(solution)/shard_map/own_rows/pallas_call | solution.py:122
  1.1 3.1 %collective-permute-start.4 = (bf16[128,2048]{1,0:T(8,128)(2,1)S(1)}, bf16[128,2048]{1,0:T(8,128)(2,1)S(1)}, u32[]{:S(2)}, u32[]{:S(2)}) collective-permute-start(bf16[128,2048]{1,0:T(8,128)(2,1)S(1)} %own_rows.1.refs_2_), channel_id=1, source_target_pairs={{0,4},{4,0},{8,12},{12,8},{1,5},{5,1},{9,13},{13,9},{2,6},{6,2},{1... | collective-permute-start | bytes 1572872 | tf_op jit(solution)/shard_map/ppermute | solution.py:28
  4.8 1.6 %collective-permute-start = (bf16[4,2048]{1,0:T(4,128)(2,1)}, bf16[4,2048]{1,0:T(4,128)(2,1)S(1)}, u32[]{:S(2)}, u32[]{:S(2)}) collective-permute-start(bf16[4,2048]{1,0:T(4,128)(2,1)} %refs_0_.1), channel_id=1, source_target_pairs={{0,2},{2,0},{1,3},{3,1},{4,6},{6,4},{5,7},{7,5},{8,10},{10,8},{9,1... | collective-permute-start | bytes 49160 | tf_op jit(solution)/shard_map/ppermute | solution.py:33
  6.4 2.5 %collective-permute-done.refs_1_ = bf16[4,2048]{1,0:T(4,128)(2,1)S(1)} collective-permute-done((bf16[4,2048]{1,0:T(4,128)(2,1)}, bf16[4,2048]{1,0:T(4,128)(2,1)S(1)}, u32[]{:S(2)}, u32[]{:S(2)}) %collective-permute-start) | collective-permute-done | bytes 16416 | tf_op jit(solution)/shard_map/ppermute | solution.py:33
  8.9 1.4 %pack.1 = (bf16[4,4352]{1,0:T(4,128)(2,1)S(1)}, bf16[4,4352]{1,0:T(4,128)(2,1)S(1)}, bf16[4,4352]{1,0:T(4,128)(2,1)S(1)}, bf16[4,4352]{1,0:T(4,128)(2,1)S(1)}, s32[7]{0:T(128)S(1)}) custom-call(s32[1,2]{1,0:T(1,128)} %plan_hbm.1, s32[4,512]{1,0:T(4,128)} %bitcast.5, s32[4,512]{1,0:T(4,128)} %bitcast.6, bf16[4,2048]{1,0:T(4,128)(2,1)} %refs_0_.1, ...), custom_call_target="tpu_custom_call" | custom-call | tf_op jit(solution)/shard_map/pack/pallas_call | solution.py:93
  10.3 4.4 %collective-permute-start.1 = (bf16[4,4352]{1,0:T(4,128)(2,1)S(1)}, bf16[4,4352]{1,0:T(4,128)(2,1)S(1)}, u32[]{:S(2)}, u32[]{:S(2)}) collective-permute-start(bf16[4,4352]{1,0:T(4,128)(2,1)S(1)} %get-tuple-element.50), channel_id=1, source_target_pairs={{0,4},{4,8},{8,12},{12,0},{1,5},{5,9},{9,13},{13,1},{2,6},{6,10},{... | collective-permute-start | bytes 104456 | tf_op jit(solution)/shard_map/ppermute | solution.py:33
  14.7 2.4 %collective-permute-start.3 = (bf16[4,4352]{1,0:T(4,128)(2,1)S(1)}, bf16[4,4352]{1,0:T(4,128)(2,1)S(1)}, u32[]{:S(2)}, u32[]{:S(2)}) collective-permute-start(bf16[4,4352]{1,0:T(4,128)(2,1)S(1)} %get-tuple-element.52), channel_id=1, source_target_pairs={{0,12},{4,0},{8,4},{12,8},{1,13},{5,1},{9,5},{13,9},{2,14},{6,2},{... | collective-permute-start | bytes 104456 | tf_op jit(solution)/shard_map/ppermute | solution.py:33
  17.1 2.0 %index.2 = (bf16[4,640,256]{2,1,0:T(8,128)(2,1)S(1)}, bf16[4,512,512]{2,1,0:T(8,128)(2,1)S(1)}, s32[4]{0:T(128)S(1)}, s32[16]{0:T(128)S(1)}, bf16[4,4,640,256]{3...) custom-call(s32[7]{0:T(128)S(1)} %get-tuple-element.49.number_ref, bf16[4,4352]{1,0:T(4,128)(2,1)S(1)} %get-tuple-element.53.refs_0_), custom_call_target="tpu_custom_call" | custom-call | tf_op jit(solution)/shard_map/index/pallas_call | solution.py:253
  19.2 1.9 %hankel.5.refs_3_ = bf16[16,128,2432]{2,1,0:T(8,128)(2,1)S(1)} custom-call(s32[7]{0:T(128)S(1)} %get-tuple-element.49.number_ref, bf16[4,4352]{1,0:T(4,128)(2,1)S(1)} %get-tuple-element.53.refs_0_), custom_call_target="tpu_custom_call" | custom-call | flops 1245184 | bytes 2490368 | tf_op jit(solution)/shard_map/hankel/pallas_call | solution.py:320
  21.1 1.9 %hankel.4.refs_3_ = bf16[16,128,2432]{2,1,0:T(8,128)(2,1)S(1)} custom-call(s32[7]{0:T(128)S(1)} %get-tuple-element.49.number_ref, bf16[4,4352]{1,0:T(4,128)(2,1)S(1)} %get-tuple-element.53.refs_0_), custom_call_target="tpu_custom_call" | custom-call | flops 1245184 | bytes 2490368 | tf_op jit(solution)/shard_map/hankel/pallas_call | solution.py:320
  23.8 3.3 %collective-permute-start.7 = (bf16[128,2048]{1,0:T(8,128)(2,1)S(1)}, bf16[128,2048]{1,0:T(8,128)(2,1)S(1)}, u32[]{:S(2)}, u32[]{:S(2)}) collective-permute-start(bf16[128,2048]{1,0:T(8,128)(2,1)S(1)} %collective-permute-done.5.refs_1_), channel_id=1, source_target_pairs={{0,4},{4,0},{8,12},{12,8},{1,5},{5,1},{9,13},{13,9},{2,6},{6,2},{1... | collective-permute-start | bytes 1572872 | tf_op jit(solution)/shard_map/ppermute | solution.py:28
  27.2 3.2 %index.3 = (bf16[4,640,256]{2,1,0:T(8,128)(2,1)S(1)}, bf16[4,512,512]{2,1,0:T(8,128)(2,1)S(1)}, s32[4]{0:T(128)S(1)}, s32[16]{0:T(128)S(1)}, bf16[4,4,640,256]{3...) custom-call(s32[7]{0:T(128)S(1)} %get-tuple-element.49.number_ref, ...), custom_call_target="tpu_custom_call", output_to_operand_aliasing={{0}: (4, {}), {1}: (5, {}), {4}: (8, {}), {5}: (9, {})} | custom-call | tf_op jit(solution)/shard_map/index/pallas_call | solution.py:253
  30.4 4.9 %hankel.6.refs_4_ = bf16[16,128,2432]{2,1,0:T(8,128)(2,1)S(1)} custom-call(s32[7]{0:T(128)S(1)} %get-tuple-element.49.number_ref, bf16[4,4352]{1,0:T(4,128)(2,1)S(1)} %collective-permute-done.1.refs_0_, bf16[4,4352]{1,0:T(4,128)(2,1)S(1)} %collective-permute-done.2.refs_1_, ...), custom_call_target="tpu_custom_call", output_to_operand_aliasing={{}: (4, {})} | custom-call | flops 3735552 | bytes 7471104 | tf_op jit(solution)/shard_map/hankel/pallas_call | solution.py:320
  35.4 1.9 %collective-permute-done.7.refs_4_ = bf16[128,2048]{1,0:T(8,128)(2,1)S(1)} collective-permute-done((bf16[128,2048]{1,0:T(8,128)(2,1)S(1)}, bf16[128,2048]{1,0:T(8,128)(2,1)S(1)}, u32[]{:S(2)}, u32[]{:S(2)}) %collective-permute-start.7) | collective-permute-done | bytes 524320 | tf_op jit(solution)/shard_map/ppermute | solution.py:28
  38.1 1.6 %collective-permute-start.8 = (bf16[128,2048]{1,0:T(8,128)(2,1)S(1)}, bf16[128,2048]{1,0:T(8,128)(2,1)S(1)}, u32[]{:S(2)}, u32[]{:S(2)}) collective-permute-start(bf16[128,2048]{1,0:T(8,128)(2,1)S(1)} %choose.2.refs_0_), channel_id=1, source_target_pairs={{0,2},{2,0},{1,3},{3,1},{4,6},{6,4},{5,7},{7,5},{8,10},{10,8},{9,1... | collective-permute-start | bytes 1572872 | tf_op jit(solution)/shard_map/ppermute | solution.py:33
  39.6 1.7 %collective-permute-start.9 = (bf16[128,2048]{1,0:T(8,128)(2,1)S(1)}, bf16[128,2048]{1,0:T(8,128)(2,1)S(1)}, u32[]{:S(2)}, u32[]{:S(2)}) collective-permute-start(bf16[128,2048]{1,0:T(8,128)(2,1)S(1)} %collective-permute-done.6.refs_0_), channel_id=1, source_target_pairs={{0,4},{4,0},{8,12},{12,8},{1,5},{5,1},{9,13},{13,9},{2,6},{6,2},{1... | collective-permute-start | bytes 1572872 | tf_op jit(solution)/shard_map/ppermute | solution.py:28
  41.4 4.9 %hankel.7.refs_4_ = bf16[16,128,2432]{2,1,0:T(8,128)(2,1)S(1)} custom-call(s32[7]{0:T(128)S(1)} %get-tuple-element.49.number_ref, bf16[4,4352]{1,0:T(4,128)(2,1)S(1)} %collective-permute-done.1.refs_0_, bf16[4,4352]{1,0:T(4,128)(2,1)S(1)} %collective-permute-done.2.refs_1_, ...), custom_call_target="tpu_custom_call", output_to_operand_aliasing={{}: (4, {})} | custom-call | flops 3735552 | bytes 7471104 | tf_op jit(solution)/shard_map/hankel/pallas_call | solution.py:320
  46.3 3.0 %collective-permute-done.8.refs_0_ = bf16[128,2048]{1,0:T(8,128)(2,1)S(1)} collective-permute-done((bf16[128,2048]{1,0:T(8,128)(2,1)S(1)}, bf16[128,2048]{1,0:T(8,128)(2,1)S(1)}, u32[]{:S(2)}, u32[]{:S(2)}) %collective-permute-start.8) | collective-permute-done | bytes 524320 | tf_op jit(solution)/shard_map/ppermute | solution.py:33
  49.3 1.4 %collective-permute-done.9.refs_5_ = bf16[128,2048]{1,0:T(8,128)(2,1)S(1)} collective-permute-done((bf16[128,2048]{1,0:T(8,128)(2,1)S(1)}, bf16[128,2048]{1,0:T(8,128)(2,1)S(1)}, u32[]{:S(2)}, u32[]{:S(2)}) %collective-permute-start.9) | collective-permute-done | bytes 524320 | tf_op jit(solution)/shard_map/ppermute | solution.py:28
  52.5 0.9 %collective-permute-done.12.refs_3_ = bf16[128,2048]{1,0:T(8,128)(2,1)S(1)} collective-permute-done((bf16[128,2048]{1,0:T(8,128)(2,1)S(1)}, bf16[128,2048]{1,0:T(8,128)(2,1)S(1)}, u32[]{:S(2)}, u32[]{:S(2)}) %collective-permute-start.12) | collective-permute-done | bytes 524320 | tf_op jit(solution)/shard_map/ppermute | solution.py:33
  54.1 9.1 %correlate.2 = (f32[4,512,512]{2,1,0:T(8,128)S(1)}, f32[4,512,512]{2,1,0:T(8,128)}) custom-call(s32[4]{0:T(128)S(1)} %get-tuple-element.65.pass_ref, s32[16]{0:T(128)S(1)} %get-tuple-element.66.count_ref, s32[7]{0:T(128)S(1)} %get-tuple-element.49.number_ref, bf16[128,2048]{1,0:T(8,128)(2,1)S(1)} %choose.2.refs_0_, ...), custom_call_target="tpu_custom_call" | custom-call | flops 6442450944 | bytes 18350080 | tf_op jit(solution)/shard_map/correlate/pallas_call | solution.py:496
  63.2 2.6 %collective-permute-done.10.refs_2_ = bf16[128,2048]{1,0:T(8,128)(2,1)S(1)} collective-permute-done((bf16[128,2048]{1,0:T(8,128)(2,1)S(1)}, bf16[128,2048]{1,0:T(8,128)(2,1)S(1)}, u32[]{:S(2)}, u32[]{:S(2)}) %collective-permute-start.10) | collective-permute-done | bytes 524320 | tf_op jit(solution)/shard_map/ppermute | solution.py:33
  66.4 1.4 %collective-permute-done.13.refs_1_ = bf16[128,2048]{1,0:T(8,128)(2,1)S(1)} collective-permute-done((bf16[128,2048]{1,0:T(8,128)(2,1)S(1)}, bf16[128,2048]{1,0:T(8,128)(2,1)S(1)}, u32[]{:S(2)}, u32[]{:S(2)}) %collective-permute-start.13) | collective-permute-done | bytes 524320 | tf_op jit(solution)/shard_map/ppermute | solution.py:33
  68.5 12.7 %correlate.3 = f32[4,512,512]{2,1,0:T(8,128)} custom-call(s32[4]{0:T(128)S(1)} %get-tuple-element.65.pass_ref, s32[16]{0:T(128)S(1)} %get-tuple-element.66.count_ref, s32[7]{0:T(128)S(1)} %get-tuple-element.49.number_ref, bf16[128,2048]{1,0:T(8,128)(2,1)S(1)} %collective-permute-done.8.refs_0_, bf16[128,2048]{1,0:T(8,128)(2,1)S(1)} %collective-permute-done.13.refs_1_, ...), custom_call_target="tpu_custom_call" | custom-call | flops 6442450944 | bytes 18350080 | tf_op jit(solution)/shard_map/correlate/pallas_call | solution.py:496
  (18 shorter events, 5.9 us)
Async XLA Ops:
  1.1 22.1 %collective-permute-start.4 = (bf16[128,2048]{1,0:T(8,128)(2,1)S(1)}, bf16[128,2048]{1,0:T(8,128)(2,1)S(1)}, u32[]{:S(2)}, u32[]{:S(2)}) collective-permute-start(bf16[128,2048]{1,0:T(8,128)(2,1)S(1)} %own_rows.1.refs_2_), channel_id=1, source_target_pairs={{0,4},{4,0},{8,12},{12,8},{1,5},{5,1},{9,13},{13,9},{2,6},{6,2},{1... | collective-permute-start | bytes 1572872 | tf_op jit(solution)/shard_map/ppermute | solution.py:28
  4.1 19.7 %collective-permute-start.5 = (bf16[128,2048]{1,0:T(8,128)(2,1)S(1)}, bf16[128,2048]{1,0:T(8,128)(2,1)S(1)}, u32[]{:S(2)}, u32[]{:S(2)}) collective-permute-start(bf16[128,2048]{1,0:T(8,128)(2,1)S(1)} %own_rows.1.refs_2_), channel_id=1, source_target_pairs={{4,8},{8,4},{5,9},{9,5},{6,10},{10,6},{7,11},{11,7},{20,24},{24,20... | collective-permute-start | bytes 1572872 | tf_op jit(solution)/shard_map/ppermute | solution.py:28
  4.8 4.0 %collective-permute-start = (bf16[4,2048]{1,0:T(4,128)(2,1)}, bf16[4,2048]{1,0:T(4,128)(2,1)S(1)}, u32[]{:S(2)}, u32[]{:S(2)}) collective-permute-start(bf16[4,2048]{1,0:T(4,128)(2,1)} %refs_0_.1), channel_id=1, source_target_pairs={{0,2},{2,0},{1,3},{3,1},{4,6},{6,4},{5,7},{7,5},{8,10},{10,8},{9,1... | collective-permute-start | bytes 49160 | tf_op jit(solution)/shard_map/ppermute | solution.py:33
  10.3 12.8 %collective-permute-start.1 = (bf16[4,4352]{1,0:T(4,128)(2,1)S(1)}, bf16[4,4352]{1,0:T(4,128)(2,1)S(1)}, u32[]{:S(2)}, u32[]{:S(2)}) collective-permute-start(bf16[4,4352]{1,0:T(4,128)(2,1)S(1)} %get-tuple-element.50), channel_id=1, source_target_pairs={{0,4},{4,8},{8,12},{12,0},{1,5},{5,9},{9,13},{13,1},{2,6},{6,10},{... | collective-permute-start | bytes 104456 | tf_op jit(solution)/shard_map/ppermute | solution.py:33
  14.7 8.4 %collective-permute-start.2 = (bf16[4,4352]{1,0:T(4,128)(2,1)S(1)}, bf16[4,4352]{1,0:T(4,128)(2,1)S(1)}, u32[]{:S(2)}, u32[]{:S(2)}) collective-permute-start(bf16[4,4352]{1,0:T(4,128)(2,1)S(1)} %get-tuple-element.51), channel_id=1, source_target_pairs={{0,8},{4,12},{8,0},{12,4},{1,9},{5,13},{9,1},{13,5},{2,10},{6,14},... | collective-permute-start | bytes 104456 | tf_op jit(solution)/shard_map/ppermute | solution.py:33
  14.7 8.4 %collective-permute-start.3 = (bf16[4,4352]{1,0:T(4,128)(2,1)S(1)}, bf16[4,4352]{1,0:T(4,128)(2,1)S(1)}, u32[]{:S(2)}, u32[]{:S(2)}) collective-permute-start(bf16[4,4352]{1,0:T(4,128)(2,1)S(1)} %get-tuple-element.52), channel_id=1, source_target_pairs={{0,12},{4,0},{8,4},{12,8},{1,13},{5,1},{9,5},{13,9},{2,14},{6,2},{... | collective-permute-start | bytes 104456 | tf_op jit(solution)/shard_map/ppermute | solution.py:33
  23.1 12.3 %collective-permute-start.6 = (bf16[128,2048]{1,0:T(8,128)(2,1)S(1)}, bf16[128,2048]{1,0:T(8,128)(2,1)S(1)}, u32[]{:S(2)}, u32[]{:S(2)}) collective-permute-start(bf16[128,2048]{1,0:T(8,128)(2,1)S(1)} %collective-permute-done.4.refs_3_), channel_id=1, source_target_pairs={{4,8},{8,4},{5,9},{9,5},{6,10},{10,6},{7,11},{11,7},{20,24},{24,20... | collective-permute-start | bytes 1572872 | tf_op jit(solution)/shard_map/ppermute | solution.py:28
  23.8 13.4 %collective-permute-start.7 = (bf16[128,2048]{1,0:T(8,128)(2,1)S(1)}, bf16[128,2048]{1,0:T(8,128)(2,1)S(1)}, u32[]{:S(2)}, u32[]{:S(2)}) collective-permute-start(bf16[128,2048]{1,0:T(8,128)(2,1)S(1)} %collective-permute-done.5.refs_1_), channel_id=1, source_target_pairs={{0,4},{4,0},{8,12},{12,8},{1,5},{5,1},{9,13},{13,9},{2,6},{6,2},{1... | collective-permute-start | bytes 1572872 | tf_op jit(solution)/shard_map/ppermute | solution.py:28
  38.1 11.2 %collective-permute-start.8 = (bf16[128,2048]{1,0:T(8,128)(2,1)S(1)}, bf16[128,2048]{1,0:T(8,128)(2,1)S(1)}, u32[]{:S(2)}, u32[]{:S(2)}) collective-permute-start(bf16[128,2048]{1,0:T(8,128)(2,1)S(1)} %choose.2.refs_0_), channel_id=1, source_target_pairs={{0,2},{2,0},{1,3},{3,1},{4,6},{6,4},{5,7},{7,5},{8,10},{10,8},{9,1... | collective-permute-start | bytes 1572872 | tf_op jit(solution)/shard_map/ppermute | solution.py:33
  39.6 11.1 %collective-permute-start.9 = (bf16[128,2048]{1,0:T(8,128)(2,1)S(1)}, bf16[128,2048]{1,0:T(8,128)(2,1)S(1)}, u32[]{:S(2)}, u32[]{:S(2)}) collective-permute-start(bf16[128,2048]{1,0:T(8,128)(2,1)S(1)} %collective-permute-done.6.refs_0_), channel_id=1, source_target_pairs={{0,4},{4,0},{8,12},{12,8},{1,5},{5,1},{9,13},{13,9},{2,6},{6,2},{1... | collective-permute-start | bytes 1572872 | tf_op jit(solution)/shard_map/ppermute | solution.py:28
  51.4 2.0 %collective-permute-start.12 = (bf16[128,2048]{1,0:T(8,128)(2,1)S(1)}, bf16[128,2048]{1,0:T(8,128)(2,1)S(1)}, u32[]{:S(2)}, u32[]{:S(2)}) collective-permute-start(bf16[128,2048]{1,0:T(8,128)(2,1)S(1)} %choose.3.refs_2_), channel_id=1, source_target_pairs={{0,1},{1,0},{2,3},{3,2},{4,5},{5,4},{6,7},{7,6},{8,9},{9,8},{10,11... | collective-permute-start | bytes 1572872 | tf_op jit(solution)/shard_map/ppermute | solution.py:33
  51.4 2.6 %collective-permute-start.11 = (bf16[128,2048]{1,0:T(8,128)(2,1)S(1)}, bf16[128,2048]{1,0:T(8,128)(2,1)S(1)}, u32[]{:S(2)}, u32[]{:S(2)}) collective-permute-start(bf16[128,2048]{1,0:T(8,128)(2,1)S(1)} %choose.2.refs_0_), channel_id=1, source_target_pairs={{0,1},{1,0},{2,3},{3,2},{4,5},{5,4},{6,7},{7,6},{8,9},{9,8},{10,11... | collective-permute-start | bytes 1572872 | tf_op jit(solution)/shard_map/ppermute | solution.py:33
  51.9 13.9 %collective-permute-start.10 = (bf16[128,2048]{1,0:T(8,128)(2,1)S(1)}, bf16[128,2048]{1,0:T(8,128)(2,1)S(1)}, u32[]{:S(2)}, u32[]{:S(2)}) collective-permute-start(bf16[128,2048]{1,0:T(8,128)(2,1)S(1)} %choose.3.refs_2_), channel_id=1, source_target_pairs={{0,2},{2,0},{1,3},{3,1},{4,6},{6,4},{5,7},{7,5},{8,10},{10,8},{9,1... | collective-permute-start | bytes 1572872 | tf_op jit(solution)/shard_map/ppermute | solution.py:33
  65.8 1.9 %collective-permute-start.13 = (bf16[128,2048]{1,0:T(8,128)(2,1)S(1)}, bf16[128,2048]{1,0:T(8,128)(2,1)S(1)}, u32[]{:S(2)}, u32[]{:S(2)}) collective-permute-start(bf16[128,2048]{1,0:T(8,128)(2,1)S(1)} %collective-permute-done.8.refs_0_), channel_id=1, source_target_pairs={{0,1},{1,0},{2,3},{3,2},{4,5},{5,4},{6,7},{7,6},{8,9},{9,8},{10,11... | collective-permute-start | bytes 1572872 | tf_op jit(solution)/shard_map/ppermute | solution.py:33
  65.8 2.7 %collective-permute-start.14 = (bf16[128,2048]{1,0:T(8,128)(2,1)S(1)}, bf16[128,2048]{1,0:T(8,128)(2,1)S(1)}, u32[]{:S(2)}, u32[]{:S(2)}) collective-permute-start(bf16[128,2048]{1,0:T(8,128)(2,1)S(1)} %collective-permute-done.10.refs_2_), channel_id=1, source_target_pairs={{0,1},{1,0},{2,3},{3,2},{4,5},{5,4},{6,7},{7,6},{8,9},{9,8},{10,11... | collective-permute-start | bytes 1572872 | tf_op jit(solution)/shard_map/ppermute | solution.py:33

commit v7 on v4

--- a/solution.py
+++ b/solution.py
@@ -27,6 +27,11 @@
     for i in range(first, size - 1, 2):
         route += [(i, i + 1), (i + 1, i)]
     return lax.ppermute(block, axis, route)
+
+
+def ends_swapped(block, axis):
+    last = lax.axis_size(axis) - 1
+    return lax.ppermute(block, axis, [(0, last), (last, 0)])
 
 
 def turned(block, axis, distance):
@@ -544,8 +549,7 @@
     def relay(step):
         for there in arrived:
             there[step] = swapped(there[1 - step], "chan", 0)
-            if step < n_chan - 1:
-                there[-step] = swapped(there[step - 1], "chan", 1)
+            there[-step] = swapped(there[step - 1], "chan", 1)
 
     def after_arrival(step, value):
         for there in arrived:
@@ -575,6 +579,7 @@
         before_start(3, (matrices, signals[0]))
     else:
         signals = [jnp.stack([own_parcel] + parcels)[:, :, : n_win * samples]] * n_win
+    own_late = [lax.optimization_barrier((matrices, own))[1] for own in owns]
     reach = range(-(n_chan - 2), n_chan - 1)
     near = choose(numbers, 2, arrived, [offset for offset in reach if offset in arrived[0]])
     if prebuilt:
@@ -582,11 +587,15 @@
         parcels, near = lax.optimization_barrier((parcels, near))
         for v in range(1, n_win):
             signals[v] = build_hankel(parcels, numbers, signals[v], n_chan, v, n_win, samples, width)
-    for step in range(3, n_chan):
+    for step in range(3, n_chan - 1):
         relay(step)
+    for there, own in zip(arrived, own_late):
+        there[n_chan - 1] = ends_swapped(own, "chan")
     near_spans = spans(near)
     if prebuilt:
-        signals, near_spans = after_arrival(n_chan - 1, (signals, near_spans))
+        near_spans = after_arrival(n_chan - 1, near_spans)
+        for there in arrived:
+            there[n_chan - 1] = lax.optimization_barrier((signals, there[n_chan - 1]))[1]
     far_spans = spans(choose(numbers, 3, arrived, sorted(arrived[0])))
 
     result = None

time: 80.9 us -> 80.9 us (level)
    ppermute x0 -> x1, waiting for transfers between devices: none -> 3.59 us  [ends_swapped(): return lax.ppermute(block, axis, [(0, last), (last, 0)])]
    ppermute x0 -> x1, starting transfers between devices: none -> 3.45 us  [ends_swapped(): return lax.ppermute(block, axis, [(0, last), (last, 0)])]
    ppermute x5 -> x4, starting transfers between devices: 10.9 us -> 7.81 us  [swapped(): return lax.ppermute(block, axis, route)]
    ppermute x5 -> x4, waiting for transfers between devices: 2.84 us -> 0.72 us  [swapped(): return lax.ppermute(block, axis, route)]
    ppermute x10, waiting for transfers between devices: 10.9 us -> 9.47 us  [turned(): lax.ppermute(block, axis, [(i, (i + distance) % size) for i in range(size)])]
  transfers between devices with their start and end apart: 15 -> 15, of which waited for: 6 -> 8; matrix products, arithmetic and copies ran while one was open for 0% -> 0% of each run, Pallas kernels for 38% -> 38%
where the time goes in v7:
time: 80.9 us; the launch traced here: 80.6 us
  Pallas kernels  43.3 us (54%)
  starting transfers between devices  23.3 us (29%)
  waiting for transfers between devices  13.8 us (17%)
    pallas_call x2, Pallas kernels, correlate(): pl.pallas_call(body, grid_spec=pltpu.PrefetchScalarGridSpec(num_scalar_pr...  20.4 us
    pallas_call x4, Pallas kernels, build_hankel(): pl.pallas_call(functools.partial(hankel_kernel, v, n_win, samples, done),...  13.7 us
    ppermute x10, starting transfers between devices, turned(): lax.ppermute(block, axis, [(i, (i + distance) % size) for i in range(size)])  12 us
    ppermute x10, waiting for transfers between devices, turned(): lax.ppermute(block, axis, [(i, (i + distance) % size) for i in range(size)])  9.47 us
    ppermute x4, starting transfers between devices, swapped(): return lax.ppermute(block, axis, route)  7.81 us
    pallas_call x2, Pallas kernels, index(): pl.pallas_call(functools.partial(index_kernel, r_dev, lists_at, cap, tile...  5.29 us
    ppermute x1, waiting for transfers between devices, ends_swapped(): return lax.ppermute(block, axis, [(0, last), (last, 0)])  3.59 us
    ppermute x1, starting transfers between devices, ends_swapped(): return lax.ppermute(block, axis, [(0, last), (last, 0)])  3.45 us
  transfers between devices with their start and end apart: 15, of which 8 were waited for; matrix products, arithmetic and copies ran while one was open for 0% of the time, Pallas kernels for 38%

profile of v7, /device:TPU:0, one launch (start us, length us, event | category | flops | bytes accessed | tf_op | source)
XLA Modules:
  0.0 80.6 jit_solution(14073766322875155595)
XLA Ops:
  0.0 1.0 %own_rows.1.refs_2_ = bf16[128,2048]{1,0:T(8,128)(2,1)S(1)} custom-call(bf16[256,2048]{1,0:T(8,128)(2,1)} %bitcast.4), custom_call_target="tpu_custom_call" | custom-call | tf_op jit(solution)/shard_map/own_rows/pallas_call | solution.py:133
  1.1 3.1 %collective-permute-start.4 = (bf16[128,2048]{1,0:T(8,128)(2,1)S(1)}, bf16[128,2048]{1,0:T(8,128)(2,1)S(1)}, u32[]{:S(2)}, u32[]{:S(2)}) collective-permute-start(bf16[128,2048]{1,0:T(8,128)(2,1)S(1)} %own_rows.1.refs_2_), channel_id=1, source_target_pairs={{0,4},{4,0},{8,12},{12,8},{1,5},{5,1},{9,13},{13,9},{2,6},{6,2},{1... | collective-permute-start | bytes 1572872 | tf_op jit(solution)/shard_map/ppermute | solution.py:29
  4.8 1.6 %collective-permute-start = (bf16[4,2048]{1,0:T(4,128)(2,1)}, bf16[4,2048]{1,0:T(4,128)(2,1)S(1)}, u32[]{:S(2)}, u32[]{:S(2)}) collective-permute-start(bf16[4,2048]{1,0:T(4,128)(2,1)} %refs_0_.1), channel_id=1, source_target_pairs={{0,2},{2,0},{1,3},{3,1},{4,6},{6,4},{5,7},{7,5},{8,10},{10,8},{9,1... | collective-permute-start | bytes 49160 | tf_op jit(solution)/shard_map/ppermute | solution.py:39
  6.4 2.5 %collective-permute-done.refs_1_ = bf16[4,2048]{1,0:T(4,128)(2,1)S(1)} collective-permute-done((bf16[4,2048]{1,0:T(4,128)(2,1)}, bf16[4,2048]{1,0:T(4,128)(2,1)S(1)}, u32[]{:S(2)}, u32[]{:S(2)}) %collective-permute-start) | collective-permute-done | bytes 16416 | tf_op jit(solution)/shard_map/ppermute | solution.py:39
  8.9 1.4 %pack.1 = (bf16[4,4352]{1,0:T(4,128)(2,1)S(1)}, bf16[4,4352]{1,0:T(4,128)(2,1)S(1)}, bf16[4,4352]{1,0:T(4,128)(2,1)S(1)}, bf16[4,4352]{1,0:T(4,128)(2,1)S(1)}, s32[7]{0:T(128)S(1)}) custom-call(s32[1,2]{1,0:T(1,128)} %plan_hbm.1, s32[4,512]{1,0:T(4,128)} %bitcast.5, s32[4,512]{1,0:T(4,128)} %bitcast.6, bf16[4,2048]{1,0:T(4,128)(2,1)} %refs_0_.1, ...), custom_call_target="tpu_custom_call" | custom-call | tf_op jit(solution)/shard_map/pack/pallas_call | solution.py:99
  10.3 4.4 %collective-permute-start.1 = (bf16[4,4352]{1,0:T(4,128)(2,1)S(1)}, bf16[4,4352]{1,0:T(4,128)(2,1)S(1)}, u32[]{:S(2)}, u32[]{:S(2)}) collective-permute-start(bf16[4,4352]{1,0:T(4,128)(2,1)S(1)} %get-tuple-element.53), channel_id=1, source_target_pairs={{0,4},{4,8},{8,12},{12,0},{1,5},{5,9},{9,13},{13,1},{2,6},{6,10},{... | collective-permute-start | bytes 104456 | tf_op jit(solution)/shard_map/ppermute | solution.py:39
  14.7 2.4 %collective-permute-start.3 = (bf16[4,4352]{1,0:T(4,128)(2,1)S(1)}, bf16[4,4352]{1,0:T(4,128)(2,1)S(1)}, u32[]{:S(2)}, u32[]{:S(2)}) collective-permute-start(bf16[4,4352]{1,0:T(4,128)(2,1)S(1)} %get-tuple-element.55), channel_id=1, source_target_pairs={{0,12},{4,0},{8,4},{12,8},{1,13},{5,1},{9,5},{13,9},{2,14},{6,2},{... | collective-permute-start | bytes 104456 | tf_op jit(solution)/shard_map/ppermute | solution.py:39
  17.1 2.0 %index.2 = (bf16[4,640,256]{2,1,0:T(8,128)(2,1)S(1)}, bf16[4,512,512]{2,1,0:T(8,128)(2,1)S(1)}, s32[4]{0:T(128)S(1)}, s32[16]{0:T(128)S(1)}, bf16[4,4,640,256]{3...) custom-call(s32[7]{0:T(128)S(1)} %get-tuple-element.52.number_ref, bf16[4,4352]{1,0:T(4,128)(2,1)S(1)} %get-tuple-element.56.refs_0_), custom_call_target="tpu_custom_call" | custom-call | tf_op jit(solution)/shard_map/index/pallas_call | solution.py:273
  19.2 1.9 %hankel.5.refs_3_ = bf16[16,128,2432]{2,1,0:T(8,128)(2,1)S(1)} custom-call(s32[7]{0:T(128)S(1)} %get-tuple-element.52.number_ref, bf16[4,4352]{1,0:T(4,128)(2,1)S(1)} %get-tuple-element.56.refs_0_), custom_call_target="tpu_custom_call" | custom-call | flops 1245184 | bytes 2490368 | tf_op jit(solution)/shard_map/hankel/pallas_call | solution.py:340
  21.1 1.9 %hankel.4.refs_3_ = bf16[16,128,2432]{2,1,0:T(8,128)(2,1)S(1)} custom-call(s32[7]{0:T(128)S(1)} %get-tuple-element.52.number_ref, bf16[4,4352]{1,0:T(4,128)(2,1)S(1)} %get-tuple-element.56.refs_0_), custom_call_target="tpu_custom_call" | custom-call | flops 1245184 | bytes 2490368 | tf_op jit(solution)/shard_map/hankel/pallas_call | solution.py:340
  23.8 3.3 %collective-permute-start.6 = (bf16[128,2048]{1,0:T(8,128)(2,1)S(1)}, bf16[128,2048]{1,0:T(8,128)(2,1)S(1)}, u32[]{:S(2)}, u32[]{:S(2)}) collective-permute-start(bf16[128,2048]{1,0:T(8,128)(2,1)S(1)} %collective-permute-done.5.refs_1_), channel_id=1, source_target_pairs={{0,4},{4,0},{8,12},{12,8},{1,5},{5,1},{9,13},{13,9},{2,6},{6,2},{1... | collective-permute-start | bytes 1572872 | tf_op jit(solution)/shard_map/ppermute | solution.py:29
  27.2 3.2 %index.3 = (bf16[4,640,256]{2,1,0:T(8,128)(2,1)S(1)}, bf16[4,512,512]{2,1,0:T(8,128)(2,1)S(1)}, s32[4]{0:T(128)S(1)}, s32[16]{0:T(128)S(1)}, bf16[4,4,640,256]{3...) custom-call(s32[7]{0:T(128)S(1)} %get-tuple-element.52.number_ref, ...), custom_call_target="tpu_custom_call", output_to_operand_aliasing={{0}: (4, {}), {1}: (5, {}), {4}: (8, {}), {5}: (9, {})} | custom-call | tf_op jit(solution)/shard_map/index/pallas_call | solution.py:273
  30.4 3.5 %collective-permute-start.9 = (bf16[128,2048]{1,0:T(8,128)(2,1)S(1)}, bf16[128,2048]{1,0:T(8,128)(2,1)S(1)}, u32[]{:S(2)}, u32[]{:S(2)}) collective-permute-start(bf16[128,2048]{1,0:T(8,128)(2,1)S(1)} %own_rows.1.refs_2_), channel_id=1, source_target_pairs={{0,12},{12,0},{1,13},{13,1},{2,14},{14,2},{3,15},{15,3},{16,28},{2... | collective-permute-start | bytes 1572872 | tf_op jit(solution)/shard_map/ppermute | solution.py:34
  33.9 4.9 %hankel.6.refs_4_ = bf16[16,128,2432]{2,1,0:T(8,128)(2,1)S(1)} custom-call(s32[7]{0:T(128)S(1)} %get-tuple-element.52.number_ref, bf16[4,4352]{1,0:T(4,128)(2,1)S(1)} %collective-permute-done.1.refs_0_, bf16[4,4352]{1,0:T(4,128)(2,1)S(1)} %collective-permute-done.2.refs_1_, ...), custom_call_target="tpu_custom_call", output_to_operand_aliasing={{}: (4, {})} | custom-call | flops 3735552 | bytes 7471104 | tf_op jit(solution)/shard_map/hankel/pallas_call | solution.py:340
  39.6 0.8 choose.2.refs_0_
  40.4 1.6 %collective-permute-start.8 = (bf16[128,2048]{1,0:T(8,128)(2,1)S(1)}, bf16[128,2048]{1,0:T(8,128)(2,1)S(1)}, u32[]{:S(2)}, u32[]{:S(2)}) collective-permute-start(bf16[128,2048]{1,0:T(8,128)(2,1)S(1)} %choose.2.refs_0_), channel_id=1, source_target_pairs={{0,2},{2,0},{1,3},{3,1},{4,6},{6,4},{5,7},{7,5},{8,10},{10,8},{9,1... | collective-permute-start | bytes 1572872 | tf_op jit(solution)/shard_map/ppermute | solution.py:39
  41.9 4.9 %hankel.7.refs_4_ = bf16[16,128,2432]{2,1,0:T(8,128)(2,1)S(1)} custom-call(s32[7]{0:T(128)S(1)} %get-tuple-element.52.number_ref, bf16[4,4352]{1,0:T(4,128)(2,1)S(1)} %collective-permute-done.1.refs_0_, bf16[4,4352]{1,0:T(4,128)(2,1)S(1)} %collective-permute-done.2.refs_1_, ...), custom_call_target="tpu_custom_call", output_to_operand_aliasing={{}: (4, {})} | custom-call | flops 3735552 | bytes 7471104 | tf_op jit(solution)/shard_map/hankel/pallas_call | solution.py:340
  46.9 3.6 %collective-permute-done.9.refs_5_ = bf16[128,2048]{1,0:T(8,128)(2,1)S(1)} collective-permute-done((bf16[128,2048]{1,0:T(8,128)(2,1)S(1)}, bf16[128,2048]{1,0:T(8,128)(2,1)S(1)}, u32[]{:S(2)}, u32[]{:S(2)}) %collective-permute-start.9) | collective-permute-done | bytes 524320 | tf_op jit(solution)/shard_map/ppermute | solution.py:34
  51.7 1.5 %collective-permute-start.10 = (bf16[128,2048]{1,0:T(8,128)(2,1)S(1)}, bf16[128,2048]{1,0:T(8,128)(2,1)S(1)}, u32[]{:S(2)}, u32[]{:S(2)}) collective-permute-start(bf16[128,2048]{1,0:T(8,128)(2,1)S(1)} %choose.3.refs_2_), channel_id=1, source_target_pairs={{0,2},{2,0},{1,3},{3,1},{4,6},{6,4},{5,7},{7,5},{8,10},{10,8},{9,1... | collective-permute-start | bytes 1572872 | tf_op jit(solution)/shard_map/ppermute | solution.py:39
  53.8 8.5 %correlate.2 = (f32[4,512,512]{2,1,0:T(8,128)S(1)}, f32[4,512,512]{2,1,0:T(8,128)}) custom-call(s32[4]{0:T(128)S(1)} %get-tuple-element.71.pass_ref, s32[16]{0:T(128)S(1)} %get-tuple-element.72.count_ref, s32[7]{0:T(128)S(1)} %get-tuple-element.52.number_ref, bf16[128,2048]{1,0:T(8,128)(2,1)S(1)} %choose.2.refs_0_, ...), custom_call_target="tpu_custom_call" | custom-call | flops 6442450944 | bytes 18350080 | tf_op jit(solution)/shard_map/correlate/pallas_call | solution.py:505
  62.3 3.7 %collective-permute-done.10.refs_2_ = bf16[128,2048]{1,0:T(8,128)(2,1)S(1)} collective-permute-done((bf16[128,2048]{1,0:T(8,128)(2,1)S(1)}, bf16[128,2048]{1,0:T(8,128)(2,1)S(1)}, u32[]{:S(2)}, u32[]{:S(2)}) %collective-permute-start.10) | collective-permute-done | bytes 524320 | tf_op jit(solution)/shard_map/ppermute | solution.py:39
  66.5 1.4 %collective-permute-done.13.refs_1_ = bf16[128,2048]{1,0:T(8,128)(2,1)S(1)} collective-permute-done((bf16[128,2048]{1,0:T(8,128)(2,1)S(1)}, bf16[128,2048]{1,0:T(8,128)(2,1)S(1)}, u32[]{:S(2)}, u32[]{:S(2)}) %collective-permute-start.13) | collective-permute-done | bytes 524320 | tf_op jit(solution)/shard_map/ppermute | solution.py:39
  67.9 0.7 collective-permute-done.14.refs_3_
  68.7 11.9 %correlate.3 = f32[4,512,512]{2,1,0:T(8,128)} custom-call(s32[4]{0:T(128)S(1)} %get-tuple-element.71.pass_ref, s32[16]{0:T(128)S(1)} %get-tuple-element.72.count_ref, s32[7]{0:T(128)S(1)} %get-tuple-element.52.number_ref, bf16[128,2048]{1,0:T(8,128)(2,1)S(1)} %collective-permute-done.8.refs_0_, bf16[128,2048]{1,0:T(8,128)(2,1)S(1)} %collective-permute-done.13.refs_1_, ...), custom_call_target="tpu_custom_call" | custom-call | flops 6442450944 | bytes 18350080 | tf_op jit(solution)/shard_map/correlate/pallas_call | solution.py:505
  (18 shorter events, 4.5 us)
Async XLA Ops:
  1.1 22.1 %collective-permute-start.4 = (bf16[128,2048]{1,0:T(8,128)(2,1)S(1)}, bf16[128,2048]{1,0:T(8,128)(2,1)S(1)}, u32[]{:S(2)}, u32[]{:S(2)}) collective-permute-start(bf16[128,2048]{1,0:T(8,128)(2,1)S(1)} %own_rows.1.refs_2_), channel_id=1, source_target_pairs={{0,4},{4,0},{8,12},{12,8},{1,5},{5,1},{9,13},{13,9},{2,6},{6,2},{1... | collective-permute-start | bytes 1572872 | tf_op jit(solution)/shard_map/ppermute | solution.py:29
  4.1 19.7 %collective-permute-start.5 = (bf16[128,2048]{1,0:T(8,128)(2,1)S(1)}, bf16[128,2048]{1,0:T(8,128)(2,1)S(1)}, u32[]{:S(2)}, u32[]{:S(2)}) collective-permute-start(bf16[128,2048]{1,0:T(8,128)(2,1)S(1)} %own_rows.1.refs_2_), channel_id=1, source_target_pairs={{4,8},{8,4},{5,9},{9,5},{6,10},{10,6},{7,11},{11,7},{20,24},{24,20... | collective-permute-start | bytes 1572872 | tf_op jit(solution)/shard_map/ppermute | solution.py:29
  4.8 4.0 %collective-permute-start = (bf16[4,2048]{1,0:T(4,128)(2,1)}, bf16[4,2048]{1,0:T(4,128)(2,1)S(1)}, u32[]{:S(2)}, u32[]{:S(2)}) collective-permute-start(bf16[4,2048]{1,0:T(4,128)(2,1)} %refs_0_.1), channel_id=1, source_target_pairs={{0,2},{2,0},{1,3},{3,1},{4,6},{6,4},{5,7},{7,5},{8,10},{10,8},{9,1... | collective-permute-start | bytes 49160 | tf_op jit(solution)/shard_map/ppermute | solution.py:39
  10.3 12.8 %collective-permute-start.1 = (bf16[4,4352]{1,0:T(4,128)(2,1)S(1)}, bf16[4,4352]{1,0:T(4,128)(2,1)S(1)}, u32[]{:S(2)}, u32[]{:S(2)}) collective-permute-start(bf16[4,4352]{1,0:T(4,128)(2,1)S(1)} %get-tuple-element.53), channel_id=1, source_target_pairs={{0,4},{4,8},{8,12},{12,0},{1,5},{5,9},{9,13},{13,1},{2,6},{6,10},{... | collective-permute-start | bytes 104456 | tf_op jit(solution)/shard_map/ppermute | solution.py:39
  14.7 8.4 %collective-permute-start.2 = (bf16[4,4352]{1,0:T(4,128)(2,1)S(1)}, bf16[4,4352]{1,0:T(4,128)(2,1)S(1)}, u32[]{:S(2)}, u32[]{:S(2)}) collective-permute-start(bf16[4,4352]{1,0:T(4,128)(2,1)S(1)} %get-tuple-element.54), channel_id=1, source_target_pairs={{0,8},{4,12},{8,0},{12,4},{1,9},{5,13},{9,1},{13,5},{2,10},{6,14},... | collective-permute-start | bytes 104456 | tf_op jit(solution)/shard_map/ppermute | solution.py:39
  14.7 8.4 %collective-permute-start.3 = (bf16[4,4352]{1,0:T(4,128)(2,1)S(1)}, bf16[4,4352]{1,0:T(4,128)(2,1)S(1)}, u32[]{:S(2)}, u32[]{:S(2)}) collective-permute-start(bf16[4,4352]{1,0:T(4,128)(2,1)S(1)} %get-tuple-element.55), channel_id=1, source_target_pairs={{0,12},{4,0},{8,4},{12,8},{1,13},{5,1},{9,5},{13,9},{2,14},{6,2},{... | collective-permute-start | bytes 104456 | tf_op jit(solution)/shard_map/ppermute | solution.py:39
  23.1 15.7 %collective-permute-start.7 = (bf16[128,2048]{1,0:T(8,128)(2,1)S(1)}, bf16[128,2048]{1,0:T(8,128)(2,1)S(1)}, u32[]{:S(2)}, u32[]{:S(2)}) collective-permute-start(bf16[128,2048]{1,0:T(8,128)(2,1)S(1)} %collective-permute-done.4.refs_3_), channel_id=1, source_target_pairs={{4,8},{8,4},{5,9},{9,5},{6,10},{10,6},{7,11},{11,7},{20,24},{24,20... | collective-permute-start | bytes 1572872 | tf_op jit(solution)/shard_map/ppermute | solution.py:29
  23.8 15.7 %collective-permute-start.6 = (bf16[128,2048]{1,0:T(8,128)(2,1)S(1)}, bf16[128,2048]{1,0:T(8,128)(2,1)S(1)}, u32[]{:S(2)}, u32[]{:S(2)}) collective-permute-start(bf16[128,2048]{1,0:T(8,128)(2,1)S(1)} %collective-permute-done.5.refs_1_), channel_id=1, source_target_pairs={{0,4},{4,0},{8,12},{12,8},{1,5},{5,1},{9,13},{13,9},{2,6},{6,2},{1... | collective-permute-start | bytes 1572872 | tf_op jit(solution)/shard_map/ppermute | solution.py:29
  30.4 20.0 %collective-permute-start.9 = (bf16[128,2048]{1,0:T(8,128)(2,1)S(1)}, bf16[128,2048]{1,0:T(8,128)(2,1)S(1)}, u32[]{:S(2)}, u32[]{:S(2)}) collective-permute-start(bf16[128,2048]{1,0:T(8,128)(2,1)S(1)} %own_rows.1.refs_2_), channel_id=1, source_target_pairs={{0,12},{12,0},{1,13},{13,1},{2,14},{14,2},{3,15},{15,3},{16,28},{2... | collective-permute-start | bytes 1572872 | tf_op jit(solution)/shard_map/ppermute | solution.py:34
  40.4 11.3 %collective-permute-start.8 = (bf16[128,2048]{1,0:T(8,128)(2,1)S(1)}, bf16[128,2048]{1,0:T(8,128)(2,1)S(1)}, u32[]{:S(2)}, u32[]{:S(2)}) collective-permute-start(bf16[128,2048]{1,0:T(8,128)(2,1)S(1)} %choose.2.refs_0_), channel_id=1, source_target_pairs={{0,2},{2,0},{1,3},{3,1},{4,6},{6,4},{5,7},{7,5},{8,10},{10,8},{9,1... | collective-permute-start | bytes 1572872 | tf_op jit(solution)/shard_map/ppermute | solution.py:39
  51.1 2.1 %collective-permute-start.12 = (bf16[128,2048]{1,0:T(8,128)(2,1)S(1)}, bf16[128,2048]{1,0:T(8,128)(2,1)S(1)}, u32[]{:S(2)}, u32[]{:S(2)}) collective-permute-start(bf16[128,2048]{1,0:T(8,128)(2,1)S(1)} %choose.3.refs_2_), channel_id=1, source_target_pairs={{0,1},{1,0},{2,3},{3,2},{4,5},{5,4},{6,7},{7,6},{8,9},{9,8},{10,11... | collective-permute-start | bytes 1572872 | tf_op jit(solution)/shard_map/ppermute | solution.py:39
  51.7 2.1 %collective-permute-start.11 = (bf16[128,2048]{1,0:T(8,128)(2,1)S(1)}, bf16[128,2048]{1,0:T(8,128)(2,1)S(1)}, u32[]{:S(2)}, u32[]{:S(2)}) collective-permute-start(bf16[128,2048]{1,0:T(8,128)(2,1)S(1)} %choose.2.refs_0_), channel_id=1, source_target_pairs={{0,1},{1,0},{2,3},{3,2},{4,5},{5,4},{6,7},{7,6},{8,9},{9,8},{10,11... | collective-permute-start | bytes 1572872 | tf_op jit(solution)/shard_map/ppermute | solution.py:39
  51.7 14.3 %collective-permute-start.10 = (bf16[128,2048]{1,0:T(8,128)(2,1)S(1)}, bf16[128,2048]{1,0:T(8,128)(2,1)S(1)}, u32[]{:S(2)}, u32[]{:S(2)}) collective-permute-start(bf16[128,2048]{1,0:T(8,128)(2,1)S(1)} %choose.3.refs_2_), channel_id=1, source_target_pairs={{0,2},{2,0},{1,3},{3,1},{4,6},{6,4},{5,7},{7,5},{8,10},{10,8},{9,1... | collective-permute-start | bytes 1572872 | tf_op jit(solution)/shard_map/ppermute | solution.py:39
  66.0 1.9 %collective-permute-start.13 = (bf16[128,2048]{1,0:T(8,128)(2,1)S(1)}, bf16[128,2048]{1,0:T(8,128)(2,1)S(1)}, u32[]{:S(2)}, u32[]{:S(2)}) collective-permute-start(bf16[128,2048]{1,0:T(8,128)(2,1)S(1)} %collective-permute-done.8.refs_0_), channel_id=1, source_target_pairs={{0,1},{1,0},{2,3},{3,2},{4,5},{5,4},{6,7},{7,6},{8,9},{9,8},{10,11... | collective-permute-start | bytes 1572872 | tf_op jit(solution)/shard_map/ppermute | solution.py:39
  66.0 2.7 %collective-permute-start.14 = (bf16[128,2048]{1,0:T(8,128)(2,1)S(1)}, bf16[128,2048]{1,0:T(8,128)(2,1)S(1)}, u32[]{:S(2)}, u32[]{:S(2)}) collective-permute-start(bf16[128,2048]{1,0:T(8,128)(2,1)S(1)} %collective-permute-done.10.refs_2_), channel_id=1, source_target_pairs={{0,1},{1,0},{2,3},{3,2},{4,5},{5,4},{6,7},{7,6},{8,9},{9,8},{10,11... | collective-permute-start | bytes 1572872 | tf_op jit(solution)/shard_map/ppermute | solution.py:39

commit v8 on v5

--- a/solution.py
+++ b/solution.py
@@ -345,43 +345,31 @@
     )(numbers, *parcels, *([earlier] if done else []))
 
 
-def window_of(blocks, tile):
-    if len(blocks) == 2:
-        return 0, 2 * tile
-    return (tile - SPARE if blocks[0] else 0), tile + SPARE
-
-
-def pick_rows(blocks, pieces, pick, gathered, tile):
-    parts = len(pieces) // len(blocks)
-    window = tile + SPARE
-    shared = tile - SPARE
-    rows_of_channel = window_of(blocks, tile)[1]
-    r_dev, samples = gathered.shape[0] // rows_of_channel, gathered.shape[1]
+def window_of(block, tile):
+    return (tile - SPARE if block else 0), tile + SPARE
+
+
+def pick_rows(block, pieces, pick, gathered, margin):
+    count, samples = gathered.shape[0], pieces[0].shape[1]
+    ones = pick[block * count : (block + 1) * count, :]
     for t in range(0, samples, STEP):
-        chosen = []
-        for place, q in enumerate(blocks):
-            block = [piece[:, t : t + STEP] for piece in pieces[place * parts : (place + 1) * parts]]
-            ones = pick[q * r_dev * window : (q + 1) * r_dev * window, :]
-            chosen.append(jnp.dot(ones, jnp.concatenate(block, axis=0), preferred_element_type=F32))
-        if len(blocks) == 1:
-            gathered[:, t : t + STEP] = chosen[0].astype(BF16)
-            continue
-        for r in range(r_dev):
-            top, bottom = [rows[r * window : (r + 1) * window] for rows in chosen]
-            rows = [top[shared:] + bottom[: window - shared]]
-            if shared:
-                rows = [top[:shared]] + rows + [bottom[window - shared :]]
-            for place, part in zip((0, shared, window) if shared else (0,), rows):
-                start = r * 2 * tile + place
-                gathered[start : start + part.shape[0], t : t + STEP] = part.astype(BF16)
-
-
-def multiply(gathered, hankel_ref, place, r, rows, lag):
-    samples = gathered.shape[1]
-    wide = jnp.concatenate(
-        [hankel_ref[place, :, t + lag : t + lag + STEP] for t in range(0, samples, LANES)], axis=0
-    )
-    return jnp.dot(gathered[r * rows : (r + 1) * rows, :], wide, preferred_element_type=F32)
+        rows = jnp.concatenate([piece[:, t : t + STEP] for piece in pieces], axis=0)
+        chosen = jnp.dot(ones, rows, preferred_element_type=F32)
+        gathered[:, margin + t : margin + t + STEP] = chosen.astype(BF16)
+
+
+def margin_of(lag_dev):
+    return lag_dev - STEP
+
+
+def multiply(gathered, hankel_ref, place, r, rows, lag_dev):
+    margin = margin_of(lag_dev)
+    length = gathered.shape[1] - margin
+    of_channel = slice(r * rows, (r + 1) * rows)
+    shifted = [gathered[of_channel, margin - lag : margin - lag + length] for lag in range(0, lag_dev, STEP)]
+    tiles = [hankel_ref[place, :, t : t + STEP] for t in range(0, length, LANES)]
+    both = jnp.dot(jnp.concatenate(shifted, axis=0), jnp.concatenate(tiles, axis=0), preferred_element_type=F32)
+    return [(slice(lag, lag + STEP), both[lag // STEP * rows :][:rows]) for lag in range(0, lag_dev, STEP)]
 
 
 def split(total, terms, slots, lags):
@@ -395,9 +383,9 @@
     return jnp.dot(jnp.concatenate([place, place], axis=1), terms[...], preferred_element_type=F32)
 
 
-def correlate_kernel(blocks, parts, v, tile, norming, prebuilt, first, last, pass_ref, count_ref, number_ref, *refs):
+def correlate_kernel(block, parts, v, tile, norming, prebuilt, first, last, pass_ref, count_ref, number_ref, *refs):
     refs = list(refs)
-    pieces = [refs.pop(0) for _ in range(len(blocks) * parts)]
+    pieces = [refs.pop(0) for _ in range(parts)]
     signal_ref, pick_ref, place_ref, more_pick_ref, more_place_ref = [refs.pop(0) for _ in range(5)]
     if not first:
         sums_ref, extra_ref = refs.pop(0), refs.pop(0)
@@ -406,7 +394,7 @@
     else:
         handed_ref, left_ref = refs.pop(0), refs.pop(0)
     gathered, terms, extra, pick_scratch, place_scratch = refs[:5]
-    begin, rows = window_of(blocks, tile)
+    begin, rows = window_of(block, tile)
     r_dev = gathered.shape[0] // rows
     samples = pieces[0].shape[1]
     lag_dev = extra.shape[1]
@@ -423,22 +411,30 @@
         for r in range(r_dev):
             hankel_rows(row_ref, r, start, hankel_ref.shape[2], hankel_ref, r)
 
-    pick_rows(blocks, pieces, pick_ref.at[0], gathered, tile)
+    margin = margin_of(lag_dev)
+    if margin:
+
+        @pl.when(group == 0)
+        def _():
+            for start in (0, margin + samples):
+                gathered[:, start : start + margin] = jnp.zeros((gathered.shape[0], margin), BF16)
+
+    pick_rows(block, pieces, pick_ref.at[0], gathered, margin)
     for r in range(r_dev):
         slots = slice(r * 2 * tile + begin, r * 2 * tile + begin + rows)
         others = [slice(r * 2 * tile, slots.start), slice(slots.stop, (r + 1) * 2 * tile)]
-        for lag in range(0, lag_dev, STEP):
-            lags = slice(lag, lag + STEP)
-            total = multiply(gathered, hankel_ref, hankel_place + r, r, rows, lag)
+        others = [other for other in others if other.start < other.stop]
+        for lags, total in multiply(gathered, hankel_ref, hankel_place + r, r, rows, lag_dev):
             if not first:
                 total += sums_ref[group, slots, lags]
             if last:
                 split(total * norming, terms, slots, lags)
                 for other in others:
-                    if other.start < other.stop:
-                        split(sums_ref[group, other, lags] * norming, terms, other, lags)
+                    split(sums_ref[group, other, lags] * norming, terms, other, lags)
             else:
                 handed_ref[group, slots, lags] = total
+                for other in others if first else []:
+                    handed_ref[group, other, lags] = jnp.zeros((other.stop - other.start, STEP), F32)
     if last:
         out_ref[0] = placed(place_ref[0], terms)
 
@@ -452,7 +448,7 @@
         def one_pass(number, carry):
             pltpu.sync_copy(more_pick_ref.at[group, number - 1], pick_scratch)
             pltpu.sync_copy(more_place_ref.at[group, number - 1], place_scratch)
-            pick_rows(blocks, pieces, pick_scratch, gathered, tile)
+            pick_rows(block, pieces, pick_scratch, gathered, margin)
             terms[...] = jnp.zeros(terms.shape, BF16)
             for r in range(r_dev):
                 needed = count_ref[group * r_dev + r] > (number - 1) * tile
@@ -460,9 +456,8 @@
 
                 @pl.when(needed)
                 def _():
-                    for lag in range(0, lag_dev, STEP):
-                        total = multiply(gathered, hankel_ref, hankel_place + r, r, rows, lag)
-                        split(total * norming, terms, slots, slice(lag, lag + STEP))
+                    for lags, total in multiply(gathered, hankel_ref, hankel_place + r, r, rows, lag_dev):
+                        split(total * norming, terms, slots, lags)
 
             extra[...] += placed(place_scratch[...], terms)
             return carry
@@ -474,13 +469,12 @@
             pltpu.sync_copy(extra, left_ref.at[group])
 
 
-def correlate(blocks, pieces, signal, prebuilt, numbers, v, matrices, before, last, tile, norming, lag_dev, n_win, r_dev):
+def correlate(block, pieces, signal, prebuilt, numbers, v, matrices, before, last, tile, norming, lag_dev, n_win, r_dev):
     pick, place, passes, counts, more_pick, more_place = matrices
-    parts = len(pieces) // len(blocks)
     groups, cap, slots = place.shape
     samples = pieces[0].shape[1]
     width = samples - LANES + lag_dev
-    rows = window_of(blocks, tile)[1]
+    rows = window_of(block, tile)[1]
     by_group = lambda shape: pl.BlockSpec(shape, lambda i, *_: (i, 0, 0))
     any_spec = pl.BlockSpec(memory_space=pl.ANY)
     whole_spec = pl.BlockSpec(memory_space=pltpu.VMEM)
@@ -500,7 +494,7 @@
         if not last:
             aliases = {3 + len(args) - 2: 0}
     scratch = [
-        pltpu.VMEM((r_dev * rows, samples), BF16),
+        pltpu.VMEM((r_dev * rows, samples + 2 * margin_of(lag_dev)), BF16),
         pltpu.VMEM((2 * slots, lag_dev), BF16),
         pltpu.VMEM((cap, lag_dev), F32),
         pltpu.VMEM(pick.shape[1:], BF16),
@@ -510,7 +504,7 @@
         scratch.append(pltpu.VMEM((r_dev, LANES, width), BF16))
         scratch.append(pltpu.VMEM((SHIFT_ROWS, n_win * samples + LAGS), F32))
     body = functools.partial(
-        correlate_kernel, blocks, parts, v, tile, norming, prebuilt, before is None, last
+        correlate_kernel, block, len(pieces), v, tile, norming, prebuilt, before is None, last
     )
     return pl.pallas_call(
         body,
@@ -601,20 +595,26 @@
     for step in range(3, n_chan):
         relay(step)
     near_spans = spans(near)
-    if prebuilt:
-        signals, near_spans = after_arrival(n_chan - 1, (signals, near_spans))
+    calls = [(v, q) for v in range(n_win) for q in range(2)]
+    calls = calls[:2] + [(v, q) for q in range(2) for v in range(1, n_win)]
+
+    def add(call, span, result):
+        v, q = call
+        return correlate(
+            q, halves(span), signals[v], prebuilt, numbers, v, matrices, result, call == calls[-1], tile, norming, lag_dev,
+            n_win, r_dev,
+        )
+
+    result = add(calls[0], near, None)
+    near_spans = after_arrival(n_chan - 1, near_spans)
+    for there in arrived:
+        there[n_chan - 1] = lax.optimization_barrier((result, signals, there[n_chan - 1]))[2]
     far_spans = spans(choose(numbers, 3, arrived, sorted(arrived[0])))
-
-    calls = [(0, (0, 1))] + [(v, (q,)) for q in range(2) for v in range(1, n_win)]
-    result = None
-    for v, blocks in calls:
-        if blocks == (1,):
+    result = add(calls[1], far_spans[0], result)
+    for call in calls[2:]:
+        if call == (1, 1):
             far_spans, result = lax.optimization_barrier((far_spans, result))
-        pieces = [half for q in blocks for half in halves((near_spans, far_spans)[q][v])]
-        result = correlate(
-            blocks, pieces, signals[v], prebuilt, numbers, v, matrices, result, (v, blocks) == calls[-1], tile, norming,
-            lag_dev, n_win, r_dev,
-        )
+        result = add(call, (near_spans, far_spans)[call[1]][call[0]], result)
     return result[None, None]
 
 

time: 85 us -> 79.9 us (0.940)
  starting transfers between devices: 23.5 us -> 21.2 us
  waiting for transfers between devices: 9.22 us -> 7.37 us
  Pallas kernels: 51.8 us -> 50.9 us
    ppermute x5, starting transfers between devices: 10.9 us -> 9.62 us  [swapped(): return lax.ppermute(block, axis, route)]
    pallas_call x3 -> x4, Pallas kernels: 28.9 us -> 27.8 us  [correlate(): pl.pallas_call(body, grid_spec=pltpu.PrefetchScalarGridSpec(num_scalar_pr...]
    ppermute x10, starting transfers between devices: 12.6 us -> 11.5 us  [turned(): lax.ppermute(block, axis, [(i, (i + distance) % size) for i in range(size)])]
    ppermute x10, waiting for transfers between devices: 6.38 us -> 5.37 us  [turned(): lax.ppermute(block, axis, [(i, (i + distance) % size) for i in range(size)])]
  transfers between devices with their start and end apart: 15 -> 15, of which waited for: 4 -> 6; matrix products, arithmetic and copies ran while one was open for 0% -> 0% of each run, Pallas kernels for 46% -> 50%
where the time goes in v8:
time: 79.9 us; the launch traced here: 79.7 us
  Pallas kernels  50.9 us (64%)
  starting transfers between devices  21.2 us (27%)
  waiting for transfers between devices  7.37 us (9%)
    pallas_call x4, Pallas kernels, correlate(): pl.pallas_call(body, grid_spec=pltpu.PrefetchScalarGridSpec(num_scalar_pr...  27.8 us
    pallas_call x4, Pallas kernels, build_hankel(): pl.pallas_call(functools.partial(hankel_kernel, v, n_win, samples, done),...  13.7 us
    ppermute x10, starting transfers between devices, turned(): lax.ppermute(block, axis, [(i, (i + distance) % size) for i in range(size)])  11.5 us
    ppermute x5, starting transfers between devices, swapped(): return lax.ppermute(block, axis, route)  9.62 us
    ppermute x10, waiting for transfers between devices, turned(): lax.ppermute(block, axis, [(i, (i + distance) % size) for i in range(size)])  5.37 us
    pallas_call x2, Pallas kernels, index(): pl.pallas_call(functools.partial(index_kernel, r_dev, lists_at, cap, tile...  5.29 us
    ppermute x5, waiting for transfers between devices, swapped(): return lax.ppermute(block, axis, route)  2 us
    pallas_call x2, Pallas kernels, choose(): pl.pallas_call(functools.partial(choose_kernel, which, offsets), in_specs...  1.63 us
  transfers between devices with their start and end apart: 15, of which 6 were waited for; matrix products, arithmetic and copies ran while one was open for 0% of the time, Pallas kernels for 50%

profile of v8, /device:TPU:0, one launch (start us, length us, event | category | flops | bytes accessed | tf_op | source)
XLA Modules:
  0.0 79.7 jit_solution(17612225427926060970)
XLA Ops:
  0.0 1.0 %own_rows.1.refs_2_ = bf16[128,2048]{1,0:T(8,128)(2,1)S(1)} custom-call(bf16[256,2048]{1,0:T(8,128)(2,1)} %bitcast.4), custom_call_target="tpu_custom_call" | custom-call | tf_op jit(solution)/shard_map/own_rows/pallas_call | solution.py:128
  1.1 3.1 %collective-permute-start.4 = (bf16[128,2048]{1,0:T(8,128)(2,1)S(1)}, bf16[128,2048]{1,0:T(8,128)(2,1)S(1)}, u32[]{:S(2)}, u32[]{:S(2)}) collective-permute-start(bf16[128,2048]{1,0:T(8,128)(2,1)S(1)} %own_rows.1.refs_2_), channel_id=1, source_target_pairs={{0,4},{4,0},{8,12},{12,8},{1,5},{5,1},{9,13},{13,9},{2,6},{6,2},{1... | collective-permute-start | bytes 1572872 | tf_op jit(solution)/shard_map/ppermute | solution.py:29
  4.8 1.6 %collective-permute-start = (bf16[4,2048]{1,0:T(4,128)(2,1)}, bf16[4,2048]{1,0:T(4,128)(2,1)S(1)}, u32[]{:S(2)}, u32[]{:S(2)}) collective-permute-start(bf16[4,2048]{1,0:T(4,128)(2,1)} %refs_0_.1), channel_id=1, source_target_pairs={{0,2},{2,0},{1,3},{3,1},{4,6},{6,4},{5,7},{7,5},{8,10},{10,8},{9,1... | collective-permute-start | bytes 49160 | tf_op jit(solution)/shard_map/ppermute | solution.py:34
  6.4 2.5 %collective-permute-done.refs_1_ = bf16[4,2048]{1,0:T(4,128)(2,1)S(1)} collective-permute-done((bf16[4,2048]{1,0:T(4,128)(2,1)}, bf16[4,2048]{1,0:T(4,128)(2,1)S(1)}, u32[]{:S(2)}, u32[]{:S(2)}) %collective-permute-start) | collective-permute-done | bytes 16416 | tf_op jit(solution)/shard_map/ppermute | solution.py:34
  8.9 1.4 %pack.1 = (bf16[4,4352]{1,0:T(4,128)(2,1)S(1)}, bf16[4,4352]{1,0:T(4,128)(2,1)S(1)}, bf16[4,4352]{1,0:T(4,128)(2,1)S(1)}, bf16[4,4352]{1,0:T(4,128)(2,1)S(1)}, s32[7]{0:T(128)S(1)}) custom-call(s32[1,2]{1,0:T(1,128)} %plan_hbm.1, s32[4,512]{1,0:T(4,128)} %bitcast.5, s32[4,512]{1,0:T(4,128)} %bitcast.6, bf16[4,2048]{1,0:T(4,128)(2,1)} %refs_0_.1, ...), custom_call_target="tpu_custom_call" | custom-call | tf_op jit(solution)/shard_map/pack/pallas_call | solution.py:94
  10.3 4.4 %collective-permute-start.1 = (bf16[4,4352]{1,0:T(4,128)(2,1)S(1)}, bf16[4,4352]{1,0:T(4,128)(2,1)S(1)}, u32[]{:S(2)}, u32[]{:S(2)}) collective-permute-start(bf16[4,4352]{1,0:T(4,128)(2,1)S(1)} %get-tuple-element.54), channel_id=1, source_target_pairs={{0,4},{4,8},{8,12},{12,0},{1,5},{5,9},{9,13},{13,1},{2,6},{6,10},{... | collective-permute-start | bytes 104456 | tf_op jit(solution)/shard_map/ppermute | solution.py:34
  14.7 2.4 %collective-permute-start.3 = (bf16[4,4352]{1,0:T(4,128)(2,1)S(1)}, bf16[4,4352]{1,0:T(4,128)(2,1)S(1)}, u32[]{:S(2)}, u32[]{:S(2)}) collective-permute-start(bf16[4,4352]{1,0:T(4,128)(2,1)S(1)} %get-tuple-element.56), channel_id=1, source_target_pairs={{0,12},{4,0},{8,4},{12,8},{1,13},{5,1},{9,5},{13,9},{2,14},{6,2},{... | collective-permute-start | bytes 104456 | tf_op jit(solution)/shard_map/ppermute | solution.py:34
  17.1 2.0 %index.2 = (bf16[4,640,256]{2,1,0:T(8,128)(2,1)S(1)}, bf16[4,512,512]{2,1,0:T(8,128)(2,1)S(1)}, s32[4]{0:T(128)S(1)}, s32[16]{0:T(128)S(1)}, bf16[4,4,640,256]{3...) custom-call(s32[7]{0:T(128)S(1)} %get-tuple-element.53.number_ref, bf16[4,4352]{1,0:T(4,128)(2,1)S(1)} %get-tuple-element.57.refs_0_), custom_call_target="tpu_custom_call" | custom-call | tf_op jit(solution)/shard_map/index/pallas_call | solution.py:268
  19.2 1.9 %hankel.5.refs_3_ = bf16[16,128,2432]{2,1,0:T(8,128)(2,1)S(1)} custom-call(s32[7]{0:T(128)S(1)} %get-tuple-element.53.number_ref, bf16[4,4352]{1,0:T(4,128)(2,1)S(1)} %get-tuple-element.57.refs_0_), custom_call_target="tpu_custom_call" | custom-call | flops 1245184 | bytes 2490368 | tf_op jit(solution)/shard_map/hankel/pallas_call | solution.py:335
  21.1 1.9 %hankel.4.refs_3_ = bf16[16,128,2432]{2,1,0:T(8,128)(2,1)S(1)} custom-call(s32[7]{0:T(128)S(1)} %get-tuple-element.53.number_ref, bf16[4,4352]{1,0:T(4,128)(2,1)S(1)} %get-tuple-element.57.refs_0_), custom_call_target="tpu_custom_call" | custom-call | flops 1245184 | bytes 2490368 | tf_op jit(solution)/shard_map/hankel/pallas_call | solution.py:335
  23.8 3.3 %collective-permute-start.7 = (bf16[128,2048]{1,0:T(8,128)(2,1)S(1)}, bf16[128,2048]{1,0:T(8,128)(2,1)S(1)}, u32[]{:S(2)}, u32[]{:S(2)}) collective-permute-start(bf16[128,2048]{1,0:T(8,128)(2,1)S(1)} %collective-permute-done.5.refs_1_), channel_id=1, source_target_pairs={{0,4},{4,0},{8,12},{12,8},{1,5},{5,1},{9,13},{13,9},{2,6},{6,2},{1... | collective-permute-start | bytes 1572872 | tf_op jit(solution)/shard_map/ppermute | solution.py:29
  27.2 3.2 %index.3 = (bf16[4,640,256]{2,1,0:T(8,128)(2,1)S(1)}, bf16[4,512,512]{2,1,0:T(8,128)(2,1)S(1)}, s32[4]{0:T(128)S(1)}, s32[16]{0:T(128)S(1)}, bf16[4,4,640,256]{3...) custom-call(s32[7]{0:T(128)S(1)} %get-tuple-element.53.number_ref, ...), custom_call_target="tpu_custom_call", output_to_operand_aliasing={{0}: (4, {}), {1}: (5, {}), {4}: (8, {}), {5}: (9, {})} | custom-call | tf_op jit(solution)/shard_map/index/pallas_call | solution.py:268
  30.4 4.9 %hankel.6.refs_2_ = bf16[16,128,2432]{2,1,0:T(8,128)(2,1)S(1)} custom-call(s32[7]{0:T(128)S(1)} %get-tuple-element.53.number_ref, bf16[4,4352]{1,0:T(4,128)(2,1)S(1)} %collective-permute-done.1.refs_0_, bf16[4,4352]{1,0:T(4,128)(2,1)S(1)} %collective-permute-done.2.refs_1_, ...), custom_call_target="tpu_custom_call", output_to_operand_aliasing={{}: (4, {})} | custom-call | flops 3735552 | bytes 7471104 | tf_op jit(solution)/shard_map/hankel/pallas_call | solution.py:335
  35.4 1.9 %collective-permute-done.7.refs_4_ = bf16[128,2048]{1,0:T(8,128)(2,1)S(1)} collective-permute-done((bf16[128,2048]{1,0:T(8,128)(2,1)S(1)}, bf16[128,2048]{1,0:T(8,128)(2,1)S(1)}, u32[]{:S(2)}, u32[]{:S(2)}) %collective-permute-start.7) | collective-permute-done | bytes 524320 | tf_op jit(solution)/shard_map/ppermute | solution.py:29
  38.1 1.8 %collective-permute-start.9 = (bf16[128,2048]{1,0:T(8,128)(2,1)S(1)}, bf16[128,2048]{1,0:T(8,128)(2,1)S(1)}, u32[]{:S(2)}, u32[]{:S(2)}) collective-permute-start(bf16[128,2048]{1,0:T(8,128)(2,1)S(1)} %collective-permute-done.6.refs_0_), channel_id=1, source_target_pairs={{0,4},{4,0},{8,12},{12,8},{1,5},{5,1},{9,13},{13,9},{2,6},{6,2},{1... | collective-permute-start | bytes 1572872 | tf_op jit(solution)/shard_map/ppermute | solution.py:29
  39.9 1.5 %collective-permute-start.11 = (bf16[128,2048]{1,0:T(8,128)(2,1)S(1)}, bf16[128,2048]{1,0:T(8,128)(2,1)S(1)}, u32[]{:S(2)}, u32[]{:S(2)}) collective-permute-start(bf16[128,2048]{1,0:T(8,128)(2,1)S(1)} %choose.2.refs_0_), channel_id=1, source_target_pairs={{0,2},{2,0},{1,3},{3,1},{4,6},{6,4},{5,7},{7,5},{8,10},{10,8},{9,1... | collective-permute-start | bytes 1572872 | tf_op jit(solution)/shard_map/ppermute | solution.py:34
  41.4 4.9 %hankel.7.refs_2_ = bf16[16,128,2432]{2,1,0:T(8,128)(2,1)S(1)} custom-call(s32[7]{0:T(128)S(1)} %get-tuple-element.53.number_ref, bf16[4,4352]{1,0:T(4,128)(2,1)S(1)} %collective-permute-done.1.refs_0_, bf16[4,4352]{1,0:T(4,128)(2,1)S(1)} %collective-permute-done.2.refs_1_, ...), custom_call_target="tpu_custom_call", output_to_operand_aliasing={{}: (4, {})} | custom-call | flops 3735552 | bytes 7471104 | tf_op jit(solution)/shard_map/hankel/pallas_call | solution.py:335
  46.4 6.0 %correlate.4 = (f32[4,512,512]{2,1,0:T(8,128)S(1)}, f32[4,512,512]{2,1,0:T(8,128)}) custom-call(s32[4]{0:T(128)S(1)} %get-tuple-element.72.pass_ref, s32[16]{0:T(128)S(1)} %get-tuple-element.73.count_ref, s32[7]{0:T(128)S(1)} %get-tuple-element.53.number_ref, bf16[128,2048]{1,0:T(8,128)(2,1)S(1)} %choose.2.refs_0_, ...), custom_call_target="tpu_custom_call" | custom-call | flops 4026531840 | bytes 8388608 | tf_op jit(solution)/shard_map/correlate/pallas_call | solution.py:509
  52.5 0.8 %choose.3.refs_0_ = bf16[128,2048]{1,0:T(8,128)(2,1)S(1)} custom-call(s32[7]{0:T(128)S(1)} %get-tuple-element.53.number_ref, bf16[128,2048]{1,0:T(8,128)(2,1)S(1)} %collective-permute-done.6.refs_0_, bf16[128,2048]{1,0:T(8,128)(2,1)S(1)} %collective-permute-done.5.refs_1_, bf16[128,2048]{1,0:T(8,128)(2,1)S(1)} %own_rows.1.refs_2_, ...), custom_call_target="tpu_custom_call" | custom-call | tf_op jit(solution)/shard_map/choose/pallas_call | solution.py:162
  53.9 1.5 %collective-permute-start.10 = (bf16[128,2048]{1,0:T(8,128)(2,1)S(1)}, bf16[128,2048]{1,0:T(8,128)(2,1)S(1)}, u32[]{:S(2)}, u32[]{:S(2)}) collective-permute-start(bf16[128,2048]{1,0:T(8,128)(2,1)S(1)} %choose.3.refs_0_), channel_id=1, source_target_pairs={{0,2},{2,0},{1,3},{3,1},{4,6},{6,4},{5,7},{7,5},{8,10},{10,8},{9,1... | collective-permute-start | bytes 1572872 | tf_op jit(solution)/shard_map/ppermute | solution.py:34
  55.4 6.2 %correlate.5 = (f32[4,512,512]{2,1,0:T(8,128)S(1)}, f32[4,512,512]{2,1,0:T(8,128)}) custom-call(s32[4]{0:T(128)S(1)} %get-tuple-element.72.pass_ref, s32[16]{0:T(128)S(1)} %get-tuple-element.73.count_ref, s32[7]{0:T(128)S(1)} %get-tuple-element.53.number_ref, bf16[128,2048]{1,0:T(8,128)(2,1)S(1)} %choose.3.refs_0_, ...), custom_call_target="tpu_custom_call", output_to_operand_aliasing={{0}: (10, {})} | custom-call | flops 4026531840 | bytes 8388608 | tf_op jit(solution)/shard_map/correlate/pallas_call | solution.py:509
  61.6 6.2 %correlate.6 = (f32[4,512,512]{2,1,0:T(8,128)S(1)}, f32[4,512,512]{2,1,0:T(8,128)}) custom-call(s32[4]{0:T(128)S(1)} %get-tuple-element.72.pass_ref, s32[16]{0:T(128)S(1)} %get-tuple-element.73.count_ref, s32[7]{0:T(128)S(1)} %get-tuple-element.53.number_ref, ...), custom_call_target="tpu_custom_call", output_to_operand_aliasing={{0}: (10, {})} | custom-call | flops 4026531840 | bytes 8388608 | tf_op jit(solution)/shard_map/correlate/pallas_call | solution.py:509
  68.3 1.9 %collective-permute-done.14.refs_1_ = bf16[128,2048]{1,0:T(8,128)(2,1)S(1)} collective-permute-done((bf16[128,2048]{1,0:T(8,128)(2,1)S(1)}, bf16[128,2048]{1,0:T(8,128)(2,1)S(1)}, u32[]{:S(2)}, u32[]{:S(2)}) %collective-permute-start.14) | collective-permute-done | bytes 524320 | tf_op jit(solution)/shard_map/ppermute | solution.py:34
  70.2 9.5 %correlate.7 = f32[4,512,512]{2,1,0:T(8,128)} custom-call(s32[4]{0:T(128)S(1)} %get-tuple-element.72.pass_ref, s32[16]{0:T(128)S(1)} %get-tuple-element.73.count_ref, s32[7]{0:T(128)S(1)} %get-tuple-element.53.number_ref, bf16[128,2048]{1,0:T(8,128)(2,1)S(1)} %collective-permute-done.10.refs_0_, bf16[128,2048]{1,0:T(8,128)(2,1)S(1)} %collective-permute-done.14.refs_1_, ...), custom_call_target="tpu_custom_call" | custom-call | flops 4026531840 | bytes 8388608 | tf_op jit(solution)/shard_map/correlate/pallas_call | solution.py:509
  (20 shorter events, 3.4 us)
Async XLA Ops:
  1.1 22.1 %collective-permute-start.4 = (bf16[128,2048]{1,0:T(8,128)(2,1)S(1)}, bf16[128,2048]{1,0:T(8,128)(2,1)S(1)}, u32[]{:S(2)}, u32[]{:S(2)}) collective-permute-start(bf16[128,2048]{1,0:T(8,128)(2,1)S(1)} %own_rows.1.refs_2_), channel_id=1, source_target_pairs={{0,4},{4,0},{8,12},{12,8},{1,5},{5,1},{9,13},{13,9},{2,6},{6,2},{1... | collective-permute-start | bytes 1572872 | tf_op jit(solution)/shard_map/ppermute | solution.py:29
  4.1 19.7 %collective-permute-start.5 = (bf16[128,2048]{1,0:T(8,128)(2,1)S(1)}, bf16[128,2048]{1,0:T(8,128)(2,1)S(1)}, u32[]{:S(2)}, u32[]{:S(2)}) collective-permute-start(bf16[128,2048]{1,0:T(8,128)(2,1)S(1)} %own_rows.1.refs_2_), channel_id=1, source_target_pairs={{4,8},{8,4},{5,9},{9,5},{6,10},{10,6},{7,11},{11,7},{20,24},{24,20... | collective-permute-start | bytes 1572872 | tf_op jit(solution)/shard_map/ppermute | solution.py:29
  4.8 4.0 %collective-permute-start = (bf16[4,2048]{1,0:T(4,128)(2,1)}, bf16[4,2048]{1,0:T(4,128)(2,1)S(1)}, u32[]{:S(2)}, u32[]{:S(2)}) collective-permute-start(bf16[4,2048]{1,0:T(4,128)(2,1)} %refs_0_.1), channel_id=1, source_target_pairs={{0,2},{2,0},{1,3},{3,1},{4,6},{6,4},{5,7},{7,5},{8,10},{10,8},{9,1... | collective-permute-start | bytes 49160 | tf_op jit(solution)/shard_map/ppermute | solution.py:34
  10.3 12.8 %collective-permute-start.1 = (bf16[4,4352]{1,0:T(4,128)(2,1)S(1)}, bf16[4,4352]{1,0:T(4,128)(2,1)S(1)}, u32[]{:S(2)}, u32[]{:S(2)}) collective-permute-start(bf16[4,4352]{1,0:T(4,128)(2,1)S(1)} %get-tuple-element.54), channel_id=1, source_target_pairs={{0,4},{4,8},{8,12},{12,0},{1,5},{5,9},{9,13},{13,1},{2,6},{6,10},{... | collective-permute-start | bytes 104456 | tf_op jit(solution)/shard_map/ppermute | solution.py:34
  14.7 8.4 %collective-permute-start.2 = (bf16[4,4352]{1,0:T(4,128)(2,1)S(1)}, bf16[4,4352]{1,0:T(4,128)(2,1)S(1)}, u32[]{:S(2)}, u32[]{:S(2)}) collective-permute-start(bf16[4,4352]{1,0:T(4,128)(2,1)S(1)} %get-tuple-element.55), channel_id=1, source_target_pairs={{0,8},{4,12},{8,0},{12,4},{1,9},{5,13},{9,1},{13,5},{2,10},{6,14},... | collective-permute-start | bytes 104456 | tf_op jit(solution)/shard_map/ppermute | solution.py:34
  14.7 8.4 %collective-permute-start.3 = (bf16[4,4352]{1,0:T(4,128)(2,1)S(1)}, bf16[4,4352]{1,0:T(4,128)(2,1)S(1)}, u32[]{:S(2)}, u32[]{:S(2)}) collective-permute-start(bf16[4,4352]{1,0:T(4,128)(2,1)S(1)} %get-tuple-element.56), channel_id=1, source_target_pairs={{0,12},{4,0},{8,4},{12,8},{1,13},{5,1},{9,5},{13,9},{2,14},{6,2},{... | collective-permute-start | bytes 104456 | tf_op jit(solution)/shard_map/ppermute | solution.py:34
  23.1 12.3 %collective-permute-start.6 = (bf16[128,2048]{1,0:T(8,128)(2,1)S(1)}, bf16[128,2048]{1,0:T(8,128)(2,1)S(1)}, u32[]{:S(2)}, u32[]{:S(2)}) collective-permute-start(bf16[128,2048]{1,0:T(8,128)(2,1)S(1)} %collective-permute-done.4.refs_3_), channel_id=1, source_target_pairs={{4,8},{8,4},{5,9},{9,5},{6,10},{10,6},{7,11},{11,7},{20,24},{24,20... | collective-permute-start | bytes 1572872 | tf_op jit(solution)/shard_map/ppermute | solution.py:29
  23.8 13.4 %collective-permute-start.7 = (bf16[128,2048]{1,0:T(8,128)(2,1)S(1)}, bf16[128,2048]{1,0:T(8,128)(2,1)S(1)}, u32[]{:S(2)}, u32[]{:S(2)}) collective-permute-start(bf16[128,2048]{1,0:T(8,128)(2,1)S(1)} %collective-permute-done.5.refs_1_), channel_id=1, source_target_pairs={{0,4},{4,0},{8,12},{12,8},{1,5},{5,1},{9,13},{13,9},{2,6},{6,2},{1... | collective-permute-start | bytes 1572872 | tf_op jit(solution)/shard_map/ppermute | solution.py:29
  38.1 8.3 %collective-permute-start.8 = (bf16[128,2048]{1,0:T(8,128)(2,1)S(1)}, bf16[128,2048]{1,0:T(8,128)(2,1)S(1)}, u32[]{:S(2)}, u32[]{:S(2)}) collective-permute-start(bf16[128,2048]{1,0:T(8,128)(2,1)S(1)} %choose.2.refs_0_), channel_id=1, source_target_pairs={{0,1},{1,0},{2,3},{3,2},{4,5},{5,4},{6,7},{7,6},{8,9},{9,8},{10,11... | collective-permute-start | bytes 1572872 | tf_op jit(solution)/shard_map/ppermute | solution.py:34
  38.1 14.3 %collective-permute-start.9 = (bf16[128,2048]{1,0:T(8,128)(2,1)S(1)}, bf16[128,2048]{1,0:T(8,128)(2,1)S(1)}, u32[]{:S(2)}, u32[]{:S(2)}) collective-permute-start(bf16[128,2048]{1,0:T(8,128)(2,1)S(1)} %collective-permute-done.6.refs_0_), channel_id=1, source_target_pairs={{0,4},{4,0},{8,12},{12,8},{1,5},{5,1},{9,13},{13,9},{2,6},{6,2},{1... | collective-permute-start | bytes 1572872 | tf_op jit(solution)/shard_map/ppermute | solution.py:29
  39.9 14.0 %collective-permute-start.11 = (bf16[128,2048]{1,0:T(8,128)(2,1)S(1)}, bf16[128,2048]{1,0:T(8,128)(2,1)S(1)}, u32[]{:S(2)}, u32[]{:S(2)}) collective-permute-start(bf16[128,2048]{1,0:T(8,128)(2,1)S(1)} %choose.2.refs_0_), channel_id=1, source_target_pairs={{0,2},{2,0},{1,3},{3,1},{4,6},{6,4},{5,7},{7,5},{8,10},{10,8},{9,1... | collective-permute-start | bytes 1572872 | tf_op jit(solution)/shard_map/ppermute | solution.py:34
  53.3 2.1 %collective-permute-start.13 = (bf16[128,2048]{1,0:T(8,128)(2,1)S(1)}, bf16[128,2048]{1,0:T(8,128)(2,1)S(1)}, u32[]{:S(2)}, u32[]{:S(2)}) collective-permute-start(bf16[128,2048]{1,0:T(8,128)(2,1)S(1)} %choose.3.refs_0_), channel_id=1, source_target_pairs={{0,1},{1,0},{2,3},{3,2},{4,5},{5,4},{6,7},{7,6},{8,9},{9,8},{10,11... | collective-permute-start | bytes 1572872 | tf_op jit(solution)/shard_map/ppermute | solution.py:34
  53.9 7.7 %collective-permute-start.12 = (bf16[128,2048]{1,0:T(8,128)(2,1)S(1)}, bf16[128,2048]{1,0:T(8,128)(2,1)S(1)}, u32[]{:S(2)}, u32[]{:S(2)}) collective-permute-start(bf16[128,2048]{1,0:T(8,128)(2,1)S(1)} %collective-permute-done.11.refs_0_), channel_id=1, source_target_pairs={{0,1},{1,0},{2,3},{3,2},{4,5},{5,4},{6,7},{7,6},{8,9},{9,8},{10,11... | collective-permute-start | bytes 1572872 | tf_op jit(solution)/shard_map/ppermute | solution.py:34
  53.9 14.3 %collective-permute-start.10 = (bf16[128,2048]{1,0:T(8,128)(2,1)S(1)}, bf16[128,2048]{1,0:T(8,128)(2,1)S(1)}, u32[]{:S(2)}, u32[]{:S(2)}) collective-permute-start(bf16[128,2048]{1,0:T(8,128)(2,1)S(1)} %choose.3.refs_0_), channel_id=1, source_target_pairs={{0,2},{2,0},{1,3},{3,1},{4,6},{6,4},{5,7},{7,5},{8,10},{10,8},{9,1... | collective-permute-start | bytes 1572872 | tf_op jit(solution)/shard_map/ppermute | solution.py:34
  68.3 1.9 %collective-permute-start.14 = (bf16[128,2048]{1,0:T(8,128)(2,1)S(1)}, bf16[128,2048]{1,0:T(8,128)(2,1)S(1)}, u32[]{:S(2)}, u32[]{:S(2)}) collective-permute-start(bf16[128,2048]{1,0:T(8,128)(2,1)S(1)} %collective-permute-done.10.refs_0_), channel_id=1, source_target_pairs={{0,1},{1,0},{2,3},{3,2},{4,5},{5,4},{6,7},{7,6},{8,9},{9,8},{10,11... | collective-permute-start | bytes 1572872 | tf_op jit(solution)/shard_map/ppermute | solution.py:34

commit v9 on v8

--- a/solution.py
+++ b/solution.py
@@ -42,17 +42,16 @@
     return pltpu.CompilerParams(vmem_limit_bytes=vmem)
 
 
-def pack_kernel(halves, lags, block_rows, n_win, plan_hbm, pair_hbm, keep_hbm, *refs):
-    span_hbms, refs = refs[:n_win], refs[n_win:]
-    plan_ref, pair_ref, keep_ref, span_refs, digit_ref, sems = refs[-6:]
+def pack_kernel(halves, lags, block_rows, plan_hbm, pair_hbm, keep_hbm, receiver_hbm, *refs):
+    plan_ref, pair_ref, keep_ref, receiver_ref, digit_ref, sems = refs[-6:]
     parcel_refs, number_ref = refs[:-7], refs[-7]
     small = []
     moves = [(plan_hbm, plan_ref), (pair_hbm, pair_ref), (keep_hbm, keep_ref)]
-    moves += [(span, span_refs.at[v]) for v, span in enumerate(span_hbms)]
+    moves.append((receiver_hbm, receiver_ref))
     for place, (source, target) in enumerate(moves):
         small.append(pltpu.make_async_copy(source, target, sems.at[place]))
         small[-1].start()
-    r_dev, samples = span_refs.shape[1:]
+    r_dev, samples = receiver_ref.shape
     n_chan, cap = pair_ref.shape
     chan, win, rep = lax.axis_index("chan"), lax.axis_index("win"), lax.axis_index("rep")
     for copy in small:
@@ -60,13 +59,13 @@
 
     packed = pair_ref[...] * 2 + keep_ref[...]
     digit_ref[:n_chan, :] = jnp.concatenate([packed // DIGIT, packed % DIGIT], axis=1).astype(F32)
-    heard = [span_refs[v].astype(F32) for v in range(n_win)]
+    heard = receiver_ref[...].astype(F32)
     part = 2 * cap // r_dev
-    spare = parcel_refs[0].shape[1] - n_win * samples - part
+    spare = parcel_refs[0].shape[1] - samples - part
     for distance, parcel_ref in enumerate(parcel_refs):
         digits = digit_ref[pl.ds(lax.rem(chan + distance, n_chan), 1), :]
         lists = [digits[:, i * part : (i + 1) * part] for i in range(r_dev)]
-        parcel = heard + [jnp.concatenate(lists, axis=0)]
+        parcel = [heard, jnp.concatenate(lists, axis=0)]
         if spare:
             parcel.append(jnp.zeros((r_dev, spare), F32))
         parcel_ref[...] = jnp.concatenate(parcel, axis=1).astype(BF16)
@@ -83,31 +82,48 @@
     number_ref[6] = win
 
 
-def pack(plan, spans, pair_index, keep, halves, lags, block_rows, n_chan):
-    n_win = len(spans)
-    r_dev, samples = spans[0].shape
+def pack(plan, receivers, pair_index, keep, halves, lags, block_rows, n_chan):
+    r_dev, samples = receivers.shape
     cap = pair_index.shape[1]
     beside = -(-2 * cap // r_dev // LANES) * LANES
     vmem, smem = pl.BlockSpec(memory_space=pltpu.VMEM), pl.BlockSpec(memory_space=pltpu.SMEM)
-    shapes = [jax.ShapeDtypeStruct((r_dev, n_win * samples + beside), BF16)] * n_chan
+    shapes = [jax.ShapeDtypeStruct((r_dev, samples + beside), BF16)] * n_chan
     shapes.append(jax.ShapeDtypeStruct((7,), jnp.int32))
     *parcels, numbers = pl.pallas_call(
-        functools.partial(pack_kernel, halves, lags, block_rows, n_win),
-        in_specs=[pl.BlockSpec(memory_space=pl.ANY)] * (3 + n_win),
+        functools.partial(pack_kernel, halves, lags, block_rows),
+        in_specs=[pl.BlockSpec(memory_space=pl.ANY)] * 4,
         out_specs=[vmem] * n_chan + [smem],
         out_shape=shapes,
         scratch_shapes=[
             pltpu.SMEM(plan.shape, plan.dtype),
             pltpu.VMEM(pair_index.shape, pair_index.dtype),
             pltpu.VMEM(keep.shape, keep.dtype),
-            pltpu.VMEM((n_win, r_dev, samples), BF16),
+            pltpu.VMEM(receivers.shape, receivers.dtype),
             pltpu.VMEM((-(-n_chan // SHIFT_ROWS) * SHIFT_ROWS, 2 * cap), F32),
-            pltpu.SemaphoreType.DMA((3 + n_win,)),
+            pltpu.SemaphoreType.DMA((4,)),
         ],
         compiler_params=params(VMEM_BYTES // 2),
         name="pack",
-    )(*[in_hbm(a) for a in (plan, pair_index, keep, spans[0])], *spans[1:])
+    )(*[in_hbm(a) for a in (plan, pair_index, keep, receivers)])
     return parcels, numbers
+
+
+def join_kernel(*refs):
+    out_ref = refs[-1]
+    samples = out_ref.shape[1]
+    out_ref[...] = jnp.concatenate([ref[:, :samples].astype(F32) for ref in refs[:-1]], axis=0).astype(BF16)
+
+
+def join(parcels, samples):
+    vmem = pl.BlockSpec(memory_space=pltpu.VMEM)
+    return pl.pallas_call(
+        join_kernel,
+        in_specs=[vmem] * len(parcels),
+        out_specs=vmem,
+        out_shape=jax.ShapeDtypeStruct((len(parcels) * parcels[0].shape[0], samples), BF16),
+        compiler_params=params(VMEM_BYTES // 4),
+        name="join",
+    )(*parcels)
 
 
 def own_kernel(source_ref, *refs):
@@ -178,15 +194,9 @@
     return jnp.where(condition, 1.0, 0.0).astype(BF16)
 
 
-def index_kernel(r_dev, lists_at, cap, tile, block_rows, done, number_ref, *refs):
+def index_kernel(r_dev, lists_at, cap, tile, block_rows, number_ref, *refs):
     pick_ref, place_ref, pass_ref, count_ref, more_pick_ref, more_place_ref, pick_scratch, place_scratch = refs[-8:]
     parcel_refs = refs[:-8]
-    if done:
-        parcel_refs, (_, _, earlier_pass_ref, earlier_count_ref, _, _) = parcel_refs[:-6], parcel_refs[-6:]
-        for group in range(done):
-            pass_ref[group] = earlier_pass_ref[group]
-            for r in range(r_dev):
-                count_ref[group * r_dev + r] = earlier_count_ref[group * r_dev + r]
     nearer, offset = number_ref[0], number_ref[1]
     slots = 2 * r_dev * tile
     window = tile + SPARE
@@ -194,7 +204,7 @@
     below = lax.broadcasted_iota(jnp.int32, (cap, cap), 0) < lax.broadcasted_iota(jnp.int32, (cap, cap), 1)
     below = ones_where(below)
     later = []
-    for group, parcel_ref in enumerate(parcel_refs, done):
+    for group, parcel_ref in enumerate(parcel_refs):
         digits = parcel_ref[:, lists_at:].astype(F32)
         digits = jnp.concatenate([digits[i : i + 1, :part] for i in range(r_dev)], axis=1).astype(jnp.int32)
         packed = digits[:, :cap] * DIGIT + digits[:, cap:]
@@ -252,23 +262,17 @@
             lax.fori_loop(1, passes, one_pass, 0)
 
 
-def index(parcels, numbers, earlier, groups, lists_at, r_dev, cap, tile, block_rows):
+def index(parcels, numbers, lists_at, r_dev, cap, tile, block_rows):
+    groups = len(parcels)
     slots = 2 * r_dev * tile
     lines = 2 * r_dev * (tile + SPARE)
     more = -(-(min(block_rows, cap) - (tile - SPARE)) // tile)
     vmem, smem = pl.BlockSpec(memory_space=pltpu.VMEM), pl.BlockSpec(memory_space=pltpu.SMEM)
     any_spec = pl.BlockSpec(memory_space=pl.ANY)
-    specs = [vmem, vmem, smem, smem, any_spec, any_spec]
-    args = list(parcels)
-    done, aliases = 0, {}
-    if earlier is not None:
-        done = groups - len(parcels)
-        aliases = {1 + len(parcels) + place: place for place in (0, 1, 4, 5)}
-        args += list(earlier[:4]) + [in_hbm(array) for array in earlier[4:]]
     return pl.pallas_call(
-        functools.partial(index_kernel, r_dev, lists_at, cap, tile, block_rows, done),
-        in_specs=[smem] + [vmem] * len(parcels) + (specs if done else []),
-        out_specs=specs,
+        functools.partial(index_kernel, r_dev, lists_at, cap, tile, block_rows),
+        in_specs=[smem] + [vmem] * groups,
+        out_specs=[vmem, vmem, smem, smem, any_spec, any_spec],
         out_shape=[
             jax.ShapeDtypeStruct((groups, lines, block_rows), BF16),
             jax.ShapeDtypeStruct((groups, cap, slots), BF16),
@@ -278,10 +282,9 @@
             pltpu.HBM((groups, more, cap, slots), BF16),
         ],
         scratch_shapes=[pltpu.VMEM((lines, block_rows), BF16), pltpu.VMEM((cap, slots), BF16)],
-        input_output_aliases=aliases,
         compiler_params=params(VMEM_BYTES),
         name="index",
-    )(numbers, *args)
+    )(numbers, *parcels)
 
 
 def lay_out(heard, number_ref, signal_ref):
@@ -313,36 +316,29 @@
         out_ref[place, first : first + 2 * SHIFT_ROWS, :] = jnp.concatenate(both, axis=0).astype(BF16)
 
 
-def hankel_kernel(v, n_win, samples, done, number_ref, *refs):
-    out_ref, signal_refs = refs[-2:]
-    parcel_refs = refs[: -3 if done else -2]
-    r_dev = parcel_refs[0].shape[0]
-    begin = first_sample(number_ref, v, n_win, samples)
-    for group, parcel_ref in enumerate(parcel_refs, done):
-        signal_ref = signal_refs.at[group % 2]
-        heard = [parcel_ref[:, w * samples : (w + 1) * samples] for w in range(n_win)]
-        lay_out(heard, number_ref, signal_ref)
-        for r in range(r_dev):
-            hankel_rows(signal_ref, r, begin, out_ref.shape[2], out_ref, group * r_dev + r)
-
-
-def build_hankel(parcels, numbers, earlier, groups, v, n_win, samples, width):
-    r_dev = parcels[0].shape[0]
-    shape = (groups * r_dev, LANES, width)
+def hankel_kernel(v, number_ref, *refs):
+    heard_refs, (out_ref, signal_ref) = refs[:-2], refs[-2:]
+    channels, samples = heard_refs[0].shape
+    begin = first_sample(number_ref, v, len(heard_refs), samples)
+    lay_out([ref[...] for ref in heard_refs], number_ref, signal_ref)
+    for channel in range(channels):
+        hankel_rows(signal_ref, channel, begin, out_ref.shape[2], out_ref, channel)
+
+
+def build_hankel(heard, numbers, v, width):
+    channels, samples = heard[0].shape
+    shape = (channels, LANES, width)
     vmem = pl.BlockSpec(memory_space=pltpu.VMEM)
-    done = 0 if earlier is None else groups - len(parcels)
-    copies = len(parcels) * r_dev * LANES * width
     return pl.pallas_call(
-        functools.partial(hankel_kernel, v, n_win, samples, done),
-        in_specs=[pl.BlockSpec(memory_space=pltpu.SMEM)] + [vmem] * (len(parcels) + (1 if done else 0)),
+        functools.partial(hankel_kernel, v),
+        in_specs=[pl.BlockSpec(memory_space=pltpu.SMEM)] + [vmem] * len(heard),
         out_specs=vmem,
-        scratch_shapes=[pltpu.VMEM((2, SHIFT_ROWS, n_win * samples + LAGS), F32)],
+        scratch_shapes=[pltpu.VMEM((channels, len(heard) * samples + LAGS), F32)],
         out_shape=jax.ShapeDtypeStruct(shape, BF16),
-        input_output_aliases={1 + len(parcels): 0} if done else {},
-        cost_estimate=pl.CostEstimate(flops=copies, bytes_accessed=2 * copies, transcendentals=0),
+        cost_estimate=pl.CostEstimate(flops=math.prod(shape), bytes_accessed=2 * math.prod(shape), transcendentals=0),
         compiler_params=params(VMEM_BYTES // 2),
         name="hankel",
-    )(numbers, *parcels, *([earlier] if done else []))
+    )(numbers, *heard)
 
 
 def window_of(block, tile):
@@ -540,14 +536,16 @@
     width = samples - LANES + lag_dev
     prebuilt = n_chan * r_dev * n_win * LANES * width * 2 <= HANKEL_BYTES
 
-    heard = [receivers] + [turned(receivers, "win", v) for v in range(1, n_win)]
-    owns = own_rows(sources[0], n_rep)
-    parcels, numbers = pack(plan, heard, pair_index[0, 0], keep[0, 0], n_rep, lag_dev, block_rows, n_chan)
-    own_parcel = parcels[0]
-    parcels = [turned(parcels[k], "chan", k) for k in range(1, n_chan)]
-    matrices = index([own_parcel], numbers, None, n_chan, n_win * samples, r_dev, cap, tile, block_rows)
+    parcels, numbers = pack(plan, receivers, pair_index[0, 0], keep[0, 0], n_rep, lag_dev, block_rows, n_chan)
+    parcels = [parcels[0]] + [turned(parcels[k], "chan", k) for k in range(1, n_chan)]
+    owns = lax.optimization_barrier((own_rows(sources[0], n_rep), parcels))[0]
+    matrices = index(parcels, numbers, samples, r_dev, cap, tile, block_rows)
+    heard = join(parcels, samples)
+    heard = [heard] + [turned(heard, "win", v) for v in range(1, n_win)]
     if prebuilt:
-        signals = [build_hankel([own_parcel], numbers, None, n_chan, v, n_win, samples, width) for v in range(n_win)]
+        signals = [build_hankel(heard, numbers, 0, width)]
+    else:
+        signals = [jnp.concatenate([span.reshape(n_chan, r_dev, samples) for span in heard], axis=2)] * n_win
 
     arrived = [{0: own} for own in owns]
 
@@ -576,22 +574,14 @@
         return [piece] + [turned(piece, "win", v) for v in range(1, n_win)]
 
     relay(1)
-    before_start(2, (matrices, parcels, signals) if prebuilt else (matrices, parcels))
-    parcels = after_arrival(1, parcels)
+    before_start(2, (matrices, signals[0]))
     relay(2)
-    matrices = index(parcels, numbers, matrices, n_chan, n_win * samples, r_dev, cap, tile, block_rows)
     if prebuilt:
-        signals[0] = build_hankel(parcels, numbers, signals[0], n_chan, 0, n_win, samples, width)
-        before_start(3, (matrices, signals[0]))
-    else:
-        signals = [jnp.stack([own_parcel] + parcels)[:, :, : n_win * samples]] * n_win
+        heard = after_arrival(1, heard)
+        signals += [build_hankel(heard, numbers, v, width) for v in range(1, n_win)]
+        before_start(3, signals)
     reach = range(-(n_chan - 2), n_chan - 1)
     near = choose(numbers, 2, arrived, [offset for offset in reach if offset in arrived[0]])
-    if prebuilt:
-        parcels = after_arrival(2, parcels)
-        parcels, near = lax.optimization_barrier((parcels, near))
-        for v in range(1, n_win):
-            signals[v] = build_hankel(parcels, numbers, signals[v], n_chan, v, n_win, samples, width)
     for step in range(3, n_chan):
         relay(step)
     near_spans = spans(near)

time: 79.9 us -> 82 us (1.026)
  waiting for transfers between devices: 7.37 us -> 15.2 us
  starting transfers between devices: 21.2 us -> 17.9 us
  Pallas kernels: 50.9 us -> 48.4 us
    ppermute x5, waiting for transfers between devices: 2 us -> 9.98 us  [swapped(): return lax.ppermute(block, axis, route)]
    ppermute x10, starting transfers between devices: 11.5 us -> 9.84 us  [turned(): lax.ppermute(block, axis, [(i, (i + distance) % size) for i in range(size)])]
    ppermute x5, starting transfers between devices: 9.62 us -> 8.08 us  [swapped(): return lax.ppermute(block, axis, route)]
    pallas_call x2 -> x1, Pallas kernels: 5.29 us -> 3.77 us  [index(): pl.pallas_call(functools.partial(index_kernel, r_dev, lists_at, cap, tile...]
    pallas_call x5 -> x4, Pallas kernels: 15.2 us -> 14.3 us  [the longest x2 12.9 us: build_hankel(): pl.pallas_call(functools.partial(hankel_kernel, v), in_specs=[pl.BlockSpe...]
  transfers between devices with their start and end apart: 15 -> 15, of which waited for: 6 -> 7; matrix products, arithmetic and copies ran while one was open for 0% -> 0% of each run, Pallas kernels for 50% -> 45%
where the time goes in v9:
time: 82 us; the launch traced here: 81.7 us
  Pallas kernels  48.4 us (59%)
  starting transfers between devices  17.9 us (22%)
  waiting for transfers between devices  15.2 us (19%)
    pallas_call x4, Pallas kernels, correlate(): pl.pallas_call(body, grid_spec=pltpu.PrefetchScalarGridSpec(num_scalar_pr...  27.9 us
    pallas_call x2, Pallas kernels, build_hankel(): pl.pallas_call(functools.partial(hankel_kernel, v), in_specs=[pl.BlockSpe...  12.9 us
    ppermute x5, waiting for transfers between devices, swapped(): return lax.ppermute(block, axis, route)  9.98 us
    ppermute x10, starting transfers between devices, turned(): lax.ppermute(block, axis, [(i, (i + distance) % size) for i in range(size)])  9.84 us
    ppermute x5, starting transfers between devices, swapped(): return lax.ppermute(block, axis, route)  8.08 us
    ppermute x10, waiting for transfers between devices, turned(): lax.ppermute(block, axis, [(i, (i + distance) % size) for i in range(size)])  5.21 us
    pallas_call x1, Pallas kernels, index(): pl.pallas_call(functools.partial(index_kernel, r_dev, lists_at, cap, tile...  3.77 us
  transfers between devices with their start and end apart: 15, of which 7 were waited for; matrix products, arithmetic and copies ran while one was open for 0% of the time, Pallas kernels for 45%

profile of v9, /device:TPU:0, one launch (start us, length us, event | category | flops | bytes accessed | tf_op | source)
XLA Modules:
  0.0 81.7 jit_solution(17155300406921658466)
XLA Ops:
  0.0 1.4 %pack.1 = (bf16[4,2304]{1,0:T(4,128)(2,1)S(1)}, bf16[4,2304]{1,0:T(4,128)(2,1)S(1)}, bf16[4,2304]{1,0:T(4,128)(2,1)S(1)}, bf16[4,2304]{1,0:T(4,128)(2,1)S(1)}, s32[7]{0:T(128)S(1)}) custom-call(s32[1,2]{1,0:T(1,128)} %plan_hbm.1, s32[4,512]{1,0:T(4,128)} %bitcast.5, s32[4,512]{1,0:T(4,128)} %bitcast.6, bf16[4,2048]{1,0:T(4,128)(2,1)} %receiver_hbm.1), custom_call_target="tpu_custom_call" | custom-call | tf_op jit(solution)/shard_map/pack/pallas_call | solution.py:92
  1.4 3.1 %collective-permute-start = (bf16[4,2304]{1,0:T(4,128)(2,1)S(1)}, bf16[4,2304]{1,0:T(4,128)(2,1)S(1)}, u32[]{:S(2)}, u32[]{:S(2)}) collective-permute-start(bf16[4,2304]{1,0:T(4,128)(2,1)S(1)} %get-tuple-element.38), channel_id=1, source_target_pairs={{0,4},{4,8},{8,12},{12,0},{1,5},{5,9},{9,13},{13,1},{2,6},{6,10},{... | collective-permute-start | bytes 55304 | tf_op jit(solution)/shard_map/ppermute | solution.py:34
  4.5 2.6 %collective-permute-start.1 = (bf16[4,2304]{1,0:T(4,128)(2,1)S(1)}, bf16[4,2304]{1,0:T(4,128)(2,1)S(1)}, u32[]{:S(2)}, u32[]{:S(2)}) collective-permute-start(bf16[4,2304]{1,0:T(4,128)(2,1)S(1)} %get-tuple-element.39), channel_id=1, source_target_pairs={{0,8},{4,12},{8,0},{12,4},{1,9},{5,13},{9,1},{13,5},{2,10},{6,14},... | collective-permute-start | bytes 55304 | tf_op jit(solution)/shard_map/ppermute | solution.py:34
  7.1 1.3 %collective-permute-start.2 = (bf16[4,2304]{1,0:T(4,128)(2,1)S(1)}, bf16[4,2304]{1,0:T(4,128)(2,1)S(1)}, u32[]{:S(2)}, u32[]{:S(2)}) collective-permute-start(bf16[4,2304]{1,0:T(4,128)(2,1)S(1)} %get-tuple-element.40), channel_id=1, source_target_pairs={{0,12},{4,0},{8,4},{12,8},{1,13},{5,1},{9,5},{13,9},{2,14},{6,2},{... | collective-permute-start | bytes 55304 | tf_op jit(solution)/shard_map/ppermute | solution.py:34
  8.4 1.0 %own_rows.1.refs_2_ = bf16[128,2048]{1,0:T(8,128)(2,1)S(1)} custom-call(bf16[256,2048]{1,0:T(8,128)(2,1)} %bitcast.4), custom_call_target="tpu_custom_call" | custom-call | tf_op jit(solution)/shard_map/own_rows/pallas_call | solution.py:144
  9.5 1.3 %collective-permute-done.2.refs_3_ = bf16[4,2304]{1,0:T(4,128)(2,1)S(1)} collective-permute-done((bf16[4,2304]{1,0:T(4,128)(2,1)S(1)}, bf16[4,2304]{1,0:T(4,128)(2,1)S(1)}, u32[]{:S(2)}, u32[]{:S(2)}) %collective-permute-start.2) | collective-permute-done | bytes 18464 | tf_op jit(solution)/shard_map/ppermute | solution.py:34
  10.8 0.7 collective-permute-start.5
  11.5 2.7 %collective-permute-start.4 = (bf16[128,2048]{1,0:T(8,128)(2,1)S(1)}, bf16[128,2048]{1,0:T(8,128)(2,1)S(1)}, u32[]{:S(2)}, u32[]{:S(2)}) collective-permute-start(bf16[128,2048]{1,0:T(8,128)(2,1)S(1)} %own_rows.1.refs_2_), channel_id=1, source_target_pairs={{0,4},{4,0},{8,12},{12,8},{1,5},{5,1},{9,13},{13,9},{2,6},{6,2},{1... | collective-permute-start | bytes 1572872 | tf_op jit(solution)/shard_map/ppermute | solution.py:29
  14.3 1.6 %collective-permute-start.3 = (bf16[16,2048]{1,0:T(8,128)(2,1)S(1)}, bf16[16,2048]{1,0:T(8,128)(2,1)S(1)}, u32[]{:S(2)}, u32[]{:S(2)}) collective-permute-start(bf16[16,2048]{1,0:T(8,128)(2,1)S(1)} %join.1.refs_0_), channel_id=1, source_target_pairs={{0,2},{2,0},{1,3},{3,1},{4,6},{6,4},{5,7},{7,5},{8,10},{10,8},{9,1... | collective-permute-start | bytes 196616 | tf_op jit(solution)/shard_map/ppermute | solution.py:34
  15.9 3.8 %index.1 = (bf16[4,640,256]{2,1,0:T(8,128)(2,1)S(1)}, bf16[4,512,512]{2,1,0:T(8,128)(2,1)S(1)}, s32[4]{0:T(128)S(1)}, s32[16]{0:T(128)S(1)}, bf16[4,4,640,256]{3...) custom-call(s32[7]{0:T(128)S(1)} %get-tuple-element.36.number_ref, bf16[4,2304]{1,0:T(4,128)(2,1)S(1)} %get-tuple-element.37.refs_0_, ...), custom_call_target="tpu_custom_call" | custom-call | tf_op jit(solution)/shard_map/index/pallas_call | solution.py:272
  19.7 6.4 %hankel.2.refs_2_ = bf16[16,128,2432]{2,1,0:T(8,128)(2,1)S(1)} custom-call(s32[7]{0:T(128)S(1)} %get-tuple-element.36.number_ref, bf16[16,2048]{1,0:T(8,128)(2,1)S(1)} %join.1.refs_0_, bf16[16,2048]{1,0:T(8,128)(2,1)S(1)} %collective-permute-done.3.refs_1_), custom_call_target="tpu_custom_call" | custom-call | flops 4980736 | bytes 9961472 | tf_op jit(solution)/shard_map/hankel/pallas_call | solution.py:332
  26.2 0.9 %collective-permute-start.6 = (bf16[128,2048]{1,0:T(8,128)(2,1)S(1)}, bf16[128,2048]{1,0:T(8,128)(2,1)S(1)}, u32[]{:S(2)}, u32[]{:S(2)}) collective-permute-start(bf16[128,2048]{1,0:T(8,128)(2,1)S(1)} %collective-permute-done.4.refs_3_), channel_id=1, source_target_pairs={{4,8},{8,4},{5,9},{9,5},{6,10},{10,6},{7,11},{11,7},{20,24},{24,20... | collective-permute-start | bytes 1572872 | tf_op jit(solution)/shard_map/ppermute | solution.py:29
  27.1 6.4 %hankel.3.refs_2_ = bf16[16,128,2432]{2,1,0:T(8,128)(2,1)S(1)} custom-call(s32[7]{0:T(128)S(1)} %get-tuple-element.36.number_ref, bf16[16,2048]{1,0:T(8,128)(2,1)S(1)} %join.1.refs_0_, bf16[16,2048]{1,0:T(8,128)(2,1)S(1)} %collective-permute-done.3.refs_1_), custom_call_target="tpu_custom_call" | custom-call | flops 4980736 | bytes 9961472 | tf_op jit(solution)/shard_map/hankel/pallas_call | solution.py:332
  33.5 4.0 %collective-permute-done.7.refs_4_ = bf16[128,2048]{1,0:T(8,128)(2,1)S(1)} collective-permute-done((bf16[128,2048]{1,0:T(8,128)(2,1)S(1)}, bf16[128,2048]{1,0:T(8,128)(2,1)S(1)}, u32[]{:S(2)}, u32[]{:S(2)}) %collective-permute-start.7) | collective-permute-done | bytes 524320 | tf_op jit(solution)/shard_map/ppermute | solution.py:29
  38.3 3.7 %collective-permute-start.9 = (bf16[128,2048]{1,0:T(8,128)(2,1)S(1)}, bf16[128,2048]{1,0:T(8,128)(2,1)S(1)}, u32[]{:S(2)}, u32[]{:S(2)}) collective-permute-start(bf16[128,2048]{1,0:T(8,128)(2,1)S(1)} %collective-permute-done.6.refs_0_), channel_id=1, source_target_pairs={{0,4},{4,0},{8,12},{12,8},{1,5},{5,1},{9,13},{13,9},{2,6},{6,2},{1... | collective-permute-start | bytes 1572872 | tf_op jit(solution)/shard_map/ppermute | solution.py:29
  42.5 6.0 %correlate.4 = (f32[4,512,512]{2,1,0:T(8,128)S(1)}, f32[4,512,512]{2,1,0:T(8,128)}) custom-call(s32[4]{0:T(128)S(1)} %get-tuple-element.41.pass_ref, s32[16]{0:T(128)S(1)} %get-tuple-element.42.count_ref, s32[7]{0:T(128)S(1)} %get-tuple-element.36.number_ref, bf16[128,2048]{1,0:T(8,128)(2,1)S(1)} %choose.2.refs_0_, ...), custom_call_target="tpu_custom_call" | custom-call | flops 4026531840 | bytes 8388608 | tf_op jit(solution)/shard_map/correlate/pallas_call | solution.py:505
  48.6 5.9 %collective-permute-done.9.refs_5_ = bf16[128,2048]{1,0:T(8,128)(2,1)S(1)} collective-permute-done((bf16[128,2048]{1,0:T(8,128)(2,1)S(1)}, bf16[128,2048]{1,0:T(8,128)(2,1)S(1)}, u32[]{:S(2)}, u32[]{:S(2)}) %collective-permute-start.9) | collective-permute-done | bytes 524320 | tf_op jit(solution)/shard_map/ppermute | solution.py:29
  54.5 0.8 %choose.3.refs_0_ = bf16[128,2048]{1,0:T(8,128)(2,1)S(1)} custom-call(s32[7]{0:T(128)S(1)} %get-tuple-element.36.number_ref, bf16[128,2048]{1,0:T(8,128)(2,1)S(1)} %collective-permute-done.6.refs_0_, bf16[128,2048]{1,0:T(8,128)(2,1)S(1)} %collective-permute-done.5.refs_1_, bf16[128,2048]{1,0:T(8,128)(2,1)S(1)} %own_rows.1.refs_2_, ...), custom_call_target="tpu_custom_call" | custom-call | tf_op jit(solution)/shard_map/choose/pallas_call | solution.py:178
  56.5 0.8 collective-permute-done.13.refs_1_
  57.3 6.2 %correlate.5 = (f32[4,512,512]{2,1,0:T(8,128)S(1)}, f32[4,512,512]{2,1,0:T(8,128)}) custom-call(s32[4]{0:T(128)S(1)} %get-tuple-element.41.pass_ref, s32[16]{0:T(128)S(1)} %get-tuple-element.42.count_ref, s32[7]{0:T(128)S(1)} %get-tuple-element.36.number_ref, bf16[128,2048]{1,0:T(8,128)(2,1)S(1)} %choose.3.refs_0_, ...), custom_call_target="tpu_custom_call", output_to_operand_aliasing={{0}: (10, {})} | custom-call | flops 4026531840 | bytes 8388608 | tf_op jit(solution)/shard_map/correlate/pallas_call | solution.py:505
  63.5 6.2 %correlate.6 = (f32[4,512,512]{2,1,0:T(8,128)S(1)}, f32[4,512,512]{2,1,0:T(8,128)}) custom-call(s32[4]{0:T(128)S(1)} %get-tuple-element.41.pass_ref, s32[16]{0:T(128)S(1)} %get-tuple-element.42.count_ref, s32[7]{0:T(128)S(1)} %get-tuple-element.36.number_ref, ...), custom_call_target="tpu_custom_call", output_to_operand_aliasing={{0}: (10, {})} | custom-call | flops 4026531840 | bytes 8388608 | tf_op jit(solution)/shard_map/correlate/pallas_call | solution.py:505
  69.7 0.6 collective-permute-done.10.refs_0_
  70.3 1.9 %collective-permute-done.14.refs_1_ = bf16[128,2048]{1,0:T(8,128)(2,1)S(1)} collective-permute-done((bf16[128,2048]{1,0:T(8,128)(2,1)S(1)}, bf16[128,2048]{1,0:T(8,128)(2,1)S(1)}, u32[]{:S(2)}, u32[]{:S(2)}) %collective-permute-start.14) | collective-permute-done | bytes 524320 | tf_op jit(solution)/shard_map/ppermute | solution.py:34
  72.2 9.5 %correlate.7 = f32[4,512,512]{2,1,0:T(8,128)} custom-call(s32[4]{0:T(128)S(1)} %get-tuple-element.41.pass_ref, s32[16]{0:T(128)S(1)} %get-tuple-element.42.count_ref, s32[7]{0:T(128)S(1)} %get-tuple-element.36.number_ref, bf16[128,2048]{1,0:T(8,128)(2,1)S(1)} %collective-permute-done.10.refs_0_, bf16[128,2048]{1,0:T(8,128)(2,1)S(1)} %collective-permute-done.14.refs_1_, ...), custom_call_target="tpu_custom_call" | custom-call | flops 4026531840 | bytes 8388608 | tf_op jit(solution)/shard_map/correlate/pallas_call | solution.py:505
  (18 shorter events, 2.6 us)
Async XLA Ops:
  1.4 8.1 %collective-permute-start = (bf16[4,2304]{1,0:T(4,128)(2,1)S(1)}, bf16[4,2304]{1,0:T(4,128)(2,1)S(1)}, u32[]{:S(2)}, u32[]{:S(2)}) collective-permute-start(bf16[4,2304]{1,0:T(4,128)(2,1)S(1)} %get-tuple-element.38), channel_id=1, source_target_pairs={{0,4},{4,8},{8,12},{12,0},{1,5},{5,9},{9,13},{13,1},{2,6},{6,10},{... | collective-permute-start | bytes 55304 | tf_op jit(solution)/shard_map/ppermute | solution.py:34
  4.5 5.0 %collective-permute-start.1 = (bf16[4,2304]{1,0:T(4,128)(2,1)S(1)}, bf16[4,2304]{1,0:T(4,128)(2,1)S(1)}, u32[]{:S(2)}, u32[]{:S(2)}) collective-permute-start(bf16[4,2304]{1,0:T(4,128)(2,1)S(1)} %get-tuple-element.39), channel_id=1, source_target_pairs={{0,8},{4,12},{8,0},{12,4},{1,9},{5,13},{9,1},{13,5},{2,10},{6,14},... | collective-permute-start | bytes 55304 | tf_op jit(solution)/shard_map/ppermute | solution.py:34
  7.1 3.8 %collective-permute-start.2 = (bf16[4,2304]{1,0:T(4,128)(2,1)S(1)}, bf16[4,2304]{1,0:T(4,128)(2,1)S(1)}, u32[]{:S(2)}, u32[]{:S(2)}) collective-permute-start(bf16[4,2304]{1,0:T(4,128)(2,1)S(1)} %get-tuple-element.40), channel_id=1, source_target_pairs={{0,12},{4,0},{8,4},{12,8},{1,13},{5,1},{9,5},{13,9},{2,14},{6,2},{... | collective-permute-start | bytes 55304 | tf_op jit(solution)/shard_map/ppermute | solution.py:34
  10.8 15.3 %collective-permute-start.5 = (bf16[128,2048]{1,0:T(8,128)(2,1)S(1)}, bf16[128,2048]{1,0:T(8,128)(2,1)S(1)}, u32[]{:S(2)}, u32[]{:S(2)}) collective-permute-start(bf16[128,2048]{1,0:T(8,128)(2,1)S(1)} %own_rows.1.refs_2_), channel_id=1, source_target_pairs={{4,8},{8,4},{5,9},{9,5},{6,10},{10,6},{7,11},{11,7},{20,24},{24,20... | collective-permute-start | bytes 1572872 | tf_op jit(solution)/shard_map/ppermute | solution.py:29
  11.5 14.7 %collective-permute-start.4 = (bf16[128,2048]{1,0:T(8,128)(2,1)S(1)}, bf16[128,2048]{1,0:T(8,128)(2,1)S(1)}, u32[]{:S(2)}, u32[]{:S(2)}) collective-permute-start(bf16[128,2048]{1,0:T(8,128)(2,1)S(1)} %own_rows.1.refs_2_), channel_id=1, source_target_pairs={{0,4},{4,0},{8,12},{12,8},{1,5},{5,1},{9,13},{13,9},{2,6},{6,2},{1... | collective-permute-start | bytes 1572872 | tf_op jit(solution)/shard_map/ppermute | solution.py:29
  14.3 5.3 %collective-permute-start.3 = (bf16[16,2048]{1,0:T(8,128)(2,1)S(1)}, bf16[16,2048]{1,0:T(8,128)(2,1)S(1)}, u32[]{:S(2)}, u32[]{:S(2)}) collective-permute-start(bf16[16,2048]{1,0:T(8,128)(2,1)S(1)} %join.1.refs_0_), channel_id=1, source_target_pairs={{0,2},{2,0},{1,3},{3,1},{4,6},{6,4},{5,7},{7,5},{8,10},{10,8},{9,1... | collective-permute-start | bytes 196616 | tf_op jit(solution)/shard_map/ppermute | solution.py:34
  26.1 11.5 %collective-permute-start.7 = (bf16[128,2048]{1,0:T(8,128)(2,1)S(1)}, bf16[128,2048]{1,0:T(8,128)(2,1)S(1)}, u32[]{:S(2)}, u32[]{:S(2)}) collective-permute-start(bf16[128,2048]{1,0:T(8,128)(2,1)S(1)} %collective-permute-done.5.refs_1_), channel_id=1, source_target_pairs={{0,4},{4,0},{8,12},{12,8},{1,5},{5,1},{9,13},{13,9},{2,6},{6,2},{1... | collective-permute-start | bytes 1572872 | tf_op jit(solution)/shard_map/ppermute | solution.py:29
  26.2 11.4 %collective-permute-start.6 = (bf16[128,2048]{1,0:T(8,128)(2,1)S(1)}, bf16[128,2048]{1,0:T(8,128)(2,1)S(1)}, u32[]{:S(2)}, u32[]{:S(2)}) collective-permute-start(bf16[128,2048]{1,0:T(8,128)(2,1)S(1)} %collective-permute-done.4.refs_3_), channel_id=1, source_target_pairs={{4,8},{8,4},{5,9},{9,5},{6,10},{10,6},{7,11},{11,7},{20,24},{24,20... | collective-permute-start | bytes 1572872 | tf_op jit(solution)/shard_map/ppermute | solution.py:29
  38.2 4.3 %collective-permute-start.8 = (bf16[128,2048]{1,0:T(8,128)(2,1)S(1)}, bf16[128,2048]{1,0:T(8,128)(2,1)S(1)}, u32[]{:S(2)}, u32[]{:S(2)}) collective-permute-start(bf16[128,2048]{1,0:T(8,128)(2,1)S(1)} %choose.2.refs_0_), channel_id=1, source_target_pairs={{0,1},{1,0},{2,3},{3,2},{4,5},{5,4},{6,7},{7,6},{8,9},{9,8},{10,11... | collective-permute-start | bytes 1572872 | tf_op jit(solution)/shard_map/ppermute | solution.py:34
  38.3 16.2 %collective-permute-start.9 = (bf16[128,2048]{1,0:T(8,128)(2,1)S(1)}, bf16[128,2048]{1,0:T(8,128)(2,1)S(1)}, u32[]{:S(2)}, u32[]{:S(2)}) collective-permute-start(bf16[128,2048]{1,0:T(8,128)(2,1)S(1)} %collective-permute-done.6.refs_0_), channel_id=1, source_target_pairs={{0,4},{4,0},{8,12},{12,8},{1,5},{5,1},{9,13},{13,9},{2,6},{6,2},{1... | collective-permute-start | bytes 1572872 | tf_op jit(solution)/shard_map/ppermute | solution.py:29
  42.0 14.0 %collective-permute-start.11 = (bf16[128,2048]{1,0:T(8,128)(2,1)S(1)}, bf16[128,2048]{1,0:T(8,128)(2,1)S(1)}, u32[]{:S(2)}, u32[]{:S(2)}) collective-permute-start(bf16[128,2048]{1,0:T(8,128)(2,1)S(1)} %choose.2.refs_0_), channel_id=1, source_target_pairs={{0,2},{2,0},{1,3},{3,1},{4,6},{6,4},{5,7},{7,5},{8,10},{10,8},{9,1... | collective-permute-start | bytes 1572872 | tf_op jit(solution)/shard_map/ppermute | solution.py:34
  55.3 2.0 %collective-permute-start.13 = (bf16[128,2048]{1,0:T(8,128)(2,1)S(1)}, bf16[128,2048]{1,0:T(8,128)(2,1)S(1)}, u32[]{:S(2)}, u32[]{:S(2)}) collective-permute-start(bf16[128,2048]{1,0:T(8,128)(2,1)S(1)} %choose.3.refs_0_), channel_id=1, source_target_pairs={{0,1},{1,0},{2,3},{3,2},{4,5},{5,4},{6,7},{7,6},{8,9},{9,8},{10,11... | collective-permute-start | bytes 1572872 | tf_op jit(solution)/shard_map/ppermute | solution.py:34
  56.0 7.5 %collective-permute-start.12 = (bf16[128,2048]{1,0:T(8,128)(2,1)S(1)}, bf16[128,2048]{1,0:T(8,128)(2,1)S(1)}, u32[]{:S(2)}, u32[]{:S(2)}) collective-permute-start(bf16[128,2048]{1,0:T(8,128)(2,1)S(1)} %collective-permute-done.11.refs_0_), channel_id=1, source_target_pairs={{0,1},{1,0},{2,3},{3,2},{4,5},{5,4},{6,7},{7,6},{8,9},{9,8},{10,11... | collective-permute-start | bytes 1572872 | tf_op jit(solution)/shard_map/ppermute | solution.py:34
  56.0 14.3 %collective-permute-start.10 = (bf16[128,2048]{1,0:T(8,128)(2,1)S(1)}, bf16[128,2048]{1,0:T(8,128)(2,1)S(1)}, u32[]{:S(2)}, u32[]{:S(2)}) collective-permute-start(bf16[128,2048]{1,0:T(8,128)(2,1)S(1)} %choose.3.refs_0_), channel_id=1, source_target_pairs={{0,2},{2,0},{1,3},{3,1},{4,6},{6,4},{5,7},{7,5},{8,10},{10,8},{9,1... | collective-permute-start | bytes 1572872 | tf_op jit(solution)/shard_map/ppermute | solution.py:34
  70.3 1.9 %collective-permute-start.14 = (bf16[128,2048]{1,0:T(8,128)(2,1)S(1)}, bf16[128,2048]{1,0:T(8,128)(2,1)S(1)}, u32[]{:S(2)}, u32[]{:S(2)}) collective-permute-start(bf16[128,2048]{1,0:T(8,128)(2,1)S(1)} %collective-permute-done.10.refs_0_), channel_id=1, source_target_pairs={{0,1},{1,0},{2,3},{3,2},{4,5},{5,4},{6,7},{7,6},{8,9},{9,8},{10,11... | collective-permute-start | bytes 1572872 | tf_op jit(solution)/shard_map/ppermute | solution.py:34
